TPU v7x, 128 devices: a whole 4x4x4 slice. The times are simulated.
128 devices in a mesh: gx: 8 (over y, core), gy: 16 (over x, z).
Axes of the slice: x: 4, y: 4, z: 4, core: 2. Of those that a mesh axis runs over, the one named last changes fastest.
Arguments:
- coords: float32 [3, 128, 256, 64], P(None, 'gx', 'gy'), may hold values from 0 to 1
- weights: float32 [128, 256, 64], P('gx', 'gy'), may hold values from 0.2 to 2
- solution: float32 [128, 256, 64], P('gx', 'gy'), may hold values from -6 to 6
- source: float32 [128, 256, 64], P('gx', 'gy'), may hold values from -6 to 6
- counts: int32 [128, 256], P('gx', 'gy'), may hold values from 16 to 64, as said below
- check_points: float32 [3, 256], replicated, may hold values from 0 to 1
- equiv_points: float32 [3, 256], replicated, may hold values from 0 to 1
- check_solve: float32 [256, 256], replicated, may hold values from -0.375 to 0.375
- up_children: float32 [4, 256, 256], replicated, may hold values from -0.1875 to 0.1875
- far_transfer: bfloat16 [40, 256, 256], replicated, may hold values from -0.078125 to 0.078125
- down_children: float32 [4, 256, 256], replicated, may hold values from -0.375 to 0.375
- pair_up: float32 [2, 256, 256], replicated, may hold values from -0.25 to 0.25
- lattice_map: float32 [256, 256], replicated, may hold values from -0.375 to 0.375
- pair_down: float32 [2, 256, 256], replicated, may hold values from -0.375 to 0.375
Outputs:
- residual: float32 [128, 256, 64], P('gx', 'gy')
Inputs may be any that keep to these rules, and one draw needn't show every extreme that they name: Slots from counts on are empty; some leaf box holds 64 points.
All inputs are finite; a program needn't handle non-finite values.
Results may differ from a plain program's by a relative error of at most 0.0003.
Values may be sent and summed in bfloat16 or wider, within the bound.
No kernel may reach another device: no remote copies, remote signals or barrier semaphores. Data moves between devices by JAX's collectives and lax.ppermute only.
A program may use at most 128 MiB of HBM per device.

v0:
```python
import jax
import jax.numpy as jnp
import numpy as np
from jax import lax
from jax.sharding import PartitionSpec as P

sharpness = 25.0
power_law = -2.25
scale_frac = 0.4
highest = lax.Precision.HIGHEST


def with_halo(block, sides, width):
    for axis, dim in sides:
        count = lax.axis_size(axis)
        forward = [(i, i + 1) for i in range(count - 1)]
        forward.append((count - 1, 0))
        backward = [(target, source) for source, target in forward]
        low = lax.ppermute(
            lax.slice_in_dim(block, block.shape[dim] - width, None, axis=dim), axis, forward
        )
        high = lax.ppermute(lax.slice_in_dim(block, 0, width, axis=dim), axis, backward)
        block = jnp.concatenate([low, block, high], axis=dim)
    return block


def from_partner(array, axis, stride):
    return lax.ppermute(array, axis, [(i, i ^ 1 << stride) for i in range(lax.axis_size(axis))])


def kernel(dist_sq):
    return (1.0 + sharpness * dist_sq) ** power_law


def far_offsets():
    result = []
    for shift_x in range(-3, 4):
        for shift_y in range(-3, 4):
            if max(abs(shift_x), abs(shift_y)) >= 2:
                result.append((shift_x, shift_y))
    return result


def reachable(parity, shift_amount):
    return abs((parity + shift_amount) // 2) <= 1


def near_block(padded):
    extent_x = padded.shape[1] - 2
    extent_y = padded.shape[2] - 2
    target = padded[:3, 1:-1, 1:-1]
    summed = jnp.zeros((2, extent_x, extent_y, padded.shape[3]), jnp.float32)
    for shift_x in (-1, 0, 1):
        for shift_y in (-1, 0, 1):
            sources = padded[
                :, 1 + shift_x : 1 + shift_x + extent_x, 1 + shift_y : 1 + shift_y + extent_y
            ]
            shifts = (float(shift_x), float(shift_y), 0.0)
            dist_sq = None
            for comp in range(3):
                gap = target[comp][..., :, None] - (sources[comp] + shifts[comp])[..., None, :]
                dist_sq = gap * gap if dist_sq is None else dist_sq + gap * gap
            kernel_vals = kernel(dist_sq)
            summed = summed + jnp.einsum(
                "xyij,cxyj->cxyi", kernel_vals, sources[3:], precision=highest
            )
    return summed


def check_block(points, check_points):
    dist_sq = None
    for comp in range(3):
        gap = check_points[comp][None, None, :, None] - points[comp][:, :, None, :]
        dist_sq = gap * gap if dist_sq is None else dist_sq + gap * gap
    kernel_vals = kernel(dist_sq)
    return jnp.einsum("xyqj,cxyj->xycq", kernel_vals, points[3:], precision=highest)


def evaluate_block(coords, local_exp, equiv_points):
    dist_sq = None
    for comp in range(3):
        gap = coords[comp][:, :, :, None] - equiv_points[comp][None, None, None, :]
        dist_sq = gap * gap if dist_sq is None else dist_sq + gap * gap
    kernel_vals = kernel(dist_sq)
    return jnp.einsum("xysq,xycq->cxys", kernel_vals, local_exp, precision=highest)


def gather_up(children, up_children):
    width = children.shape[3]
    grouped = children.reshape(
        children.shape[0] // 2, 2, children.shape[1] // 2, 2, children.shape[2], width
    )
    return jnp.einsum(
        "xaybcq,abqr->xycr", grouped, up_children.reshape(2, 2, width, width), precision=highest
    )


def spread_down(parents, down_children):
    width = parents.shape[3]
    spread = jnp.einsum(
        "xycq,abqr->xaybcr", parents, down_children.reshape(2, 2, width, width), precision=highest
    )
    return spread.reshape(2 * parents.shape[0], 2 * parents.shape[1], parents.shape[2], width)


def far_level(padded, operator):
    extent_x = padded.shape[0] - 6
    extent_y = padded.shape[1] - 6
    width = operator.shape[1]
    summed = jnp.zeros((extent_x, extent_y, padded.shape[2], width), jnp.float32)
    for parity_x in (0, 1):
        for parity_y in (0, 1):
            pieces = []
            chosen = []
            for number, (shift_x, shift_y) in enumerate(far_offsets()):
                if reachable(parity_x, shift_x) and reachable(parity_y, shift_y):
                    start_x = 3 + shift_x + parity_x
                    start_y = 3 + shift_y + parity_y
                    pieces.append(
                        padded[
                            start_x : start_x + extent_x - parity_x : 2,
                            start_y : start_y + extent_y - parity_y : 2,
                        ]
                    )
                    chosen.append(number)
            stacked = jnp.concatenate(pieces, axis=-1)
            matrix = operator[np.array(chosen)].reshape(len(chosen) * width, width)
            product = jnp.dot(
                stacked.reshape(-1, len(chosen) * width), matrix, preferred_element_type=jnp.float32
            )
            summed = summed.at[parity_x::2, parity_y::2].set(
                product.reshape(extent_x // 2, extent_y // 2, padded.shape[2], width)
            )
    return summed


def select_matrix(operator, position):
    return lax.dynamic_index_in_dim(operator, position, 0, keepdims=False)


def pair_merge(vector_now, partner, position, pair_up):
    lower_part = jnp.where(position == 0, vector_now, partner)
    upper_part = jnp.where(position == 0, partner, vector_now)
    return jnp.dot(lower_part, pair_up[0], precision=highest) + jnp.dot(
        upper_part, pair_up[1], precision=highest
    )


def box_rims(box_grid):
    return with_halo(box_grid.astype(jnp.bfloat16), (("gx", 0), ("gy", 1)), 3)


def shards(
    coords,
    weights,
    solution,
    source,
    counts,
    check_points,
    equiv_points,
    check_solve,
    up_children,
    far_transfer,
    down_children,
    pair_up,
    lattice_map,
    pair_down,
):
    slot_index = jnp.arange(coords.shape[3], dtype=jnp.int32)
    live_slots = (slot_index[None, None, :] < counts[:, :, None]).astype(jnp.float32)
    density = jnp.stack([weights * live_slots, weights * solution * live_slots])
    points = jnp.concatenate([coords, density], axis=0)
    padded_points = with_halo(points, (("gx", 1), ("gy", 2)), 1)
    check_pot = check_block(points, check_points)
    leaf_mult = jnp.einsum("xycq,qr->xycr", check_pot, check_solve, precision=highest)
    parent_mult = gather_up(leaf_mult, up_children)
    far_leaves = far_level(box_rims(leaf_mult), far_transfer)
    far_parents = far_level(box_rims(parent_mult), far_transfer)
    near_field = near_block(padded_points)
    grand_mult = gather_up(parent_mult, up_children)
    great_mult = gather_up(grand_mult, up_children)
    device_mult = gather_up(great_mult, up_children)
    bits_x = lax.axis_size("gx").bit_length() - 1
    bits_y = lax.axis_size("gy").bit_length() - 1
    place_x = lax.axis_index("gx")
    place_y = lax.axis_index("gy")
    vector_now = device_mult[0, 0]
    for level_bit in range(bits_y):
        partner = from_partner(vector_now, "gy", level_bit)
        vector_now = pair_merge(vector_now, partner, place_y // 2**level_bit % 2, pair_up)
    for level_bit in range(bits_x):
        partner = from_partner(vector_now, "gx", level_bit)
        vector_now = pair_merge(vector_now, partner, place_x // 2**level_bit % 2, pair_up)
    local_exp = jnp.dot(vector_now, lattice_map, precision=highest)
    for level_bit in reversed(range(bits_x)):
        local_exp = jnp.dot(
            local_exp, select_matrix(pair_down, place_x // 2**level_bit % 2), precision=highest
        )
    for level_bit in reversed(range(bits_y)):
        local_exp = jnp.dot(
            local_exp, select_matrix(pair_down, place_y // 2**level_bit % 2), precision=highest
        )
    device_local = local_exp[None, None]
    great_local = spread_down(device_local, down_children)
    grand_local = spread_down(great_local, down_children)
    parent_local = spread_down(grand_local, down_children) + far_parents
    leaf_local = spread_down(parent_local, down_children) + far_leaves
    potential = near_field + evaluate_block(coords, leaf_local, equiv_points)
    return live_slots * (source - scale_frac * (solution * potential[0] - potential[1]))


def solution(mesh):
    return jax.shard_map(
        shards,
        mesh=mesh,
        in_specs=(
            P(None, "gx", "gy", None),
            P("gx", "gy", None),
            P("gx", "gy", None),
            P("gx", "gy", None),
            P("gx", "gy"),
            P(),
            P(),
            P(),
            P(),
            P(),
            P(),
            P(),
            P(),
            P(),
        ),
        out_specs=P("gx", "gy", None),
        check_vma=False,
    )
```

profile of v0, /device:TPU:0, one launch (start us, length us, event | category | flops | bytes accessed | tf_op | source)
XLA Modules:
  0.0 781.3 jit_solution(5483367807986191049)
XLA Ops:
  3.1 26.2 %fusion.12 = f32[16,16,2,256]{3,2,1,0:T(2,128)S(1)} fusion(f32[16,16,64]{2,1,0:T(8,128)S(1)} %get-tuple-element.36, f32[256]{0:T(256)S(1)} %bitcast.348, f32[16,16,64]{2,1,0:T(8,128)S(1)} %get-tuple-element.37, f32[256]{0:T(256)S(1)} %bitcast.349, f32[16,16,64]{2,1,0:T(8,128)S(1)} %get-tuple-element.35, f32[256]{0:T(256)S(1)} %bitcast.347, ...), kind=kOutput, calls=%fused_computation.24 | convolution fusion | flops 142639104 | bytes 855040 | tf_op jit(solution)/shard_map/xyqj,cxyj->xycq/dot_general | solution.py:76
  35.7 3.0 collective-permute-start.12
  40.8 23.5 %fusion.90 = f32[16,16,2,64]{3,2,1,0:T(2,128)} fusion(f32[16,16,64]{2,1,0:T(8,128)S(1)} %copy-done.111, f32[16,16,64]{2,1,0:T(8,128)S(1)} %copy-done.116, f32[16,16,64]{2,1,0:T(8,128)S(1)} %copy-done.106, f32[1,16,16,64]{3,0,2,1:T(1,128)S(1)} %bitcast.295, f32[1,16,16,64]{3,0,2,1:T(1,128)S(1)} %bitcast.286), kind=kOutput, calls=%fused_computation.102 | convolution fusion | flops 35684352 | bytes 458752 | tf_op jit(solution)/shard_map/xyij,cxyj->cxyi/dot_general | solution.py:64
  64.9 3.6 collective-permute-start.5
  74.6 3.1 collective-permute-start.7
  86.4 3.1 collective-permute-start.10
  92.3 5.1 gather_fusion.3
  97.3 5.1 gather_fusion.1
  102.4 5.2 gather_fusion.2
  107.6 5.1 gather_fusion
  126.6 24.1 %fusion.54 = f32[16,16,2,64]{3,2,1,0:T(2,128)} fusion(f32[16,16,64]{2,1,0:T(8,128)S(1)} %bitcast.338, f32[16,16,64]{2,1,0:T(8,128)S(1)} %bitcast.337, f32[16,16,64]{2,1,0:T(8,128)S(1)} %bitcast.336, f32[16,16,64]{2,1,0:T(8,128)S(1)} %copy-done.112, f32[16,16,64]{2,1,0:T(8,128)S(1)} %copy-done.117, f32[16,16,64]{2,1,0:T(8,128)S(1)} %copy-done.107, ...), kind=kOutput, calls=%fused_computation.66 | convolution fusion | flops 35749888 | bytes 872448 | tf_op jit(solution)/shard_map/xyij,cxyj->cxyi/dot_general | solution.py:64
  150.7 23.9 %fusion.126 = f32[16,16,2,64]{3,2,1,0:T(2,128)} fusion(f32[16,16,64]{2,1,0:T(8,128)S(1)} %bitcast.335, f32[16,16,64]{2,1,0:T(8,128)S(1)} %bitcast.334, f32[16,16,64]{2,1,0:T(8,128)S(1)} %bitcast.333, f32[16,16,64]{2,1,0:T(8,128)S(1)} %copy-done.112, f32[16,16,64]{2,1,0:T(8,128)S(1)} %copy-done.117, f32[16,16,64]{2,1,0:T(8,128)S(1)} %copy-done.107, ...), kind=kOutput, calls=%fused_computation.138 | convolution fusion | flops 35749888 | bytes 872448 | tf_op jit(solution)/shard_map/xyij,cxyj->cxyi/dot_general | solution.py:64
  174.6 5.3 collective-permute-start.3
  202.5 5.7 collective-permute-start.14
  212.0 23.3 %fusion.114 = f32[16,16,2,64]{3,2,1,0:T(2,128)} fusion(f32[16,16,64]{2,1,0:T(8,128)S(1)} %bitcast.331, f32[16,16,64]{2,1,0:T(8,128)S(1)} %bitcast.332, f32[16,16,64]{2,1,0:T(8,128)S(1)} %bitcast.330, f32[16,16,64]{2,1,0:T(8,128)S(1)} %copy-done.113, f32[16,16,64]{2,1,0:T(8,128)S(1)} %copy-done.118, f32[16,16,64]{2,1,0:T(8,128)S(1)} %copy-done.108, ...), kind=kOutput, calls=%fused_computation.126 | convolution fusion | flops 35651584 | bytes 1179648 | tf_op jit(solution)/shard_map/xyij,cxyj->cxyi/dot_general | solution.py:64
  235.3 23.2 %fusion.42 = f32[16,16,2,64]{3,2,1,0:T(2,128)} fusion(f32[16,16,64]{2,1,0:T(8,128)S(1)} %bitcast.327, f32[16,16,64]{2,1,0:T(8,128)S(1)} %bitcast.328, f32[16,16,64]{2,1,0:T(8,128)S(1)} %bitcast.329, f32[16,16,64]{2,1,0:T(8,128)S(1)} %copy-done.113, f32[16,16,64]{2,1,0:T(8,128)S(1)} %copy-done.118, f32[16,16,64]{2,1,0:T(8,128)S(1)} %copy-done.108, ...), kind=kOutput, calls=%fused_computation.54 | convolution fusion | flops 35651584 | bytes 1179648 | tf_op jit(solution)/shard_map/xyij,cxyj->cxyi/dot_general | solution.py:64
  258.5 23.2 %fusion.78 = f32[16,16,2,64]{3,2,1,0:T(2,128)} fusion(f32[16,16,64]{2,1,0:T(8,128)S(1)} %bitcast.324, f32[16,16,64]{2,1,0:T(8,128)S(1)} %bitcast.325, f32[16,16,64]{2,1,0:T(8,128)S(1)} %bitcast.326, f32[16,16,64]{2,1,0:T(8,128)S(1)} %copy-done.113, f32[16,16,64]{2,1,0:T(8,128)S(1)} %copy-done.118, f32[16,16,64]{2,1,0:T(8,128)S(1)} %copy-done.108, ...), kind=kOutput, calls=%fused_computation.90 | convolution fusion | flops 35651584 | bytes 1179648 | tf_op jit(solution)/shard_map/xyij,cxyj->cxyi/dot_general | solution.py:64
  281.7 23.2 %fusion.102 = f32[16,16,2,64]{3,2,1,0:T(2,128)} fusion(f32[16,16,64]{2,1,0:T(8,128)S(1)} %bitcast.323, f32[16,16,64]{2,1,0:T(8,128)S(1)} %bitcast.322, f32[16,16,64]{2,1,0:T(8,128)S(1)} %bitcast.321, f32[16,16,64]{2,1,0:T(8,128)S(1)} %copy-done.113, f32[16,16,64]{2,1,0:T(8,128)S(1)} %copy-done.118, f32[16,16,64]{2,1,0:T(8,128)S(1)} %copy-done.108, ...), kind=kOutput, calls=%fused_computation.114 | convolution fusion | flops 35651584 | bytes 1179648 | tf_op jit(solution)/shard_map/xyij,cxyj->cxyi/dot_general | solution.py:64
  305.0 23.2 %fusion.66 = f32[16,16,2,64]{3,2,1,0:T(2,128)} fusion(f32[16,16,64]{2,1,0:T(8,128)S(1)} %bitcast.320, f32[16,16,64]{2,1,0:T(8,128)S(1)} %bitcast.319, f32[16,16,64]{2,1,0:T(8,128)S(1)} %bitcast.318, f32[16,16,64]{2,1,0:T(8,128)S(1)} %copy-done.113, f32[16,16,64]{2,1,0:T(8,128)S(1)} %copy-done.118, f32[16,16,64]{2,1,0:T(8,128)S(1)} %copy-done.108, ...), kind=kOutput, calls=%fused_computation.78 | convolution fusion | flops 35651584 | bytes 1179648 | tf_op jit(solution)/shard_map/xyij,cxyj->cxyi/dot_general | solution.py:64
  328.2 23.3 %fusion.138 = f32[16,16,2,64]{3,2,1,0:T(2,128)} fusion(f32[16,16,64]{2,1,0:T(8,128)S(1)} %bitcast.316, f32[16,16,64]{2,1,0:T(8,128)S(1)} %copy-done.113, f32[16,16,64]{2,1,0:T(8,128)S(1)} %bitcast.315, f32[16,16,64]{2,1,0:T(8,128)S(1)} %copy-done.118, f32[16,16,64]{2,1,0:T(8,128)S(1)} %bitcast.317, f32[16,16,64]{2,1,0:T(8,128)S(1)} %copy-done.108, ...), kind=kOutput, calls=%fused_computation.150 | convolution fusion | flops 35651584 | bytes 1179648 | tf_op jit(solution)/shard_map/xyij,cxyj->cxyi/dot_general | solution.py:64
  385.5 2.5 slice.1089
  390.6 2.5 slice.1176
  393.1 5.3 collective-permute-start.18
  496.8 2.8 fusion.436
  513.0 2.5 slice.1179
  518.0 2.5 slice.1175
  523.0 2.5 slice.1173
  525.5 2.5 slice.1172
  532.9 2.5 slice.1169
  535.4 2.7 slice.1168
  540.6 2.5 slice.1166
  548.0 2.5 slice.1163
  550.5 2.5 slice.1160
  555.5 2.5 slice.1158
  558.0 2.5 slice.1157
  560.5 2.5 slice.1154
  566.2 2.5 slice.1148
  571.2 2.5 slice.1146
  578.7 2.5 slice.1143
  581.2 2.5 slice.1142
  588.6 2.5 slice.1139
  601.1 2.5 slice.1133
  606.0 2.5 slice.1131
  611.0 2.5 slice.1129
  613.5 2.5 slice.1127
  620.9 2.5 slice.1124
  633.4 2.5 slice.1115
  640.8 2.5 slice.1112
  645.8 2.5 slice.1110
  648.3 2.5 slice.1109
  655.7 2.5 slice.1106
  663.2 2.5 slice.1103
  665.7 2.5 slice.1100
  673.3 2.5 slice.1086
  675.8 2.5 slice.1085
  683.3 2.5 slice.1082
  690.7 2.5 slice.1079
  695.7 2.5 slice.1077
  703.2 2.5 slice.1073
  737.1 3.2 scatter_fusion.4
  740.2 3.2 scatter_fusion.5
  743.4 3.2 scatter_fusion.6
  746.6 3.2 scatter_fusion.7
  750.0 29.0 %fusion = f32[16,16,2,64]{3,2,1,0:T(2,128)S(1)} fusion(f32[256]{0:T(256)S(1)} %bitcast.345, f32[16,16,64]{2,1,0:T(8,128)S(1)} %copy-done.114, f32[256]{0:T(256)S(1)} %bitcast.346, f32[16,16,64]{2,1,0:T(8,128)S(1)} %copy-done.119, f32[256]{0:T(256)S(1)} %bitcast.344, f32[16,16,64]{2,1,0:T(8,128)S(1)} %copy-done.109, f32[16,16,2,256]{3,2,1,0:T(2,128)S(1)} %bitcast.312), kind=kOutput, calls=%fused_computation.12 | convolution fusion | flops 142606336 | bytes 855040 | tf_op jit(solution)/shard_map/xysq,xycq->cxys/dot_general | solution.py:85
  (898 shorter events, 352.5 us)
Async XLA Ops:
  0.0 30.3 %copy-start = (f32[4,256,256]{2,1,0:T(8,128)S(1)}, f32[4,256,256]{2,1,0:T(8,128)}, u32[]{:S(2)}) copy-start(f32[4,256,256]{2,1,0:T(8,128)} %param.38) | copy-start | bytes 3145732
  1.9 27.4 %copy-start.105 = (f32[16,16,64]{2,1,0:T(8,128)}, f32[16,16,64]{2,1,0:T(8,128)S(1)}, u32[]{:S(2)}) copy-start(f32[16,16,64]{2,1,0:T(8,128)S(1)} %get-tuple-element.35) | copy-start | bytes 196612
  1.9 27.4 %copy-start.110 = (f32[16,16,64]{2,1,0:T(8,128)}, f32[16,16,64]{2,1,0:T(8,128)S(1)}, u32[]{:S(2)}) copy-start(f32[16,16,64]{2,1,0:T(8,128)S(1)} %get-tuple-element.36) | copy-start | bytes 196612
  1.9 27.4 %copy-start.115 = (f32[16,16,64]{2,1,0:T(8,128)}, f32[16,16,64]{2,1,0:T(8,128)S(1)}, u32[]{:S(2)}) copy-start(f32[16,16,64]{2,1,0:T(8,128)S(1)} %get-tuple-element.37) | copy-start | bytes 196612
  3.1 26.2 %copy-start.88 = (f32[256,256]{1,0:T(8,128)S(1)}, f32[256,256]{1,0:T(8,128)}, u32[]{:S(2)}) copy-start(f32[256,256]{1,0:T(8,128)} %param.37) | copy-start | bytes 786436
  29.9 8.7 %copy-start.11 = (bf16[16,16,2,256]{3,1,2,0:T(8,128)(2,1)}, bf16[16,16,2,256]{3,1,2,0:T(8,128)(2,1)S(1)}, u32[]{:S(2)}) copy-start(bf16[16,16,2,256]{3,1,2,0:T(8,128)(2,1)S(1)} %get-tuple-element.64) | copy-start | bytes 786436
  33.0 31.4 %collective-permute-start.4 = (f32[2,256]{1,0:T(2,128)S(1)}, f32[2,256]{1,0:T(2,128)S(1)}, u32[]{:S(2)}, u32[]{:S(2)}) collective-permute-start(f32[2,256]{1,0:T(2,128)S(1)} %convolution_bitcast_fusion.8), channel_id=1, source_target_pairs={{0,1},{1,0},{2,3},{3,2},{4,5},{5,4},{6,7},{7,6},{8,9},{9,8},{10,11... | collective-permute-start | bytes 6152 | tf_op jit(solution)/shard_map/ppermute | solution.py:28
  35.7 138.9 %collective-permute-start.11 = (bf16[3,8,2,256]{3,1,2,0:T(8,128)(2,1)}, bf16[3,8,2,256]{3,1,2,0:T(8,128)(2,1)}, u32[]{:S(2)}, u32[]{:S(2)}) collective-permute-start(bf16[3,8,2,256]{3,1,2,0:T(8,128)(2,1)} %get-tuple-element.46), channel_id=1, source_target_pairs={{0,16},{16,32},{32,48},{48,64},{64,80},{80,96},{96,112},{112,0},{1... | collective-permute-start | bytes 73736 | tf_op jit(solution)/shard_map/ppermute | solution.py:19
  35.7 144.2 %collective-permute-start.12 = (bf16[3,8,2,256]{3,1,2,0:T(8,128)(2,1)}, bf16[3,8,2,256]{3,1,2,0:T(8,128)(2,1)}, u32[]{:S(2)}, u32[]{:S(2)}) collective-permute-start(bf16[3,8,2,256]{3,1,2,0:T(8,128)(2,1)} %get-tuple-element.47), channel_id=1, source_target_pairs={{16,0},{32,16},{48,32},{64,48},{80,64},{96,80},{112,96},{0,112},{1... | collective-permute-start | bytes 73736 | tf_op jit(solution)/shard_map/ppermute | solution.py:22
  39.3 312.2 %collective-permute-start.15 = (bf16[3,16,2,256]{3,1,2,0:T(8,128)(2,1)}, bf16[3,16,2,256]{3,1,2,0:T(8,128)(2,1)}, u32[]{:S(2)}, u32[]{:S(2)}) collective-permute-start(bf16[3,16,2,256]{3,1,2,0:T(8,128)(2,1)} %get-tuple-element.40), channel_id=1, source_target_pairs={{0,16},{16,32},{32,48},{48,64},{64,80},{80,96},{96,112},{112,0},{1... | collective-permute-start | bytes 147464 | tf_op jit(solution)/shard_map/ppermute | solution.py:19
  40.3 82.2 %collective-permute-start = (f32[5,1,16,64]{3,0,2,1:T(8,128)}, f32[5,1,16,64]{3,0,2,1:T(8,128)S(1)}, u32[]{:S(2)}, u32[]{:S(2)}) collective-permute-start(f32[5,1,16,64]{3,0,2,1:T(8,128)} %get-tuple-element.33), channel_id=1, source_target_pairs={{0,16},{16,32},{32,48},{48,64},{64,80},{80,96},{96,112},{112,0},{1... | collective-permute-start | bytes 61448 | tf_op jit(solution)/shard_map/ppermute | solution.py:19
  40.8 23.7 %copy-start.1 = (f32[2,256,256]{2,1,0:T(8,128)S(1)}, f32[2,256,256]{2,1,0:T(8,128)}, u32[]{:S(2)}) copy-start(f32[2,256,256]{2,1,0:T(8,128)} %param.41) | copy-start | bytes 1572868
  40.8 31.2 %copy-start.179 = (f32[3,256]{1,0:T(4,128)S(1)}, f32[3,256]{1,0:T(4,128)}, u32[]{:S(2)}) copy-start(f32[3,256]{1,0:T(4,128)} %param.36) | copy-start | bytes 9220
  64.3 13.3 %copy-start.185 = (s32[27]{0:T(128)S(1)}, s32[27]{0:T(128)}, u32[]{:S(2)}) copy-start(s32[27]{0:T(128)} %constant.329) | copy-start | bytes 328
  64.3 13.3 %copy-start.186 = (s32[27]{0:T(128)S(1)}, s32[27]{0:T(128)}, u32[]{:S(2)}) copy-start(s32[27]{0:T(128)} %constant.328) | copy-start | bytes 328
  64.3 15.8 %copy-start.183 = (s32[27]{0:T(128)S(1)}, s32[27]{0:T(128)}, u32[]{:S(2)}) copy-start(s32[27]{0:T(128)} %constant.331) | copy-start | bytes 328
  64.3 15.8 %copy-start.184 = (s32[27]{0:T(128)S(1)}, s32[27]{0:T(128)}, u32[]{:S(2)}) copy-start(s32[27]{0:T(128)} %constant.330) | copy-start | bytes 328
  64.9 5.2 collective-permute-start.5
  70.5 3.6 collective-permute-start.6
  74.6 5.1 collective-permute-start.7
  80.1 1.2 collective-permute-start.8
  81.7 3.6 collective-permute-start.9
  86.4 26.3 %collective-permute-start.10 = (f32[2,256]{1,0:T(2,128)}, f32[2,256]{1,0:T(2,128)}, u32[]{:S(2)}, u32[]{:S(2)}) collective-permute-start(f32[2,256]{1,0:T(2,128)} %convolution_add_fusion.1), channel_id=1, source_target_pairs={{0,64},{16,80},{32,96},{48,112},{64,0},{80,16},{96,32},{112,48},{1... | collective-permute-start | bytes 6152 | tf_op jit(solution)/shard_map/ppermute | solution.py:28
  112.7 11.1 %collective-permute-start.1 = (f32[5,1,16,64]{3,0,2,1:T(8,128)}, f32[5,1,16,64]{3,0,2,1:T(8,128)S(1)}, u32[]{:S(2)}, u32[]{:S(2)}) collective-permute-start(f32[5,1,16,64]{3,0,2,1:T(8,128)} %get-tuple-element.34), channel_id=1, source_target_pairs={{16,0},{32,16},{48,32},{64,48},{80,64},{96,80},{112,96},{0,112},{1... | collective-permute-start | bytes 61448 | tf_op jit(solution)/shard_map/ppermute | solution.py:22
  122.5 229.0 %collective-permute-start.16 = (bf16[3,16,2,256]{3,1,2,0:T(8,128)(2,1)}, bf16[3,16,2,256]{3,1,2,0:T(8,128)(2,1)S(1)}, u32[]{:S(2)}, u32[]{:S(2)}) collective-permute-start(bf16[3,16,2,256]{3,1,2,0:T(8,128)(2,1)} %get-tuple-element.41), channel_id=1, source_target_pairs={{16,0},{32,16},{48,32},{64,48},{80,64},{96,80},{112,96},{0,112},{1... | collective-permute-start | bytes 147464 | tf_op jit(solution)/shard_map/ppermute | solution.py:22
  124.5 78.0 %collective-permute-start.2 = (f32[5,18,1,64]{3,0,2,1:T(8,128)}, f32[5,18,1,64]{3,0,2,1:T(8,128)}, u32[]{:S(2)}, u32[]{:S(2)}) collective-permute-start(f32[5,18,1,64]{3,0,2,1:T(8,128)} %get-tuple-element.25), channel_id=1, source_target_pairs={{0,1},{1,2},{2,3},{3,4},{4,5},{5,6},{6,7},{7,8},{8,9},{9,10},{10,1... | collective-permute-start | bytes 69128 | tf_op jit(solution)/shard_map/ppermute | solution.py:19
  150.7 57.6 %copy-start.15 = (f32[5,1,16,64]{3,0,2,1:T(8,128)S(1)}, f32[5,1,16,64]{3,0,2,1:T(8,128)}, u32[]{:S(2)}) copy-start(f32[5,1,16,64]{3,0,2,1:T(8,128)} %copy-done.14) | copy-start | bytes 61444
  174.6 33.6 %collective-permute-start.3 = (f32[5,18,1,64]{3,0,2,1:T(8,128)}, f32[5,18,1,64]{3,0,2,1:T(8,128)S(1)}, u32[]{:S(2)}, u32[]{:S(2)}) collective-permute-start(f32[5,18,1,64]{3,0,2,1:T(8,128)} %get-tuple-element.26), channel_id=1, source_target_pairs={{1,0},{2,1},{3,2},{4,3},{5,4},{6,5},{7,6},{8,7},{9,8},{10,9},{11,1... | collective-permute-start | bytes 69128 | tf_op jit(solution)/shard_map/ppermute | solution.py:22
  202.5 196.0 %collective-permute-start.13 = (bf16[14,3,2,256]{3,1,2,0:T(4,128)(2,1)}, bf16[14,3,2,256]{3,1,2,0:T(4,128)(2,1)}, u32[]{:S(2)}, u32[]{:S(2)}) collective-permute-start(bf16[14,3,2,256]{3,1,2,0:T(4,128)(2,1)} %get-tuple-element.44), channel_id=1, source_target_pairs={{0,1},{1,2},{2,3},{3,4},{4,5},{5,6},{6,7},{7,8},{8,9},{9,10},{10,1... | collective-permute-start | bytes 129032 | tf_op jit(solution)/shard_map/ppermute | solution.py:19
  202.5 196.0 %collective-permute-start.14 = (bf16[14,3,2,256]{3,1,2,0:T(4,128)(2,1)}, bf16[14,3,2,256]{3,1,2,0:T(4,128)(2,1)}, u32[]{:S(2)}, u32[]{:S(2)}) collective-permute-start(bf16[14,3,2,256]{3,1,2,0:T(4,128)(2,1)} %get-tuple-element.45), channel_id=1, source_target_pairs={{1,0},{2,1},{3,2},{4,3},{5,4},{6,5},{7,6},{8,7},{9,8},{10,9},{11,1... | collective-permute-start | bytes 129032 | tf_op jit(solution)/shard_map/ppermute | solution.py:22
  328.2 23.3 %copy-start.12 = (bf16[16,16,2,256]{3,1,2,0:T(8,128)(2,1)S(1)}, bf16[16,16,2,256]{3,1,2,0:T(8,128)(2,1)}, u32[]{:S(2)}) copy-start(bf16[16,16,2,256]{3,1,2,0:T(8,128)(2,1)} %copy-done.11) | copy-start | bytes 786436
  351.5 48.0 %copy-start.98 = (bf16[3,16,2,256]{3,1,2,0:T(8,128)(2,1)}, bf16[3,16,2,256]{3,1,2,0:T(8,128)(2,1)S(1)}, u32[]{:S(2)}) copy-start(bf16[3,16,2,256]{3,1,2,0:T(8,128)(2,1)S(1)} %collective-permute-done.16) | copy-start | bytes 147460
  393.1 118.7 %collective-permute-start.17 = (bf16[22,3,2,256]{3,1,2,0:T(4,128)(2,1)}, bf16[22,3,2,256]{3,1,2,0:T(4,128)(2,1)S(1)}, u32[]{:S(2)}, u32[]{:S(2)}) collective-permute-start(bf16[22,3,2,256]{3,1,2,0:T(4,128)(2,1)} %get-tuple-element.38), channel_id=1, source_target_pairs={{0,1},{1,2},{2,3},{3,4},{4,5},{5,6},{6,7},{7,8},{8,9},{9,10},{10,1... | collective-permute-start | bytes 202760 | tf_op jit(solution)/shard_map/ppermute | solution.py:19
  393.1 91.4 %copy-start.150 = (bf16[4,4,2,256]{3,1,2,0:T(4,128)(2,1)S(1)}, bf16[4,4,2,256]{3,1,2,0:T(4,128)(2,1)}, u32[]{:S(2)}) copy-start(bf16[4,4,2,256]{3,1,2,0:T(4,128)(2,1)} %slice.1043) | copy-start | bytes 49156
  393.1 91.5 %copy-start.148 = (bf16[4,4,2,256]{3,1,2,0:T(4,128)(2,1)S(1)}, bf16[4,4,2,256]{3,1,2,0:T(4,128)(2,1)}, u32[]{:S(2)}) copy-start(bf16[4,4,2,256]{3,1,2,0:T(4,128)(2,1)} %slice.1044) | copy-start | bytes 49156
  393.1 118.7 %collective-permute-start.18 = (bf16[22,3,2,256]{3,1,2,0:T(4,128)(2,1)}, bf16[22,3,2,256]{3,1,2,0:T(4,128)(2,1)}, u32[]{:S(2)}, u32[]{:S(2)}) collective-permute-start(bf16[22,3,2,256]{3,1,2,0:T(4,128)(2,1)} %get-tuple-element.39), channel_id=1, source_target_pairs={{1,0},{2,1},{3,2},{4,3},{5,4},{6,5},{7,6},{8,7},{9,8},{10,9},{11,1... | collective-permute-start | bytes 202760 | tf_op jit(solution)/shard_map/ppermute | solution.py:22
  399.5 88.1 %copy-start.141 = (bf16[4,4,2,256]{3,1,2,0:T(4,128)(2,1)S(1)}, bf16[4,4,2,256]{3,1,2,0:T(4,128)(2,1)}, u32[]{:S(2)}) copy-start(bf16[4,4,2,256]{3,1,2,0:T(4,128)(2,1)} %slice.1049) | copy-start | bytes 49156
  399.5 88.1 %copy-start.138 = (bf16[4,4,2,256]{3,1,2,0:T(4,128)(2,1)S(1)}, bf16[4,4,2,256]{3,1,2,0:T(4,128)(2,1)}, u32[]{:S(2)}) copy-start(bf16[4,4,2,256]{3,1,2,0:T(4,128)(2,1)} %slice.1050) | copy-start | bytes 49156
  407.5 89.0 %copy-start.132 = (bf16[4,4,2,256]{3,1,2,0:T(4,128)(2,1)S(1)}, bf16[4,4,2,256]{3,1,2,0:T(4,128)(2,1)}, u32[]{:S(2)}) copy-start(bf16[4,4,2,256]{3,1,2,0:T(4,128)(2,1)} %slice.1064) | copy-start | bytes 49156
  408.7 87.8 %copy-start.131 = (bf16[4,4,2,256]{3,1,2,0:T(4,128)(2,1)S(1)}, bf16[4,4,2,256]{3,1,2,0:T(4,128)(2,1)}, u32[]{:S(2)}) copy-start(bf16[4,4,2,256]{3,1,2,0:T(4,128)(2,1)} %slice.1065) | copy-start | bytes 49156
  411.2 85.3 %copy-start.164 = (bf16[4,4,2,256]{3,1,2,0:T(4,128)(2,1)S(1)}, bf16[4,4,2,256]{3,1,2,0:T(4,128)(2,1)}, u32[]{:S(2)}) copy-start(bf16[4,4,2,256]{3,1,2,0:T(4,128)(2,1)} %slice.1067) | copy-start | bytes 49156
  671.1 41.5 %copy-start.32 = (bf16[8,8,2,256]{3,1,2,0:T(8,128)(2,1)S(1)}, bf16[8,8,2,256]{3,1,2,0:T(8,128)(2,1)}, u32[]{:S(2)}) copy-start(bf16[8,8,2,256]{3,1,2,0:T(8,128)(2,1)} %slice.1155) | copy-start | bytes 196612
  671.4 41.3 %copy-start.31 = (bf16[8,8,2,256]{3,1,2,0:T(8,128)(2,1)S(1)}, bf16[8,8,2,256]{3,1,2,0:T(8,128)(2,1)}, u32[]{:S(2)}) copy-start(bf16[8,8,2,256]{3,1,2,0:T(8,128)(2,1)} %slice.1156) | copy-start | bytes 196612
  672.8 43.3 %copy-start.30 = (bf16[8,8,2,256]{3,1,2,0:T(8,128)(2,1)S(1)}, bf16[8,8,2,256]{3,1,2,0:T(8,128)(2,1)}, u32[]{:S(2)}) copy-start(bf16[8,8,2,256]{3,1,2,0:T(8,128)(2,1)} %slice.1161) | copy-start | bytes 196612
  673.1 43.0 %copy-start.29 = (bf16[8,8,2,256]{3,1,2,0:T(8,128)(2,1)S(1)}, bf16[8,8,2,256]{3,1,2,0:T(8,128)(2,1)}, u32[]{:S(2)}) copy-start(bf16[8,8,2,256]{3,1,2,0:T(8,128)(2,1)} %slice.1162) | copy-start | bytes 196612
  705.7 21.4 %copy-start.28 = (bf16[8,8,2,256]{3,1,2,0:T(8,128)(2,1)S(1)}, bf16[8,8,2,256]{3,1,2,0:T(8,128)(2,1)}, u32[]{:S(2)}) copy-start(bf16[8,8,2,256]{3,1,2,0:T(8,128)(2,1)} %slice.1176) | copy-start | bytes 196612
  709.0 18.2 %copy-start.75 = (bf16[8,8,2,256]{3,1,2,0:T(8,128)(2,1)S(1)}, bf16[8,8,2,256]{3,1,2,0:T(8,128)(2,1)}, u32[]{:S(2)}) copy-start(bf16[8,8,2,256]{3,1,2,0:T(8,128)(2,1)} %slice.1178) | copy-start | bytes 196612
  709.9 17.3 %copy-start.73 = (bf16[8,8,2,256]{3,1,2,0:T(8,128)(2,1)S(1)}, bf16[8,8,2,256]{3,1,2,0:T(8,128)(2,1)}, u32[]{:S(2)}) copy-start(bf16[8,8,2,256]{3,1,2,0:T(8,128)(2,1)} %slice.1179) | copy-start | bytes 196612
  710.7 16.4 %copy-start.10 = (bf16[27,256,256]{2,1,0:T(8,128)(2,1)S(1)}, bf16[27,256,256]{2,1,0:T(8,128)(2,1)}, u32[]{:S(2)}) copy-start(bf16[27,256,256]{2,1,0:T(8,128)(2,1)} %gather_fusion.3) | copy-start | bytes 10616836
  737.0 12.8 %copy-start.109 = (f32[16,16,64]{2,1,0:T(8,128)S(1)}, f32[16,16,64]{2,1,0:T(8,128)}, u32[]{:S(2)}) copy-start(f32[16,16,64]{2,1,0:T(8,128)} %copy-done.105) | copy-start | bytes 196612
  737.0 12.8 %copy-start.114 = (f32[16,16,64]{2,1,0:T(8,128)S(1)}, f32[16,16,64]{2,1,0:T(8,128)}, u32[]{:S(2)}) copy-start(f32[16,16,64]{2,1,0:T(8,128)} %copy-done.110) | copy-start | bytes 196612
  737.0 12.8 %copy-start.119 = (f32[16,16,64]{2,1,0:T(8,128)S(1)}, f32[16,16,64]{2,1,0:T(8,128)}, u32[]{:S(2)}) copy-start(f32[16,16,64]{2,1,0:T(8,128)} %copy-done.115) | copy-start | bytes 196612
  737.0 12.8 %copy-start.180 = (f32[1,256]{1,0:T(1,128)S(1)}, f32[1,256]{1,0:T(1,128)}, u32[]{:S(2)}) copy-start(f32[1,256]{1,0:T(1,128)} %get-tuple-element.51) | copy-start | bytes 3076
  737.0 12.8 %copy-start.181 = (f32[1,256]{1,0:T(1,128)S(1)}, f32[1,256]{1,0:T(1,128)}, u32[]{:S(2)}) copy-start(f32[1,256]{1,0:T(1,128)} %get-tuple-element.52) | copy-start | bytes 3076
  737.0 12.8 %copy-start.182 = (f32[1,256]{1,0:T(1,128)S(1)}, f32[1,256]{1,0:T(1,128)}, u32[]{:S(2)}) copy-start(f32[1,256]{1,0:T(1,128)} %get-tuple-element.53) | copy-start | bytes 3076
  749.9 29.1 %copy-start.89 = (f32[16,16,2,64]{3,2,1,0:T(2,128)S(1)}, f32[16,16,2,64]{3,2,1,0:T(2,128)}, u32[]{:S(2)}) copy-start(f32[16,16,2,64]{3,2,1,0:T(2,128)} %fusion.90) | copy-start | bytes 393220
  749.9 29.1 %copy-start.90 = (f32[16,16,2,64]{3,2,1,0:T(2,128)S(1)}, f32[16,16,2,64]{3,2,1,0:T(2,128)}, u32[]{:S(2)}) copy-start(f32[16,16,2,64]{3,2,1,0:T(2,128)} %fusion.54) | copy-start | bytes 393220
  749.9 29.1 %copy-start.91 = (f32[16,16,2,64]{3,2,1,0:T(2,128)S(1)}, f32[16,16,2,64]{3,2,1,0:T(2,128)}, u32[]{:S(2)}) copy-start(f32[16,16,2,64]{3,2,1,0:T(2,128)} %fusion.126) | copy-start | bytes 393220
  749.9 29.1 %copy-start.92 = (f32[16,16,2,64]{3,2,1,0:T(2,128)S(1)}, f32[16,16,2,64]{3,2,1,0:T(2,128)}, u32[]{:S(2)}) copy-start(f32[16,16,2,64]{3,2,1,0:T(2,128)} %fusion.114) | copy-start | bytes 393220
  749.9 29.1 %copy-start.93 = (f32[16,16,2,64]{3,2,1,0:T(2,128)S(1)}, f32[16,16,2,64]{3,2,1,0:T(2,128)}, u32[]{:S(2)}) copy-start(f32[16,16,2,64]{3,2,1,0:T(2,128)} %fusion.42) | copy-start | bytes 393220
  749.9 29.1 %copy-start.94 = (f32[16,16,2,64]{3,2,1,0:T(2,128)S(1)}, f32[16,16,2,64]{3,2,1,0:T(2,128)}, u32[]{:S(2)}) copy-start(f32[16,16,2,64]{3,2,1,0:T(2,128)} %fusion.78) | copy-start | bytes 393220
  749.9 29.1 %copy-start.95 = (f32[16,16,2,64]{3,2,1,0:T(2,128)S(1)}, f32[16,16,2,64]{3,2,1,0:T(2,128)}, u32[]{:S(2)}) copy-start(f32[16,16,2,64]{3,2,1,0:T(2,128)} %fusion.102) | copy-start | bytes 393220
  749.9 29.1 %copy-start.96 = (f32[16,16,2,64]{3,2,1,0:T(2,128)S(1)}, f32[16,16,2,64]{3,2,1,0:T(2,128)}, u32[]{:S(2)}) copy-start(f32[16,16,2,64]{3,2,1,0:T(2,128)} %fusion.66) | copy-start | bytes 393220
  749.9 29.1 %copy-start.97 = (f32[16,16,2,64]{3,2,1,0:T(2,128)S(1)}, f32[16,16,2,64]{3,2,1,0:T(2,128)}, u32[]{:S(2)}) copy-start(f32[16,16,2,64]{3,2,1,0:T(2,128)} %fusion.138) | copy-start | bytes 393220
  (142 other events, 289.0 us)
where the time goes:
time: 792 us; the launch traced here: 781 us
  local copies, waits for them, and re-layouts  428 us (54%)
  matrix products  290 us (37%)
  starting transfers between devices  36.2 us (5%)
  other arithmetic  13.4 us (2%)
  waiting for transfers between devices  8.13 us (1%)
    slice x216, local copies, waits for them, and re-layouts, far_level(): padded[start_x:start_x + extent_x - parity_x:2, start_y:start_y + extent_...  337 us
    dot_general x9, matrix products, near_block(): jnp.einsum('xyij,cxyj->cxyi', kernel_vals, sources[3:], precision=highest)  211 us
    unnamed x583, local copies, waits for them, and re-layouts  43.6 us
    dot_general x1, matrix products, evaluate_block(): jnp.einsum('xysq,xycq->cxys', kernel_vals, local_exp, precision=highest)  29 us
    dot_general x1, matrix products, check_block(): jnp.einsum('xyqj,cxyj->xycq', kernel_vals, points[3:], precision=highest)  26.2 us
    ppermute x6, starting transfers between devices, with_halo(): lax.ppermute(lax.slice_in_dim(block, 0, width, axis=dim), axis, backward)  20.7 us
    gather x4, local copies, waits for them, and re-layouts, far_level(): matrix = operator[np.array(chosen)].reshape(len(chosen) * width, width)  20.5 us
    scatter x8, local copies, waits for them, and re-layouts, far_level(): summed.at[parity_x::2, parity_y::2]  17.4 us
  transfers between devices with their start and end apart: 19, of which 5 were waited for; matrix products, arithmetic and copies ran while one was open for 55% of the time, Pallas kernels for 0%

commit v1 on v0

v1 whole, which is shorter than its diff:
```python
import jax
import jax.numpy as jnp
import numpy as np
from jax import lax
from jax.experimental import pallas as pl
from jax.experimental.pallas import tpu as pltpu
from jax.sharding import PartitionSpec as P

f32 = jnp.float32
bf16 = jnp.bfloat16
scale_frac = 0.4
highest = lax.Precision.HIGHEST
NX = 16
LANES = NX * 64
PADDED = LANES + 128
FEATS = 64
AXES = ("gx", "gy")
VMEM = pl.BlockSpec(memory_space=pltpu.VMEM)
PARAMS = pltpu.CompilerParams(vmem_limit_bytes=60 << 20)


def far_offsets():
    return [
        (x, y) for x in range(-3, 4) for y in range(-3, 4) if max(abs(x), abs(y)) >= 2
    ]


def dot(a, b, precision=None):
    return jnp.dot(a, b, preferred_element_type=f32, precision=precision)


def dot_t(a, b):
    return lax.dot_general(a, b, (((1,), (1,)), ((), ())), preferred_element_type=f32)


def split3(block):
    hi = block.astype(bf16).astype(f32)
    rest = block - hi
    mid = rest.astype(bf16).astype(f32)
    return hi, mid, rest - mid


def centred(block):
    row = lax.broadcasted_iota(jnp.int32, block.shape, 0)
    moved = jnp.where(row < 3, 5.0 * block - 2.5, 0.0)
    return row, moved, jnp.sum(moved * moved, axis=0, keepdims=True)


def row_feats(block):
    row, moved, norm = centred(block)
    packed = jnp.where(
        row < 3, moved, jnp.where(row == 5, norm + 1.0, jnp.where(row == 6, 1.0, 0.0))
    )
    hi, mid, lo = split3(packed)
    role = jnp.concatenate(
        [hi[0:1], mid[0:1], lo[0:1], hi[1:2], mid[1:2], lo[1:2], hi[6:7] * 25.0, hi[7:8]], axis=0
    )
    tens = jnp.where(row < 6, 10.0, 0.0)
    return jnp.concatenate([hi, hi, hi, mid, mid, lo, role, tens], axis=0).astype(bf16)


def col_feats(block, role_scale=1.0):
    row, moved, norm = centred(block)
    packed = jnp.where(row < 3, moved, jnp.where(row == 6, norm, 0.0))
    hi, mid, lo = split3(packed)
    one = jnp.where(row == 5, 1.0, 0.0)
    def part(value, marks, keep_norm):
        out = jnp.where(row < 3, value * -2.0, 0.0)
        if keep_norm:
            out = jnp.where(row == 6, value, out)
        return out + one if marks else out
    ones = jnp.where(row < 7, 1.0, 0.0)
    role = jnp.concatenate(
        [hi[0:1], mid[0:1], lo[0:1], hi[1:2], mid[1:2], lo[1:2], hi[7:8], hi[7:8]], axis=0
    )
    return jnp.concatenate(
        [
            part(hi, True, True),
            part(mid, False, True),
            part(lo, False, True),
            part(hi, True, False),
            part(mid, False, False),
            part(hi, True, False),
            ones * role_scale,
            role * role_scale,
        ],
        axis=0,
    ).astype(bf16)


def power(u):
    return jnp.exp2(jnp.log2(u) * -2.25)


def box_perm(side):
    order = []
    for e in (0, 1):
        for f in (0, 1):
            for b in range(side):
                for a in range(side):
                    for c in (0, 1):
                        order.append(((2 * b + f) * 2 * side + 2 * a + e) * 2 + c)
    out = np.zeros((len(order), len(order)), np.float32)
    out[np.arange(len(order)), order] = 1.0
    return out


def eye(n):
    return (
        lax.broadcasted_iota(jnp.int32, (n, n), 0) == lax.broadcasted_iota(jnp.int32, (n, n), 1)
    ).astype(bf16)


def gather4(blocks, matrices):
    n = blocks.shape[0] // 4
    total = None
    for p in range(4):
        term = dot(blocks[p * n : (p + 1) * n], matrices[p], highest)
        total = term if total is None else total + term
    return total


def upward_kernel(
    place, pts, check_pts, solve, up_child, pair_up, perm8, perm4,
    feats, leaf_r, parent_r, up_out, pot,
):
    check_cols = col_feats(check_pts[...], 0.0)
    ident = eye(128)

    def strip(a, carry):
        block = pts[a]
        rows = row_feats(block)
        for m in range(NX // 2):
            lanes = slice(128 * m, 128 * m + 128)
            f = dot_t(ident, rows[:, lanes]).astype(bf16)
            feats[pl.ds(pl.multiple_of(a * LANES + 128 * m, 128), 128), :] = f
            w = jnp.transpose(block[:, lanes])
            k = power(dot(f, check_cols))
            for half in range(2):
                span = slice(64 * half, 64 * half + 64)
                at = (lax.rem(a, 2) * 2 + half) * 128 + m * 16 + lax.div(a, 2) * 2
                for c in range(2):
                    pot[pl.ds(at + c, 1), :] = jnp.sum(
                        k[span] * w[span, 3 + c : 4 + c], axis=0, keepdims=True
                    )
        return carry

    lax.fori_loop(0, NX, strip, 0)
    leaf = dot(pot[...], solve[...], highest)
    leaf_r[...] = leaf.astype(bf16)
    parent = gather4(leaf, up_child)
    parent = dot(perm8[...], parent, highest)
    parent_r[...] = parent.astype(bf16)
    grand = dot(perm4[...], gather4(parent, up_child), highest)
    great = gather4(grand, up_child)
    vec = None
    for b in range(2):
        for a in range(2):
            at = (b * 2 + a) * 2
            term = dot(
                jnp.concatenate([great[at : at + 2]] * 4, axis=0), up_child[2 * a + b], highest
            )
            vec = term if vec is None else vec + term
    for bit in range(4):
        vec = dot(vec, pair_up[lax.rem(lax.div(place[1], 2**bit), 2)], highest)
    for bit in range(3):
        vec = dot(vec, pair_up[lax.rem(lax.div(place[0], 2**bit), 2)], highest)
    up_out[...] = vec


def role_tiles():
    def column(sx, sy):
        return [-10.0 * sx] * 3 + [-10.0 * sy] * 3 + [float(sx * sx + sy * sy), 0.0] + [
            float(sx)
        ] * 3 + [float(sy)] * 3 + [0.0, 0.0]
    pairs = [((t, -1), (t, 0)) for t in (-1, 0, 1)] + [((-1, 1), (0, 1)), ((1, 1), (1, 1))]
    out = np.zeros((5, 16, 128), np.float32)
    for n, (left, right) in enumerate(pairs):
        out[n, :, :64] = np.array(column(*left))[:, None]
        out[n, :, 64:] = np.array(column(*right))[:, None]
    return out


def sum_lanes(acc0, acc1):
    row = lax.broadcasted_iota(jnp.int32, (8, 256), 0)
    total = None
    for c, acc in enumerate((acc0, acc1)):
        hi = acc.astype(bf16)
        lo = (acc - hi.astype(f32)).astype(bf16)
        ones = jnp.where(row == c, 1.0, 0.0).astype(bf16)
        term = dot_t(ones, jnp.concatenate([hi, lo], axis=1))
        total = term if total is None else total + term
    return total


def near_kernel(pts, feats, roles, out, cols0, cols1, dens1):
    lane = lax.broadcasted_iota(jnp.int32, (1, 128), 1)
    first = lane < 64
    first_cols = lax.broadcasted_iota(jnp.int32, (FEATS, 128), 1) < 64

    def prepare(t, carry):
        block = pts[t]
        cols = col_feats(block)
        cols0[t] = cols
        moved = pltpu.roll(block, PADDED - 64, 1)
        cols1[t] = col_feats(moved)
        dens1[t] = moved
        return carry

    lax.fori_loop(0, NX + 2, prepare, 0)

    def step(i, carry):
        a = lax.div(i, 2)
        half = lax.rem(i, 2)
        for mm in range(4):
            base = pl.multiple_of(half * 512 + mm * 128, 128)
            here = pl.ds(base, 128)
            after = pl.ds(pl.multiple_of(base + 128, 128), 128)
            sums = []
            for odd in range(2):
                own, other = ((cols0, cols1), (cols1, cols0))[odd]
                d_own, d_other = ((pts, dens1), (dens1, pts))[odd]
                far = here if odd == 0 else after
                blocks = [own[a + t, :, here] for t in range(3)]
                blocks.append(jnp.where(first_cols, own[a, :, after], other[a + 1, :, far]))
                blocks.append(own[a + 2, :, after])
                blocks = [
                    jnp.concatenate([x[:48], x[48:] * roles[n]], axis=0)
                    for n, x in enumerate(blocks)
                ]
                rows = feats[pl.ds(pl.multiple_of(a * LANES + base + 64 * odd, 64), 64), :]
                k = power(dot(rows, jnp.concatenate(blocks, axis=1)))
                accs = []
                for c in range(2):
                    r = pl.ds(3 + c, 1)
                    dens = [d_own[a + t, r, here] for t in range(3)]
                    dens.append(jnp.where(first, d_own[a, r, after], d_other[a + 1, r, far]))
                    dens.append(jnp.where(first, d_own[a + 2, r, after], 0.0))
                    acc = None
                    for n in range(5):
                        term = k[:, 128 * n : 128 * n + 128] * dens[n]
                        acc = term if acc is None else acc + term
                    accs.append(acc)
                sums.append(accs)
            both = [jnp.concatenate([sums[0][c], sums[1][c]], axis=0) for c in range(2)]
            out[a, :, here] = sum_lanes(*both)
        return carry

    lax.fori_loop(0, 2 * NX, step, 0)


def reachable(parity, shift):
    return abs((parity + shift) // 2) <= 1


def far_kernel(boxes, transfer, leaf_out, parent_out):
    for px in (0, 1):
        for py in (0, 1):
            total = None
            for number, (sx, sy) in enumerate(far_offsets()):
                if not (reachable(px, sx) and reachable(py, sy)):
                    continue
                dx, dy = (px + sx) // 2, (py + sy) // 2
                source = (px + sx) % 2 * 2 + (py + sy) % 2
                window = jnp.concatenate(
                    [
                        boxes[source, dx + 1, 1 + dy : 9 + dy].reshape(128, 256),
                        boxes[source, dx + 1, 11 + dy : 15 + dy].reshape(64, 256),
                    ],
                    axis=0,
                )
                term = dot(window, transfer[number])
                total = term if total is None else total + term
            p = px * 2 + py
            leaf_out[p] = total[:128]
            parent_out[p] = total[128:]


def downward_kernel(
    place, gathered, lattice, pair_down, down_child, perm8, perm4, far_leaf, far_parent,
    equiv_pts, feats, near, solution, source, live, out, local, pot,
):
    vec = jnp.sum(gathered[...], axis=0)
    vec = dot(jnp.concatenate([vec] * 4, axis=0), lattice[...], highest)
    for bit in (2, 1, 0):
        vec = dot(vec, pair_down[lax.rem(lax.div(place[0], 2**bit), 2)], highest)
    for bit in (3, 2, 1, 0):
        vec = dot(vec, pair_down[lax.rem(lax.div(place[1], 2**bit), 2)], highest)
    great = jnp.concatenate(
        [dot(vec, down_child[2 * a + b], highest)[:2] for b in range(2) for a in range(2)], axis=0
    )
    spread = lambda x: jnp.concatenate([dot(x, down_child[p], highest) for p in range(4)], axis=0)
    grand = dot(perm4[...], spread(great), highest)
    parent = spread(grand) + far_parent[...]
    parent = dot(perm8[...], parent, highest)
    local[...] = spread(parent) + far_leaf[...]
    equiv_cols = col_feats(equiv_pts[...], 0.0)

    def step(i, carry):
        a = lax.div(i, 2)
        half = lax.rem(i, 2)
        for mm in range(4):
            base = pl.multiple_of(half * 512 + mm * 128, 128)
            m = half * 4 + mm
            rows = feats[pl.ds(pl.multiple_of(a * LANES + base, 128), 128), :]
            k = power(dot(rows, equiv_cols))
            accs = []
            for c in range(2):
                parts = []
                for odd in range(2):
                    at = (lax.rem(a, 2) * 2 + odd) * 128 + m * 16 + lax.div(a, 2) * 2 + c
                    weight = local[pl.ds(at, 1), :]
                    kk = k[64 * odd : 64 * odd + 64]
                    parts.append(kk[:, :128] * weight[:, :128] + kk[:, 128:] * weight[:, 128:])
                accs.append(jnp.concatenate(parts, axis=0))
            sums = sum_lanes(*accs) + near[a, :, pl.ds(base, 128)]
            for c in range(2):
                pot[m, pl.ds(16 * c + a, 1), :] = sums[c : c + 1]
        return carry

    lax.fori_loop(0, 2 * NX, step, 0)
    both = jnp.concatenate([pot[m] for m in range(NX // 2)], axis=1)
    result = source[...] - scale_frac * (solution[...] * both[:NX] - both[NX:])
    out[...] = jnp.where(live[...] > 0.0, result, 0.0)


def ring(axis, step):
    count = lax.axis_size(axis)
    return [(i, (i + step) % count) for i in range(count)]


def with_halo(block, axis, dim, width):
    low = lax.ppermute(
        lax.slice_in_dim(block, block.shape[dim] - width, None, axis=dim), axis, ring(axis, 1)
    )
    high = lax.ppermute(lax.slice_in_dim(block, 0, width, axis=dim), axis, ring(axis, -1))
    return low, high


def call(kernel, n_in, out_shape, scratch, smem=0):
    return pl.pallas_call(
        kernel,
        out_shape=out_shape,
        in_specs=[pl.BlockSpec(memory_space=pltpu.SMEM)] * smem + [VMEM] * n_in,
        out_specs=jax.tree.map(lambda _: VMEM, out_shape),
        scratch_shapes=scratch,
        compiler_params=PARAMS,
    )


def shape(*dims, dtype=f32):
    return jax.ShapeDtypeStruct(dims, dtype)


def shards(
    coords, weights, solution, source, counts, check_points, equiv_points, check_solve,
    up_children, far_transfer, down_children, pair_up, lattice_map, pair_down,
):
    slot = lax.broadcasted_iota(jnp.int32, (NX, NX, 64), 2)
    live = (slot < counts[:, :, None]).astype(f32)
    flat = lambda x: x.reshape(NX, LANES)
    live = flat(live)
    sol = flat(solution)
    w0 = flat(weights) * live
    w1 = w0 * sol
    xyz = coords.reshape(3, NX, LANES)
    zero = jnp.zeros_like(w0)
    pts = jnp.stack([xyz[0], xyz[1], xyz[2], w0, w1, zero, zero, zero], axis=1)
    low, high = with_halo(pts, "gx", 0, 1)
    tall = jnp.concatenate([low, pts, high], axis=0)
    low, high = with_halo(tall, "gy", 2, 64)
    padded = jnp.concatenate([low, tall, high], axis=2)

    place = jnp.stack([lax.axis_index("gx"), lax.axis_index("gy")]).astype(jnp.int32)
    eight = lambda x: jnp.pad(x, ((0, 5), (0, 0)))
    perm8, perm4 = box_perm(4), box_perm(2)
    feats, leaf_r, parent_r, up = call(
        upward_kernel, 7,
        (shape(NX * LANES, FEATS, dtype=bf16), shape(512, 256, dtype=bf16),
         shape(128, 256, dtype=bf16), shape(8, 256)),
        [pltpu.VMEM((512, 256), f32)], smem=1,
    )(place, pts, eight(check_points), check_solve, up_children, pair_up, perm8, perm4)

    gathered = lax.all_to_all(
        jnp.broadcast_to(up[None, :2], (128, 2, 256)), AXES, 0, 0, tiled=True
    )

    boxes = jnp.concatenate(
        [
            leaf_r.reshape(4, 8, 16, 256),
            jnp.pad(parent_r.reshape(4, 4, 8, 256), ((0, 0), (0, 0), (0, 8), (0, 0))),
        ],
        axis=1,
    )
    ends = lambda n, p: jnp.concatenate([boxes[:, n : n + 1], boxes[:, p : p + 1]], axis=1)
    low = lax.ppermute(ends(7, 11), "gy", ring("gy", 1))
    high = lax.ppermute(ends(0, 8), "gy", ring("gy", -1))
    wide = jnp.concatenate(
        [low[:, :1], boxes[:, :8], high[:, :1], low[:, 1:], boxes[:, 8:], high[:, 1:]], axis=1
    )
    last = jnp.concatenate([wide[:, :10, 14:16], wide[:, 10:, 6:8]], axis=1)
    low = lax.ppermute(last, "gx", ring("gx", 1))
    high = lax.ppermute(wide[:, :, :2], "gx", ring("gx", -1))
    before = jnp.concatenate([low, wide[:, :, :14]], axis=2)
    after = jnp.concatenate(
        [
            jnp.concatenate([wide[:, :10, 2:], high[:, :10]], axis=2),
            jnp.concatenate([wide[:, 10:, 2:8], high[:, 10:], wide[:, 10:, 8:]], axis=2),
        ],
        axis=1,
    )
    windows = jnp.stack([before, wide, after], axis=1)

    near = call(
        near_kernel, 3, shape(NX, 8, LANES),
        [pltpu.VMEM((NX + 2, FEATS, PADDED), bf16)] * 2 + [pltpu.VMEM((NX + 2, 8, PADDED), f32)],
    )(padded, feats, jnp.asarray(role_tiles(), bf16))

    far_leaf, far_parent = call(
        far_kernel, 2, (shape(4, 128, 256), shape(4, 64, 256)), []
    )(windows, far_transfer)
    far_parent = far_parent.reshape(4, 4, 16, 256)[:, :, :8].reshape(128, 256)

    out = call(
        downward_kernel, 14, shape(NX, LANES),
        [pltpu.VMEM((512, 256), f32), pltpu.VMEM((NX // 2, 2 * NX, 128), f32)], smem=1,
    )(
        place, gathered, lattice_map, pair_down, down_children, perm8.T, perm4.T,
        far_leaf.reshape(512, 256), far_parent, eight(equiv_points), feats, near,
        sol, flat(source), live,
    )
    return out.reshape(NX, NX, 64)


def solution(mesh):
    box = P("gx", "gy", None)
    return jax.shard_map(
        shards,
        mesh=mesh,
        in_specs=(P(None, "gx", "gy", None), box, box, box, P("gx", "gy")) + (P(),) * 9,
        out_specs=box,
        check_vma=False,
    )
```

time: 792 us -> 147 us (0.19); the launches traced: 781 us -> 146 us
  local copies, waits for them, and re-layouts: 428 us -> 15.6 us
  matrix products: 290 us -> 0 us
  Pallas kernels: 0 us -> 104 us
  starting transfers between devices: 36.2 us -> 22.8 us
  other arithmetic: 13.4 us -> 3.42 us
  waiting for transfers between devices: 8.13 us -> 0.03 us
    slice x218 -> x10, local copies, waits for them, and re-layouts: 339 us -> 4.41 us  [the longest x1 1.57 us: shards(): far_parent = far_parent.reshape(4, 4, 16, 256)[:, :, :8].reshape(128, 256)]
    dot_general x50 -> x0, matrix products: 290 us -> none  [the longest x9 211 us: near_block(): jnp.einsum('xyij,cxyj->cxyi', kernel_vals, sources[3:], precision=highest)]
    pallas_call x0 -> x4, Pallas kernels: none -> 104 us  [the longest x1 36.4 us: shards(): call(near_kernel, 3, shape(NX, 8, LANES), [pltpu.VMEM((NX + 2, FEATS, PAD...]
    unnamed x583 -> x23, local copies, waits for them, and re-layouts: 43.6 us -> 0.8 us
    gather x4 -> x0, local copies, waits for them, and re-layouts: 20.5 us -> none  [far_level(): matrix = operator[np.array(chosen)].reshape(len(chosen) * width, width)]
    ppermute x13 -> x6, starting transfers between devices: 35.7 us -> 16 us  [the longest x2 7.21 us: with_halo(): lax.ppermute(lax.slice_in_dim(block, 0, width, axis=dim), axis, ring(axis...]
    scatter x8 -> x0, local copies, waits for them, and re-layouts: 17.4 us -> none  [far_level(): summed.at[parity_x::2, parity_y::2]]
    ppermute x13 -> x6, waiting for transfers between devices: 8.11 us -> 0.02 us  [the longest x2 0.01 us: with_halo(): lax.ppermute(lax.slice_in_dim(block, 0, width, axis=dim), axis, ring(axis...]
  transfers between devices with their start and end apart: 19 -> 9, of which waited for: 5 -> 0; matrix products, arithmetic and copies ran while one was open for 55% -> 8% of each run, Pallas kernels for 0% -> 47%
where the time goes in v1:
time: 147 us; the launch traced here: 146 us
  Pallas kernels  104 us (71%)
  starting transfers between devices  22.8 us (16%)
  local copies, waits for them, and re-layouts  15.6 us (11%)
  other arithmetic  3.42 us (2%)
    pallas_call x1, Pallas kernels, shards(): call(near_kernel, 3, shape(NX, 8, LANES), [pltpu.VMEM((NX + 2, FEATS, PAD...  36.4 us
    pallas_call x1, Pallas kernels, shards(): call(downward_kernel, 14, shape(NX, LANES), [pltpu.VMEM((512, 256), f32),...  35.7 us
    pallas_call x1, Pallas kernels, shards(): call(upward_kernel, 7, (shape(NX * LANES, FEATS, dtype=bf16), shape(512,...  24.8 us
    ppermute x2, starting transfers between devices, with_halo(): lax.ppermute(lax.slice_in_dim(block, 0, width, axis=dim), axis, ring(axis...  7.21 us
    pallas_call x1, Pallas kernels, shards(): call(far_kernel, 2, (shape(4, 128, 256), shape(4, 64, 256)), [])  6.77 us
    all_to_all x1, starting transfers between devices, shards(): lax.all_to_all(jnp.broadcast_to(up[None, :2], (128, 2, 256)), AXES, 0, 0,...  5.62 us
    ppermute x1, starting transfers between devices, shards(): high = lax.ppermute(ends(0, 8), 'gy', ring('gy', -1))  4.41 us
    reshape x4, local copies, waits for them, and re-layouts, shards(): flat = lambda x: x.reshape(NX, LANES)  3.48 us
  transfers between devices with their start and end apart: 9, of which 0 were waited for; matrix products, arithmetic and copies ran while one was open for 8% of the time, Pallas kernels for 47%

profile of v1, /device:TPU:0, one launch (start us, length us, event | category | flops | bytes accessed | tf_op | source)
XLA Modules:
  0.0 145.9 jit_solution(805202417682523518)
XLA Ops:
  0.0 0.8 lt.26
  0.8 0.1 lt.27
  0.9 0.1 iota.18
  1.0 1.0 reshape.135
  2.0 1.0 reshape.136
  3.1 0.0 copy-start.7
  3.1 1.1 fusion.7
  4.2 0.1 stack_squeeze.10
  4.3 0.1 stack_squeeze.11
  4.4 0.1 stack_squeeze.9
  4.6 0.1 fusion.4
  4.8 0.7 stack.33.pts
  5.5 0.0 copy-start
  5.6 0.0 collective-permute-start.4
  5.6 2.9 %collective-permute-start.5 = (f32[1,8,1024]{2,1,0:T(8,128)S(1)}, f32[1,8,1024]{2,1,0:T(8,128)S(1)}, u32[]{:S(2)}, u32[]{:S(2)}) collective-permute-start(f32[1,8,1024]{2,1,0:T(8,128)S(1)} %get-tuple-element.22), channel_id=1, source_target_pairs={{0,112},{16,0},{32,16},{48,32},{64,48},{80,64},{96,80},{112,96},{1... | collective-permute-start | bytes 98312 | tf_op jit(solution)/shard_map/ppermute | solution.py:336
  8.5 0.0 copy-done.7
  8.5 0.6 pad.11.check_pts
  9.1 0.6 pad_add_fusion.place
  9.7 0.0 copy-done
  9.7 0.0 copy-start.4
  9.7 24.8 %shard_map.181 = (bf16[16384,64]{1,0:T(8,128)(2,1)}, bf16[512,256]{1,0:T(8,128)(2,1)}, bf16[128,256]{1,0:T(8,128)(2,1)}, f32[8,256]{1,0:T(8,128)}) custom-call(s32[2]{0:T(128)} %pad_add_fusion.place, f32[16,8,1024]{2,1,0:T(8,128)} %copy-done, f32[8,256]{1,0:T(8,128)} %pad.11.check_pts, f32[256,256]{1,0:T(8,128)} %solve.1, f32[4,256,256]{2,1,0:T(8,128)} %up_child.1, ...), custom_call_target="tpu_custom_call" | custom-call | tf_op jit(solution)/shard_map/pallas_call | solution.py:377
  34.6 0.9 pad_slice_fusion.1
  35.5 2.1 %collective-permute-start = (bf16[4,2,16,256]{3,2,1,0:T(8,128)(2,1)S(1)}, bf16[4,2,16,256]{3,2,1,0:T(8,128)(2,1)S(1)}, u32[]{:S(2)}, u32[]{:S(2)}) collective-permute-start(bf16[4,2,16,256]{3,2,1,0:T(8,128)(2,1)S(1)} %pad_maximum_fusion.9), channel_id=1, source_target_pairs={{0,1},{1,2},{2,3},{3,4},{4,5},{5,6},{6,7},{7,8},{8,9},{9,10},{10,1... | collective-permute-start | bytes 196616 | tf_op jit(solution)/shard_map/ppermute | solution.py:396
  37.5 4.4 %collective-permute-start.1 = (bf16[4,2,16,256]{3,2,1,0:T(8,128)(2,1)S(1)}, bf16[4,2,16,256]{3,2,1,0:T(8,128)(2,1)S(1)}, u32[]{:S(2)}, u32[]{:S(2)}) collective-permute-start(bf16[4,2,16,256]{3,2,1,0:T(8,128)(2,1)S(1)} %pad_maximum_fusion.10), channel_id=1, source_target_pairs={{0,15},{1,0},{2,1},{3,2},{4,3},{5,4},{6,5},{7,6},{8,7},{9,8},{10,9... | collective-permute-start | bytes 196616 | tf_op jit(solution)/shard_map/ppermute | solution.py:397
  41.9 0.7 slice.89
  42.6 0.8 broadcast_in_dim.2
  43.4 5.6 %all-to-all-start = ((f32[128,2,256]{2,1,0:T(2,128)}), f32[128,2,256]{2,1,0:T(2,128)S(1)}, u32[]{:S(2)}, u32[]{:S(2)}) async-start(f32[128,2,256]{2,1,0:T(2,128)} %broadcast_in_dim.2), calls=%async_computation | async-start | bytes 524288 | tf_op jit(solution)/shard_map/all_to_all | solution.py:384
  49.1 0.0 copy-start.5
  49.1 0.1 lt.29
  49.2 0.6 compare_convert_fusion.live
  49.8 0.0 copy-done.4
  49.8 0.7 reshape.142.solution
  50.5 0.0 copy-done.6
  50.5 0.7 reshape.143.source
  51.2 0.0 copy-done.8
  51.2 0.6 pad.13.equiv_pts
  51.8 0.0 collective-permute-done.4
  51.8 0.0 collective-permute-done.5
  51.8 0.0 copy-done.1
  51.9 0.1 fusion.5
  52.0 1.1 collective-permute-start.6
  53.1 4.3 %collective-permute-start.7 = (f32[18,8,64]{2,1,0:T(8,128)S(1)}, f32[18,8,64]{2,1,0:T(8,128)S(1)}, u32[]{:S(2)}, u32[]{:S(2)}) collective-permute-start(f32[18,8,64]{2,1,0:T(8,128)S(1)} %get-tuple-element.19), channel_id=1, source_target_pairs={{0,15},{1,0},{2,1},{3,2},{4,3},{5,4},{6,5},{7,6},{8,7},{9,8},{10,9... | collective-permute-start | bytes 110600 | tf_op jit(solution)/shard_map/ppermute | solution.py:336
  57.4 0.0 collective-permute-done
  57.4 0.0 copy-done.2
  57.4 0.0 collective-permute-done.1
  57.5 0.0 copy-done.5
  57.6 2.3 %collective-permute-start.3 = (bf16[4,16,2,256]{3,2,1,0:T(2,128)(2,1)S(1)}, bf16[4,16,2,256]{3,2,1,0:T(2,128)(2,1)S(1)}, u32[]{:S(2)}, u32[]{:S(2)}) collective-permute-start(bf16[4,16,2,256]{3,2,1,0:T(2,128)(2,1)S(1)} %slice.119), channel_id=1, source_target_pairs={{0,112},{16,0},{32,16},{48,32},{64,48},{80,64},{96,80},{112,96},{1... | collective-permute-start | bytes 196616 | tf_op jit(solution)/shard_map/ppermute | solution.py:403
  59.9 0.1 fusion.3
  60.0 0.0 collective-permute-start.2
  60.0 0.0 collective-permute-done.6
  60.0 0.0 collective-permute-done.7
  60.0 1.1 concatenate.50.pts
  61.1 36.4 %shard_map.183.near = f32[16,8,1024]{2,1,0:T(8,128)} custom-call(f32[18,8,1152]{2,1,0:T(8,128)} %concatenate.50.pts, bf16[16384,64]{1,0:T(8,128)(2,1)} %get-tuple-element.16.feats, bf16[5,16,128]{2,1,0:T(8,128)(2,1)} %constant.30.clone.roles), custom_call_target="tpu_custom_call" | custom-call | tf_op jit(solution)/shard_map/pallas_call | solution.py:414
  97.6 0.0 collective-permute-done.3
  97.6 0.3 fusion.2
  97.9 0.0 collective-permute-done.2
  97.9 0.2 maximum_bitcast_fusion
  98.2 1.4 pad_maximum_fusion.boxes
  99.5 6.8 %shard_map.182 = (f32[4,128,256]{2,1,0:T(8,128)}, f32[4,64,256]{2,1,0:T(8,128)}) custom-call(bf16[4,3,16,16,256]{4,3,2,1,0:T(8,128)(2,1)} %pad_maximum_fusion.boxes, bf16[40,256,256]{2,1,0:T(8,128)(2,1)} %transfer.1), custom_call_target="tpu_custom_call" | custom-call | tf_op jit(solution)/shard_map/pallas_call | solution.py:419
  106.3 1.6 %slice.124 = f32[4,4,8,256]{3,2,1,0:T(8,128)} slice(f32[4,4,16,256]{3,2,1,0:T(8,128)} %bitcast.33), slice={[0:4], [0:4], [0:8], [0:256]} | slice | bytes 262144 | tf_op jit(solution)/shard_map/slice | solution.py:422
  107.9 0.0 all-to-all-done.gathered
  107.9 0.7 copy-done.3
  108.6 35.7 %shard_map.184 = f32[16,1024]{1,0:T(8,128)} custom-call(s32[2]{0:T(128)} %pad_add_fusion.place, f32[128,2,256]{2,1,0:T(2,128)} %copy-done.3, f32[256,256]{1,0:T(8,128)} %lattice.1, f32[2,256,256]{2,1,0:T(8,128)} %pair_down.1, f32[4,256,256]{2,1,0:T(8,128)} %down_child.1, f32[128,128]{1,0:T(8,128)} %constant.31.clone.perm8, f32[32,32]{1,0:T(8,128)} %constant.32.clone.perm4, ...), custom_call_target="tpu_custom_call" | custom-call | tf_op jit(solution)/shard_map/pallas_call | solution.py:424
  144.3 1.6 %reshape.144 = f32[16,16,64]{2,1,0:T(8,128)} reshape(f32[16,1024]{1,0:T(8,128)} %shard_map.184) | data formatting | bytes 131072 | tf_op jit(solution)/shard_map/reshape | solution.py:432
  (24 shorter events, 0.4 us)
Async XLA Ops:
  3.1 5.4 %copy-start.7 = (f32[3,256]{1,0:T(4,128)S(1)}, f32[3,256]{1,0:T(4,128)}, u32[]{:S(2)}) copy-start(f32[3,256]{1,0:T(4,128)} %param.24) | copy-start | bytes 9220
  5.5 4.2 %copy-start = (f32[16,8,1024]{2,1,0:T(8,128)}, f32[16,8,1024]{2,1,0:T(8,128)S(1)}, u32[]{:S(2)}) copy-start(f32[16,8,1024]{2,1,0:T(8,128)S(1)} %stack.33.pts) | copy-start | bytes 1572868
  5.6 46.3 %collective-permute-start.4 = (f32[1,8,1024]{2,1,0:T(8,128)S(1)}, f32[1,8,1024]{2,1,0:T(8,128)S(1)}, u32[]{:S(2)}, u32[]{:S(2)}) collective-permute-start(f32[1,8,1024]{2,1,0:T(8,128)S(1)} %get-tuple-element.21), channel_id=1, source_target_pairs={{0,16},{16,32},{32,48},{48,64},{64,80},{80,96},{96,112},{112,0},{1... | collective-permute-start | bytes 98312 | tf_op jit(solution)/shard_map/ppermute | solution.py:333
  5.6 46.2 %collective-permute-start.5 = (f32[1,8,1024]{2,1,0:T(8,128)S(1)}, f32[1,8,1024]{2,1,0:T(8,128)S(1)}, u32[]{:S(2)}, u32[]{:S(2)}) collective-permute-start(f32[1,8,1024]{2,1,0:T(8,128)S(1)} %get-tuple-element.22), channel_id=1, source_target_pairs={{0,112},{16,0},{32,16},{48,32},{64,48},{80,64},{96,80},{112,96},{1... | collective-permute-start | bytes 98312 | tf_op jit(solution)/shard_map/ppermute | solution.py:336
  9.7 40.1 %copy-start.4 = (f32[16,16,64]{2,1,0:T(8,128)S(1)}, f32[16,16,64]{2,1,0:T(8,128)}, u32[]{:S(2)}) copy-start(f32[16,16,64]{2,1,0:T(8,128)} %param.21) | copy-start | bytes 196612
  9.7 40.8 %copy-start.6 = (f32[16,16,64]{2,1,0:T(8,128)S(1)}, f32[16,16,64]{2,1,0:T(8,128)}, u32[]{:S(2)}) copy-start(f32[16,16,64]{2,1,0:T(8,128)} %param.22) | copy-start | bytes 196612
  34.6 16.7 %copy-start.8 = (f32[3,256]{1,0:T(4,128)S(1)}, f32[3,256]{1,0:T(4,128)}, u32[]{:S(2)}) copy-start(f32[3,256]{1,0:T(4,128)} %param.25) | copy-start | bytes 9220
  34.6 17.3 %copy-start.1 = (f32[16,8,1024]{2,1,0:T(8,128)S(1)}, f32[16,8,1024]{2,1,0:T(8,128)}, u32[]{:S(2)}) copy-start(f32[16,8,1024]{2,1,0:T(8,128)} %copy-done) | copy-start | bytes 1572868
  35.5 21.9 %collective-permute-start = (bf16[4,2,16,256]{3,2,1,0:T(8,128)(2,1)S(1)}, bf16[4,2,16,256]{3,2,1,0:T(8,128)(2,1)S(1)}, u32[]{:S(2)}, u32[]{:S(2)}) collective-permute-start(bf16[4,2,16,256]{3,2,1,0:T(8,128)(2,1)S(1)} %pad_maximum_fusion.9), channel_id=1, source_target_pairs={{0,1},{1,2},{2,3},{3,4},{4,5},{5,6},{6,7},{7,8},{8,9},{9,10},{10,1... | collective-permute-start | bytes 196616 | tf_op jit(solution)/shard_map/ppermute | solution.py:396
  37.5 19.9 %copy-start.2 = (bf16[512,256]{1,0:T(8,128)(2,1)S(1)}, bf16[512,256]{1,0:T(8,128)(2,1)}, u32[]{:S(2)}) copy-start(bf16[512,256]{1,0:T(8,128)(2,1)} %get-tuple-element.12) | copy-start | bytes 786436
  37.5 19.9 %collective-permute-start.1 = (bf16[4,2,16,256]{3,2,1,0:T(8,128)(2,1)S(1)}, bf16[4,2,16,256]{3,2,1,0:T(8,128)(2,1)S(1)}, u32[]{:S(2)}, u32[]{:S(2)}) collective-permute-start(bf16[4,2,16,256]{3,2,1,0:T(8,128)(2,1)S(1)} %pad_maximum_fusion.10), channel_id=1, source_target_pairs={{0,15},{1,0},{2,1},{3,2},{4,3},{5,4},{6,5},{7,6},{8,7},{9,8},{10,9... | collective-permute-start | bytes 196616 | tf_op jit(solution)/shard_map/ppermute | solution.py:397
  43.4 64.5 %all-to-all-start = ((f32[128,2,256]{2,1,0:T(2,128)}), f32[128,2,256]{2,1,0:T(2,128)S(1)}, u32[]{:S(2)}, u32[]{:S(2)}) async-start(f32[128,2,256]{2,1,0:T(2,128)} %broadcast_in_dim.2), calls=%async_computation | async-start | bytes 524288 | tf_op jit(solution)/shard_map/all_to_all | solution.py:384
  49.1 8.4 %copy-start.5 = (bf16[128,256]{1,0:T(8,128)(2,1)S(1)}, bf16[128,256]{1,0:T(8,128)(2,1)}, u32[]{:S(2)}) copy-start(bf16[128,256]{1,0:T(8,128)(2,1)} %get-tuple-element.13) | copy-start | bytes 196612
  52.0 8.0 %collective-permute-start.6 = (f32[18,8,64]{2,1,0:T(8,128)S(1)}, f32[18,8,64]{2,1,0:T(8,128)S(1)}, u32[]{:S(2)}, u32[]{:S(2)}) collective-permute-start(f32[18,8,64]{2,1,0:T(8,128)S(1)} %get-tuple-element.20), channel_id=1, source_target_pairs={{0,1},{1,2},{2,3},{3,4},{4,5},{5,6},{6,7},{7,8},{8,9},{9,10},{10,1... | collective-permute-start | bytes 110600 | tf_op jit(solution)/shard_map/ppermute | solution.py:333
  53.1 6.9 %collective-permute-start.7 = (f32[18,8,64]{2,1,0:T(8,128)S(1)}, f32[18,8,64]{2,1,0:T(8,128)S(1)}, u32[]{:S(2)}, u32[]{:S(2)}) collective-permute-start(f32[18,8,64]{2,1,0:T(8,128)S(1)} %get-tuple-element.19), channel_id=1, source_target_pairs={{0,15},{1,0},{2,1},{3,2},{4,3},{5,4},{6,5},{7,6},{8,7},{9,8},{10,9... | collective-permute-start | bytes 110600 | tf_op jit(solution)/shard_map/ppermute | solution.py:336
  57.6 40.0 %collective-permute-start.3 = (bf16[4,16,2,256]{3,2,1,0:T(2,128)(2,1)S(1)}, bf16[4,16,2,256]{3,2,1,0:T(2,128)(2,1)S(1)}, u32[]{:S(2)}, u32[]{:S(2)}) collective-permute-start(bf16[4,16,2,256]{3,2,1,0:T(2,128)(2,1)S(1)} %slice.119), channel_id=1, source_target_pairs={{0,112},{16,0},{32,16},{48,32},{64,48},{80,64},{96,80},{112,96},{1... | collective-permute-start | bytes 196616 | tf_op jit(solution)/shard_map/ppermute | solution.py:403
  60.0 37.9 %collective-permute-start.2 = (bf16[4,16,2,256]{3,2,1,0:T(2,128)(2,1)S(1)}, bf16[4,16,2,256]{3,2,1,0:T(2,128)(2,1)S(1)}, u32[]{:S(2)}, u32[]{:S(2)}) collective-permute-start(bf16[4,16,2,256]{3,2,1,0:T(2,128)(2,1)S(1)} %fusion.3), channel_id=1, source_target_pairs={{0,16},{16,32},{32,48},{48,64},{64,80},{80,96},{96,112},{112,0},{1... | collective-permute-start | bytes 196616 | tf_op jit(solution)/shard_map/ppermute | solution.py:402
  107.9 0.7 copy-start.3

commit v2 on v1

v2 whole, which is shorter than its diff:
```python
import jax
import jax.numpy as jnp
import numpy as np
from jax import lax
from jax.experimental import pallas as pl
from jax.experimental.pallas import tpu as pltpu
from jax.sharding import PartitionSpec as P

f32 = jnp.float32
bf16 = jnp.bfloat16
scale_frac = 0.4
NX = 16
LANES = NX * 64
PADDED = LANES + 128
FEATS = 64
AXES = ("gx", "gy")
VMEM = pl.BlockSpec(memory_space=pltpu.VMEM)
PARAMS = pltpu.CompilerParams(vmem_limit_bytes=60 << 20)


def far_offsets():
    return [
        (x, y) for x in range(-3, 4) for y in range(-3, 4) if max(abs(x), abs(y)) >= 2
    ]


def dot(a, b):
    return jnp.dot(a, b, preferred_element_type=f32)


def dot_t(a, b):
    return lax.dot_general(a, b, (((1,), (1,)), ((), ())), preferred_element_type=f32)


def split3(block):
    hi = block.astype(bf16).astype(f32)
    rest = block - hi
    mid = rest.astype(bf16).astype(f32)
    return hi, mid, rest - mid


def centred(block):
    row = lax.broadcasted_iota(jnp.int32, block.shape, 0)
    moved = jnp.where(row < 3, 5.0 * block - 2.5, 0.0)
    return row, moved, jnp.sum(moved * moved, axis=0, keepdims=True)


def row_feats(block):
    row, moved, norm = centred(block)
    packed = jnp.where(
        row < 3, moved, jnp.where(row == 5, norm + 1.0, jnp.where(row == 6, 1.0, 0.0))
    )
    hi, mid, lo = split3(packed)
    role = jnp.concatenate(
        [hi[0:1], mid[0:1], lo[0:1], hi[1:2], mid[1:2], lo[1:2], hi[6:7] * 25.0, hi[7:8]], axis=0
    )
    tens = jnp.where(row < 6, 10.0, 0.0)
    return jnp.concatenate([hi, hi, hi, mid, mid, lo, role, tens], axis=0).astype(bf16)


def col_feats(block, role_scale=1.0):
    row, moved, norm = centred(block)
    packed = jnp.where(row < 3, moved, jnp.where(row == 6, norm, 0.0))
    hi, mid, lo = split3(packed)
    one = jnp.where(row == 5, 1.0, 0.0)
    def part(value, marks, keep_norm):
        out = jnp.where(row < 3, value * -2.0, 0.0)
        if keep_norm:
            out = jnp.where(row == 6, value, out)
        return out + one if marks else out
    ones = jnp.where(row < 7, 1.0, 0.0)
    role = jnp.concatenate(
        [hi[0:1], mid[0:1], lo[0:1], hi[1:2], mid[1:2], lo[1:2], hi[7:8], hi[7:8]], axis=0
    )
    return jnp.concatenate(
        [
            part(hi, True, True),
            part(mid, False, True),
            part(lo, False, True),
            part(hi, True, False),
            part(mid, False, False),
            part(hi, True, False),
            ones * role_scale,
            role * role_scale,
        ],
        axis=0,
    ).astype(bf16)


def power(u):
    return jnp.exp2(jnp.log2(u) * -2.25)


def box_perm(side):
    order = []
    for e in (0, 1):
        for f in (0, 1):
            for b in range(side):
                for a in range(side):
                    for c in (0, 1):
                        order.append(((2 * b + f) * 2 * side + 2 * a + e) * 2 + c)
    out = np.zeros((len(order), len(order)), np.float32)
    out[np.arange(len(order)), order] = 1.0
    return out


def eye(n):
    return (
        lax.broadcasted_iota(jnp.int32, (n, n), 0) == lax.broadcasted_iota(jnp.int32, (n, n), 1)
    ).astype(bf16)


def split_into(source, hi, lo, first):
    def part(i, carry):
        rows = pl.ds(pl.multiple_of(i * 64, 64), 64)
        for n in range(source.shape[0]):
            w = source[n, rows, :]
            h = w.astype(bf16)
            hi[first + n, rows, :] = h
            lo[first + n, rows, :] = (w - h.astype(f32)).astype(bf16)
        return carry

    lax.fori_loop(0, 4, part, 0)


def dot3(x, hi, lo):
    n = x.shape[0]
    top = x.astype(bf16).astype(f32)
    both = jnp.concatenate([top, x - top], axis=0).astype(bf16)
    main = dot(both, hi)
    if n % 16:
        rest = dot(both, lo)
        return main[:n] + main[n:] + rest[:n]
    return main[:n] + main[n:] + dot(top.astype(bf16), lo)


def permute(perm, x):
    hi, mid, lo = split3(x)
    out = dot(perm, jnp.concatenate([hi, mid, lo], axis=1).astype(bf16))
    return out[:, :256] + out[:, 256:512] + out[:, 512:]


def gather4(blocks, hi, lo, first):
    n = blocks.shape[0] // 4
    total = None
    for p in range(4):
        term = dot3(blocks[p * n : (p + 1) * n], hi[first + p], lo[first + p])
        total = term if total is None else total + term
    return total


def pairs(ref, *index):
    even = ref[(*index, pl.ds(0, NX // 2, stride=2))]
    odd = ref[(*index, pl.ds(1, NX // 2, stride=2))]
    return jnp.concatenate([even, odd], axis=1)


def live_pairs(counts, a):
    n = counts[pl.ds(pl.multiple_of(a * 8, 8), 8), :]
    lane = lax.broadcasted_iota(jnp.int32, (8, 128), 1)
    return lax.rem(lane, 64) < jnp.where(lane < 64, n[:, 0:1], n[:, 1:2])


def pad_points(points):
    return jnp.concatenate([points[...], jnp.zeros((5, 256), f32)], axis=0)


def upward_kernel(
    coords, weights, solution, counts, check_pts, solve, up_child, pair_up, perm8, perm4,
    feats, pts, boxes, gy_next, gy_prev, gx_edge, up_out,
    u0, u1, w0, w1, pot, hi, lo,
):
    check_cols = col_feats(pad_points(check_pts), 0.0)
    ident = eye(128)
    split_into(solve, hi, lo, 0)
    split_into(up_child, hi, lo, 1)
    split_into(pair_up, hi, lo, 5)

    def prepare(a, u, w):
        alive = live_pairs(counts, a)
        weight = jnp.where(alive, pairs(weights, a), 0.0)
        parts = [pairs(coords, c, a) for c in range(3)]
        parts += [weight, weight * pairs(solution, a)]
        zero = jnp.zeros((3, 128), f32)
        block = jnp.concatenate(
            [
                jnp.concatenate([x[m : m + 1] for x in parts] + [zero], axis=0)
                for m in range(NX // 2)
            ],
            axis=1,
        )
        pts[a] = block
        rows = row_feats(block)
        for m in range(NX // 2):
            lanes = slice(128 * m, 128 * m + 128)
            f = dot_t(ident, rows[:, lanes]).astype(bf16)
            feats[pl.ds(pl.multiple_of(a * LANES + 128 * m, 128), 128), :] = f
            w[lanes, :] = jnp.transpose(block[:, lanes])
            u[lanes, :] = dot(f, check_cols)

    def finish(a, u, w):
        for m in range(NX // 2):
            for half in range(2):
                span = slice(128 * m + 64 * half, 128 * m + 64 * half + 64)
                k = power(u[span, :])
                at = (lax.rem(a, 2) * 2 + half) * 128 + m * 16 + lax.div(a, 2) * 2
                for c in range(2):
                    pot[pl.ds(at + c, 1), :] = jnp.sum(
                        k * w[span, 3 + c : 4 + c], axis=0, keepdims=True
                    )

    prepare(0, u0, w0)

    def step(i, carry):
        prepare(2 * i + 1, u1, w1)
        finish(2 * i, u0, w0)
        prepare(jnp.minimum(2 * i + 2, NX - 1), u0, w0)
        finish(2 * i + 1, u1, w1)
        return carry

    lax.fori_loop(0, NX // 2, step, 0)
    leaf = dot3(pot[...], hi[0], lo[0])
    parent = permute(perm8[...], gather4(leaf, hi, lo, 1))
    leaf_r = leaf.astype(bf16).astype(f32)
    parent_r = parent.astype(bf16).astype(f32)
    for p in range(4):
        own = leaf_r[128 * p : 128 * p + 128]
        coarse = parent_r[32 * p : 32 * p + 32]
        for b in range(8):
            boxes[p, b] = own[16 * b : 16 * b + 16]
        for b in range(4):
            boxes[p, 8 + b, 0:8] = coarse[8 * b : 8 * b + 8]
            boxes[p, 8 + b, 8:16] = jnp.zeros((8, 256), f32)
        for msg, b, bb in ((gy_next, 7, 3), (gy_prev, 0, 0)):
            msg[16 * p : 16 * p + 16, :] = own[16 * b : 16 * b + 16]
            msg[64 + 8 * p : 72 + 8 * p, :] = coarse[8 * bb : 8 * bb + 8]
        for e in range(2):
            for c in range(2):
                at = 64 * c + 16 * p
                for b in range(8):
                    row = 16 * b + 14 * e + c
                    gx_edge[e, at + 1 + b : at + 2 + b, :] = own[row : row + 1]
                for b in range(4):
                    row = 8 * b + 6 * e + c
                    gx_edge[e, at + 11 + b : at + 12 + b, :] = coarse[row : row + 1]
                for gap in (0, 9, 10, 15):
                    gx_edge[e, at + gap : at + gap + 1, :] = jnp.zeros((1, 256), f32)
    for msg, start in ((gy_next, LANES - 64), (gy_prev, 0)):
        for k in range(4):
            piece = pts[4 * k : 4 * k + 4, :, start : start + 64].reshape(32, 64)
            msg[96:128, 64 * k : 64 * k + 64] = piece
    for e, t in ((0, 0), (1, NX - 1)):
        for k in range(4):
            gx_edge[e, 128 + 8 * k : 136 + 8 * k, :] = pts[t, :, 256 * k : 256 * k + 256]
        gx_edge[e, 160:168, :] = jnp.zeros((8, 256), f32)
    grand = permute(perm4[...], gather4(parent, hi, lo, 1))
    great = gather4(grand, hi, lo, 1)
    vec = None
    for b in range(2):
        for a in range(2):
            at = (b * 2 + a) * 2
            rows = jnp.concatenate([great[at : at + 2]] * 4, axis=0)
            term = dot3(rows, hi[1 + 2 * a + b], lo[1 + 2 * a + b])
            vec = term if vec is None else vec + term
    for axis, bits in ((1, 4), (0, 3)):
        place = lax.axis_index(AXES[axis])
        for bit in range(bits):
            n = 5 + lax.rem(lax.div(place, 2**bit), 2)
            vec = dot3(vec, hi[n], lo[n])
    up_out[...] = vec


def pack_kernel(low, high, edge, out):
    out[...] = edge[...]
    for e in range(2):
        for p in range(4):
            for c in range(2):
                at = 64 * c + 16 * p
                fine = 16 * p + 14 * e + c
                coarse = 64 + 8 * p + 6 * e + c
                for gap, ref, row in (
                    (0, low, fine), (9, high, fine), (10, low, coarse), (15, high, coarse)
                ):
                    out[e, at + gap : at + gap + 1, :] = ref[row : row + 1, :]
        rows = slice(96, 104) if e == 0 else slice(120, 128)
        lanes = slice(0, 64) if e == 0 else slice(192, 256)
        out[e, 160:168, 0:64] = low[rows, lanes]
        out[e, 160:168, 64:128] = high[rows, lanes]


def role_tiles():
    def column(sx, sy):
        return [-10.0 * sx] * 3 + [-10.0 * sy] * 3 + [float(sx * sx + sy * sy), 0.0] + [
            float(sx)
        ] * 3 + [float(sy)] * 3 + [0.0, 0.0]
    pairs = [((t, -1), (t, 0)) for t in (-1, 0, 1)] + [((-1, 1), (0, 1)), ((1, 1), (1, 1))]
    out = np.zeros((5, 16, 128), np.float32)
    for n, (left, right) in enumerate(pairs):
        out[n, :, :64] = np.array(column(*left))[:, None]
        out[n, :, 64:] = np.array(column(*right))[:, None]
    return out


def sum_lanes(acc0, acc1):
    row = lax.broadcasted_iota(jnp.int32, (8, 256), 0)
    total = None
    for c, acc in enumerate((acc0, acc1)):
        hi = acc.astype(bf16)
        lo = (acc - hi.astype(f32)).astype(bf16)
        ones = jnp.where(row == c, 1.0, 0.0).astype(bf16)
        term = dot_t(ones, jnp.concatenate([hi, lo], axis=1))
        total = term if total is None else total + term
    return total


def middle_kernel(
    pts, gy_low, gy_high, gx_low, gx_high, feats, boxes, roles, transfer_hbm,
    near, leaf_out, parent_out,
    transfer, arrived, dens0, dens1, cols0, cols1, u0, u1, extended, windows,
):
    fetch = pltpu.make_async_copy(transfer_hbm, transfer, arrived)
    fetch.start()
    first = lax.broadcasted_iota(jnp.int32, (1, 128), 1) < 64
    first_cols = lax.broadcasted_iota(jnp.int32, (FEATS, 128), 1) < 64

    for t in range(NX + 2):
        if t in (0, NX + 1):
            ref = gx_low if t == 0 else gx_high
            own = jnp.concatenate([ref[128 + 8 * k : 136 + 8 * k, :] for k in range(4)], axis=1)
            low, high = ref[160:168, 0:64], ref[160:168, 64:128]
        else:
            s = t - 1
            rows = slice(96 + 8 * (s % 4), 104 + 8 * (s % 4))
            lanes = slice(64 * (s // 4), 64 * (s // 4) + 64)
            own, low, high = pts[s], gy_low[rows, lanes], gy_high[rows, lanes]
        dens0[t, :, 0:64] = low
        dens0[t, :, 64 : 64 + LANES] = own
        dens0[t, :, 64 + LANES :] = high
        dens1[t, :, 0:LANES] = own
        dens1[t, :, LANES : LANES + 64] = high
        dens1[t, :, LANES + 64 :] = jnp.zeros((8, 64), f32)

    def prepare(t, carry):
        cols0[t] = col_feats(dens0[t])
        cols1[t] = col_feats(dens1[t])
        return carry

    lax.fori_loop(0, NX + 2, prepare, 0)

    def distances(a, half, u):
        for mm in range(4):
            base = half * 512 + mm * 128
            here, after = slice(base, base + 128), slice(base + 128, base + 256)
            for odd in range(2):
                own, other = ((cols0, cols1), (cols1, cols0))[odd]
                far = here if odd == 0 else after
                blocks = [own[a + t, :, here] for t in range(3)]
                blocks.append(jnp.where(first_cols, own[a, :, after], other[a + 1, :, far]))
                blocks.append(own[a + 2, :, after])
                blocks = [
                    jnp.concatenate([x[:48], x[48:] * roles[n]], axis=0)
                    for n, x in enumerate(blocks)
                ]
                start = pl.multiple_of(a * LANES + base + 64 * odd, 64)
                rows = feats[pl.ds(start, 64), :]
                at = 64 * (2 * mm + odd)
                u[at : at + 64, :] = dot(rows, jnp.concatenate(blocks, axis=1))

    def finish(a, half, u):
        for mm in range(4):
            base = half * 512 + mm * 128
            here, after = slice(base, base + 128), slice(base + 128, base + 256)
            sums = []
            for odd in range(2):
                d_own, d_other = ((dens0, dens1), (dens1, dens0))[odd]
                far = here if odd == 0 else after
                accs = [None, None]
                at = 64 * (2 * mm + odd)
                for n in range(5):
                    k = power(u[at : at + 64, 128 * n : 128 * n + 128])
                    for c in range(2):
                        r = slice(3 + c, 4 + c)
                        if n < 3:
                            dens = d_own[a + n, r, here]
                        elif n == 3:
                            dens = jnp.where(first, d_own[a, r, after], d_other[a + 1, r, far])
                        else:
                            dens = jnp.where(first, d_own[a + 2, r, after], 0.0)
                        term = k * dens
                        accs[c] = term if n == 0 else accs[c] + term
                sums.append(accs)
            both = [jnp.concatenate([sums[0][c], sums[1][c]], axis=0) for c in range(2)]
            total = sum_lanes(*both)
            for c in range(2):
                near[c, pl.ds(a * 8 + half * 4 + mm, 1), :] = total[c : c + 1]

    distances(0, 0, u0)

    def step(a, carry):
        distances(a, 1, u1)
        finish(a, 0, u0)
        distances(jnp.minimum(a + 1, NX - 1), 0, u0)
        finish(a, 1, u1)
        return carry

    lax.fori_loop(0, NX, step, 0)

    blank = jnp.zeros((8, 256), f32)
    for p in range(4):
        for slot in range(16):
            n = p * 16 + slot
            own_rows = extended.at[p, slot]
            if slot in (0, 9):
                own_rows[8:24, :] = (gy_low if slot == 0 else gy_high)[16 * p : 16 * p + 16, :]
            elif slot in (10, 15):
                ref = gy_low if slot == 10 else gy_high
                own_rows[8:16, :] = ref[64 + 8 * p : 72 + 8 * p, :]
                own_rows[16:24, :] = blank
            else:
                own_rows[8:24, :] = boxes[p, slot - 1 if slot < 9 else slot - 3]
            end = 24 if slot < 10 else 16
            for c in range(2):
                row = 64 * c + n
                own_rows[6 + c : 7 + c, :] = gx_low[row : row + 1, :]
                own_rows[end + c : end + c + 1, :] = gx_high[row : row + 1, :]
            if slot >= 10:
                own_rows[24:26, :] = jnp.zeros((2, 256), f32)
            for d in range(3):
                windows[p, d, slot] = own_rows[6 + 2 * d : 22 + 2 * d, :].astype(bf16)
    fetch.wait()
    far_level(windows, transfer, leaf_out, parent_out)


def reachable(parity, shift):
    return abs((parity + shift) // 2) <= 1


def far_level(boxes, transfer, leaf_out, parent_out):
    for px in (0, 1):
        for py in (0, 1):
            total = None
            for number, (sx, sy) in enumerate(far_offsets()):
                if not (reachable(px, sx) and reachable(py, sy)):
                    continue
                dx, dy = (px + sx) // 2, (py + sy) // 2
                source = (px + sx) % 2 * 2 + (py + sy) % 2
                window = jnp.concatenate(
                    [
                        boxes[source, dx + 1, 1 + dy : 9 + dy].reshape(128, 256),
                        boxes[source, dx + 1, 11 + dy : 15 + dy].reshape(64, 256),
                    ],
                    axis=0,
                )
                term = dot(window, transfer[number])
                total = term if total is None else total + term
            p = px * 2 + py
            leaf_out[128 * p : 128 * p + 128, :] = total[:128]
            for b in range(4):
                at = 32 * p + 8 * b
                parent_out[at : at + 8, :] = total[128 + 16 * b : 136 + 16 * b]


def downward_kernel(
    gathered, lattice, pair_down, down_child, perm8, perm4, far_leaf, far_parent,
    equiv_pts, feats, near, solution, source, counts, out, local, pot, u0, u1, hi, lo,
):
    split_into(lattice, hi, lo, 0)
    split_into(pair_down, hi, lo, 1)
    split_into(down_child, hi, lo, 3)
    vec = jnp.sum(gathered[...], axis=0)
    vec = dot3(jnp.concatenate([vec] * 4, axis=0), hi[0], lo[0])
    for axis, bits in ((0, 3), (1, 4)):
        place = lax.axis_index(AXES[axis])
        for bit in reversed(range(bits)):
            n = 1 + lax.rem(lax.div(place, 2**bit), 2)
            vec = dot3(vec, hi[n], lo[n])
    child = lambda x, p: dot3(x, hi[3 + p], lo[3 + p])
    great = jnp.concatenate([child(vec, 2 * a + b)[:2] for b in range(2) for a in range(2)], axis=0)
    spread = lambda x: jnp.concatenate([child(x, p) for p in range(4)], axis=0)
    grand = permute(perm4[...], spread(great))
    parent = spread(grand) + far_parent[...]
    parent = permute(perm8[...], parent)
    local[...] = spread(parent) + far_leaf[...]
    equiv_cols = col_feats(pad_points(equiv_pts), 0.0)

    def distances(a, half, u):
        rows = feats[pl.ds(pl.multiple_of(a * LANES + half * 512, 512), 512), :]
        u[...] = dot(rows, equiv_cols)

    def finish(a, half, u):
        for mm in range(4):
            m = half * 4 + mm
            accs = [[], []]
            for odd in range(2):
                at = 64 * (2 * mm + odd)
                k = power(u[at : at + 64, :])
                for c in range(2):
                    row = (lax.rem(a, 2) * 2 + odd) * 128 + m * 16 + lax.div(a, 2) * 2 + c
                    weight = local[pl.ds(row, 1), :]
                    accs[c].append(k[:, :128] * weight[:, :128] + k[:, 128:] * weight[:, 128:])
            total = sum_lanes(*[jnp.concatenate(x, axis=0) for x in accs])
            for c in range(2):
                pot[c, pl.ds(a * 8 + m, 1), :] = total[c : c + 1]

    distances(0, 0, u0)

    def step(a, carry):
        distances(a, 1, u1)
        finish(a, 0, u0)
        distances(jnp.minimum(a + 1, NX - 1), 0, u0)
        finish(a, 1, u1)
        return carry

    lax.fori_loop(0, NX, step, 0)
    for a in range(NX):
        rows = slice(8 * a, 8 * a + 8)
        total = [pot[c, rows, :] + near[c, rows, :] for c in range(2)]
        value = pairs(source, a) - scale_frac * (pairs(solution, a) * total[0] - total[1])
        value = jnp.where(live_pairs(counts, a), value, 0.0)
        out[a, pl.ds(0, NX // 2, stride=2), :] = value[:, :64]
        out[a, pl.ds(1, NX // 2, stride=2), :] = value[:, 64:]


def ring(axis, step):
    count = lax.axis_size(axis)
    return [(i, (i + step) % count) for i in range(count)]


def call(kernel, in_specs, out_shape, scratch):
    return pl.pallas_call(
        kernel,
        out_shape=out_shape,
        in_specs=in_specs,
        out_specs=jax.tree.map(lambda _: VMEM, out_shape),
        scratch_shapes=scratch,
        compiler_params=PARAMS,
    )


def shape(*dims, dtype=f32):
    return jax.ShapeDtypeStruct(dims, dtype)


def shards(
    coords, weights, solution, source, counts, check_points, equiv_points, check_solve,
    up_children, far_transfer, down_children, pair_up, lattice_map, pair_down,
):
    counts = counts.reshape(NX * NX // 2, 2)
    perm8, perm4 = box_perm(4), box_perm(2)
    halves = [pltpu.VMEM((7, 256, 256), bf16)] * 2
    feats, pts, boxes, gy_next, gy_prev, gx_edge, up = call(
        upward_kernel,
        [VMEM] * 10,
        (
            shape(NX * LANES, FEATS, dtype=bf16),
            shape(NX, 8, LANES),
            shape(4, 12, 16, 256),
            shape(128, 256),
            shape(128, 256),
            shape(2, 168, 256),
            shape(8, 256),
        ),
        [pltpu.VMEM((LANES, 256), f32)] * 2
        + [pltpu.VMEM((LANES, 8), f32)] * 2
        + [pltpu.VMEM((512, 256), f32)]
        + halves,
    )(
        coords, weights, solution, counts, check_points, check_solve[None], up_children, pair_up,
        jnp.asarray(perm8, bf16), jnp.asarray(perm4, bf16),
    )
    gy_low = lax.ppermute(gy_next, "gy", ring("gy", 1))
    gy_high = lax.ppermute(gy_prev, "gy", ring("gy", -1))
    edge = call(pack_kernel, [VMEM] * 3, shape(2, 168, 256), [])(gy_low, gy_high, gx_edge)
    gx_low = lax.ppermute(edge[1], "gx", ring("gx", 1))
    gx_high = lax.ppermute(edge[0], "gx", ring("gx", -1))
    gathered = lax.all_to_all(
        jnp.broadcast_to(up[None, :2], (128, 2, 256)), AXES, 0, 0, tiled=True
    )
    near, far_leaf, far_parent = call(
        middle_kernel,
        [VMEM] * 8 + [pl.BlockSpec(memory_space=pl.ANY)],
        (shape(2, 128, 128), shape(512, 256), shape(128, 256)),
        [pltpu.VMEM((40, 256, 256), bf16), pltpu.SemaphoreType.DMA]
        + [pltpu.VMEM((NX + 2, 8, PADDED), f32)] * 2
        + [pltpu.VMEM((NX + 2, FEATS, PADDED), bf16)] * 2
        + [pltpu.VMEM((512, 640), f32)] * 2
        + [pltpu.VMEM((4, 16, 32, 256), f32), pltpu.VMEM((4, 3, 16, 16, 256), bf16)],
    )(
        pts, gy_low, gy_high, gx_low, gx_high, feats, boxes, jnp.asarray(role_tiles(), bf16),
        far_transfer,
    )
    return call(
        downward_kernel,
        [VMEM] * 14,
        shape(NX, NX, 64),
        [pltpu.VMEM((512, 256), f32), pltpu.VMEM((2, 128, 128), f32)]
        + [pltpu.VMEM((512, 256), f32)] * 2
        + halves,
    )(
        gathered, lattice_map[None], pair_down, down_children,
        jnp.asarray(perm8.T, bf16), jnp.asarray(perm4.T, bf16), far_leaf, far_parent,
        equiv_points, feats, near, solution, source, counts,
    )


def solution(mesh):
    box = P("gx", "gy", None)
    return jax.shard_map(
        shards,
        mesh=mesh,
        in_specs=(P(None, "gx", "gy", None), box, box, box, P("gx", "gy")) + (P(),) * 9,
        out_specs=box,
        check_vma=False,
    )
```

time: 147 us -> 97.7 us (0.66)
  Pallas kernels: 104 us -> 70.2 us
  local copies, waits for them, and re-layouts: 15.6 us -> 5.93 us
  starting transfers between devices: 22.8 us -> 15.2 us
  waiting for transfers between devices: 0.03 us -> 6.04 us
  other arithmetic: 3.42 us -> 0 us
    pallas_call x4, Pallas kernels: 104 us -> 70.2 us  [the longest x1 30.7 us: shards(): call(middle_kernel, [VMEM] * 8 + [pl.BlockSpec(memory_space=pl.ANY)], (sh...]
    ppermute x8 -> x4, starting transfers between devices: 17.1 us -> 8.38 us  [the longest x1 4.39 us: shards(): gy_high = lax.ppermute(gy_prev, 'gy', ring('gy', -1))]
    ppermute x8 -> x4, waiting for transfers between devices: 0.02 us -> 6.04 us  [the longest x1 3.11 us: shards(): gx_low = lax.ppermute(edge[1], 'gx', ring('gx', 1))]
    slice x10 -> x0, local copies, waits for them, and re-layouts: 3.72 us -> none  [the longest x1 1.57 us: shards(): far_parent = far_parent.reshape(4, 4, 16, 256)[:, :, :8].reshape(128, 256)]
    reshape x5 -> x1, local copies, waits for them, and re-layouts: 5.06 us -> 1.4 us  [shards(): counts = counts.reshape(NX * NX // 2, 2)]
    another operation x4 -> x0, other arithmetic: 2.49 us -> none  [the longest x3 1.88 us: shards(): windows = jnp.stack([before, wide, after], axis=1)]
  transfers between devices with their start and end apart: 9 -> 5, of which waited for: 0 -> 2; matrix products, arithmetic and copies ran while one was open for 8% -> 3% of each run, Pallas kernels for 47% -> 34%
where the time goes in v2:
time: 97.7 us; the launch traced here: 97.4 us
  Pallas kernels  70.2 us (72%)
  starting transfers between devices  15.2 us (16%)
  waiting for transfers between devices  6.04 us (6%)
  local copies, waits for them, and re-layouts  5.93 us (6%)
    pallas_call x1, Pallas kernels, shards(): call(middle_kernel, [VMEM] * 8 + [pl.BlockSpec(memory_space=pl.ANY)], (sh...  30.7 us
    pallas_call x1, Pallas kernels, shards(): call(upward_kernel, [VMEM] * 10, (shape(NX * LANES, FEATS, dtype=bf16), s...  21.7 us
    pallas_call x1, Pallas kernels, shards(): call(downward_kernel, [VMEM] * 14, shape(NX, NX, 64), [pltpu.VMEM((512, 2...  15.9 us
    all_to_all x1, starting transfers between devices, shards(): lax.all_to_all(jnp.broadcast_to(up[None, :2], (128, 2, 256)), AXES, 0, 0,...  6.78 us
    ppermute x1, starting transfers between devices, shards(): gy_high = lax.ppermute(gy_prev, 'gy', ring('gy', -1))  4.39 us
    ppermute x1, waiting for transfers between devices, shards(): gx_low = lax.ppermute(edge[1], 'gx', ring('gx', 1))  3.11 us
    ppermute x1, waiting for transfers between devices, shards(): gx_high = lax.ppermute(edge[0], 'gx', ring('gx', -1))  2.92 us
    unnamed x10, local copies, waits for them, and re-layouts  2.03 us
  transfers between devices with their start and end apart: 5, of which 2 were waited for; matrix products, arithmetic and copies ran while one was open for 3% of the time, Pallas kernels for 34%

profile of v2, /device:TPU:0, one launch (start us, length us, event | category | flops | bytes accessed | tf_op | source)
XLA Modules:
  0.0 97.4 jit_solution(14313869838279900673)
XLA Ops:
  0.0 1.4 %reshape.4.counts = s32[128,2]{1,0:T(8,128)} reshape(s32[16,16]{1,0:T(8,128)} %param.23) | data formatting | bytes 2048 | tf_op jit(solution)/shard_map/reshape | solution.py:548
  1.4 21.7 %shard_map.181 = (bf16[16384,64]{1,0:T(8,128)(2,1)}, f32[16,8,1024]{2,1,0:T(8,128)}, f32[4,12,16,256]{3,2,1,0:T(8,128)}, f32[128,256]{1,0:T(8,128)}, f32[128,256...) custom-call(f32[3,16,16,64]{3,2,1,0:T(8,128)} %coords.1, f32[16,16,64]{2,1,0:T(8,128)} %weights.1, ...), custom_call_target="tpu_custom_call" | custom-call | tf_op jit(solution)/shard_map/pallas_call | solution.py:551
  23.1 2.0 %collective-permute-start = (f32[128,256]{1,0:T(8,128)}, f32[128,256]{1,0:T(8,128)S(1)}, u32[]{:S(2)}, u32[]{:S(2)}) collective-permute-start(f32[128,256]{1,0:T(8,128)} %get-tuple-element.17), channel_id=1, source_target_pairs={{0,1},{1,2},{2,3},{3,4},{4,5},{5,6},{6,7},{7,8},{8,9},{9,10},{10,1... | collective-permute-start | bytes 393224 | tf_op jit(solution)/shard_map/ppermute | solution.py:571
  25.1 4.4 %collective-permute-start.1 = (f32[128,256]{1,0:T(8,128)}, f32[128,256]{1,0:T(8,128)S(1)}, u32[]{:S(2)}, u32[]{:S(2)}) collective-permute-start(f32[128,256]{1,0:T(8,128)} %get-tuple-element.18), channel_id=1, source_target_pairs={{0,15},{1,0},{2,1},{3,2},{4,3},{5,4},{6,5},{7,6},{8,7},{9,8},{10,9... | collective-permute-start | bytes 393224 | tf_op jit(solution)/shard_map/ppermute | solution.py:572
  29.5 0.7 slice.9
  30.2 0.8 broadcast_in_dim.13
  30.9 6.8 %all-to-all-start = ((f32[128,2,256]{2,1,0:T(2,128)}), f32[128,2,256]{2,1,0:T(2,128)S(1)}, u32[]{:S(2)}, u32[]{:S(2)}) async-start(f32[128,2,256]{2,1,0:T(2,128)} %broadcast_in_dim.13), calls=%async_computation | async-start | bytes 524288 | tf_op jit(solution)/shard_map/all_to_all | solution.py:576
  37.7 0.0 collective-permute-done.low.gy_low
  37.7 0.0 copy-start.1
  37.7 0.0 collective-permute-done.1.high.gy_high
  37.8 0.0 copy-start.2
  37.8 0.6 copy-done.1
  38.4 0.0 copy-done.2
  38.4 1.9 %shard_map.182 = f32[2,168,256]{2,1,0:T(8,128)} custom-call(f32[128,256]{1,0:T(8,128)} %copy-done.1, f32[128,256]{1,0:T(8,128)} %copy-done.2, f32[2,168,256]{2,1,0:T(8,128)} %get-tuple-element.19.edge), custom_call_target="tpu_custom_call" | custom-call | tf_op jit(solution)/shard_map/pallas_call | solution.py:573
  40.3 1.0 %slice_bitcast_fusion = (f32[168,256]{1,0:T(8,128)S(1)}, f32[168,256]{1,0:T(8,128)S(1)}) fusion(f32[2,168,256]{2,1,0:T(8,128)} %shard_map.182), kind=kLoop, calls=%fused_computation | loop fusion | bytes 688128 | tf_op jit(solution)/shard_map/squeeze | solution.py:575
  41.4 2.0 %collective-permute-start.3 = (f32[168,256]{1,0:T(8,128)S(1)}, f32[168,256]{1,0:T(8,128)S(1)}, u32[]{:S(2)}, u32[]{:S(2)}) collective-permute-start(f32[168,256]{1,0:T(8,128)S(1)} %get-tuple-element.25), channel_id=1, source_target_pairs={{0,112},{16,0},{32,16},{48,32},{64,48},{80,64},{96,80},{112,96},{1... | collective-permute-start | bytes 516104 | tf_op jit(solution)/shard_map/ppermute | solution.py:575
  43.3 0.0 collective-permute-start.2
  43.3 2.9 %collective-permute-done.3.gx_high = f32[168,256]{1,0:T(8,128)S(1)} collective-permute-done((f32[168,256]{1,0:T(8,128)S(1)}, f32[168,256]{1,0:T(8,128)S(1)}, u32[]{:S(2)}, u32[]{:S(2)}) %collective-permute-start.3) | collective-permute-done | bytes 172064 | tf_op jit(solution)/shard_map/ppermute | solution.py:575
  46.3 0.0 copy-start.3
  46.3 3.1 %collective-permute-done.2.gx_low = f32[168,256]{1,0:T(8,128)S(1)} collective-permute-done((f32[168,256]{1,0:T(8,128)S(1)}, f32[168,256]{1,0:T(8,128)S(1)}, u32[]{:S(2)}, u32[]{:S(2)}) %collective-permute-start.2) | collective-permute-done | bytes 172064 | tf_op jit(solution)/shard_map/ppermute | solution.py:574
  49.4 0.0 copy-start.4
  49.4 0.0 copy-done.3
  49.4 0.7 copy-done.4
  50.1 30.7 %shard_map.183 = (f32[2,128,128]{2,1,0:T(8,128)}, f32[512,256]{1,0:T(8,128)}, f32[128,256]{1,0:T(8,128)}) custom-call(f32[16,8,1024]{2,1,0:T(8,128)} %get-tuple-element.16.pts, f32[128,256]{1,0:T(8,128)} %copy-done.1, f32[128,256]{1,0:T(8,128)} %copy-done.2, f32[168,256]{1,0:T(8,128)} %copy-done.4, f32[168,256]{1,0:T(8,128)} %copy-done.3, ...), custom_call_target="tpu_custom_call" | custom-call | tf_op jit(solution)/shard_map/pallas_call | solution.py:579
  80.8 0.0 all-to-all-done.gathered
  80.8 0.0 copy-start
  80.8 0.7 copy-done
  81.5 15.9 %shard_map.184 = f32[16,16,64]{2,1,0:T(8,128)} custom-call(f32[128,2,256]{2,1,0:T(2,128)} %copy-done, f32[1,256,256]{2,1,0:T(8,128)} %bitcast.7, f32[2,256,256]{2,1,0:T(8,128)} %pair_down.1, f32[4,256,256]{2,1,0:T(8,128)} %down_child.1, bf16[128,128]{1,0:T(8,128)(2,1)} %constant.13.clone.perm8, bf16[32,32]{1,0:T(8,128)(2,1)} %constant.14.clone.perm4, ...), custom_call_target="tpu_custom_call" | custom-call | tf_op jit(solution)/shard_map/pallas_call | solution.py:592
Async XLA Ops:
  23.1 14.7 %collective-permute-start = (f32[128,256]{1,0:T(8,128)}, f32[128,256]{1,0:T(8,128)S(1)}, u32[]{:S(2)}, u32[]{:S(2)}) collective-permute-start(f32[128,256]{1,0:T(8,128)} %get-tuple-element.17), channel_id=1, source_target_pairs={{0,1},{1,2},{2,3},{3,4},{4,5},{5,6},{6,7},{7,8},{8,9},{9,10},{10,1... | collective-permute-start | bytes 393224 | tf_op jit(solution)/shard_map/ppermute | solution.py:571
  25.1 12.7 %collective-permute-start.1 = (f32[128,256]{1,0:T(8,128)}, f32[128,256]{1,0:T(8,128)S(1)}, u32[]{:S(2)}, u32[]{:S(2)}) collective-permute-start(f32[128,256]{1,0:T(8,128)} %get-tuple-element.18), channel_id=1, source_target_pairs={{0,15},{1,0},{2,1},{3,2},{4,3},{5,4},{6,5},{7,6},{8,7},{9,8},{10,9... | collective-permute-start | bytes 393224 | tf_op jit(solution)/shard_map/ppermute | solution.py:572
  30.9 49.9 %all-to-all-start = ((f32[128,2,256]{2,1,0:T(2,128)}), f32[128,2,256]{2,1,0:T(2,128)S(1)}, u32[]{:S(2)}, u32[]{:S(2)}) async-start(f32[128,2,256]{2,1,0:T(2,128)} %broadcast_in_dim.13), calls=%async_computation | async-start | bytes 524288 | tf_op jit(solution)/shard_map/all_to_all | solution.py:576
  37.7 0.7 copy-start.1
  37.8 0.7 copy-start.2
  41.4 4.9 %collective-permute-start.3 = (f32[168,256]{1,0:T(8,128)S(1)}, f32[168,256]{1,0:T(8,128)S(1)}, u32[]{:S(2)}, u32[]{:S(2)}) collective-permute-start(f32[168,256]{1,0:T(8,128)S(1)} %get-tuple-element.25), channel_id=1, source_target_pairs={{0,112},{16,0},{32,16},{48,32},{64,48},{80,64},{96,80},{112,96},{1... | collective-permute-start | bytes 516104 | tf_op jit(solution)/shard_map/ppermute | solution.py:575
  43.3 6.0 %collective-permute-start.2 = (f32[168,256]{1,0:T(8,128)S(1)}, f32[168,256]{1,0:T(8,128)S(1)}, u32[]{:S(2)}, u32[]{:S(2)}) collective-permute-start(f32[168,256]{1,0:T(8,128)S(1)} %get-tuple-element.26), channel_id=1, source_target_pairs={{0,16},{16,32},{32,48},{48,64},{64,80},{80,96},{96,112},{112,0},{1... | collective-permute-start | bytes 516104 | tf_op jit(solution)/shard_map/ppermute | solution.py:574
  46.3 3.1 %copy-start.3 = (f32[168,256]{1,0:T(8,128)}, f32[168,256]{1,0:T(8,128)S(1)}, u32[]{:S(2)}) copy-start(f32[168,256]{1,0:T(8,128)S(1)} %collective-permute-done.3.gx_high) | copy-start | bytes 516100
  49.4 0.7 copy-start.4
  80.8 0.7 copy-start

commit v3 on v2

--- a/solution.py
+++ b/solution.py
@@ -156,9 +156,17 @@
 
 
 def live_pairs(counts, a):
-    n = counts[pl.ds(pl.multiple_of(a * 8, 8), 8), :]
-    lane = lax.broadcasted_iota(jnp.int32, (8, 128), 1)
-    return lax.rem(lane, 64) < jnp.where(lane < 64, n[:, 0:1], n[:, 1:2])
+    row = counts[pl.ds(a, 1), :].astype(f32)
+    box = lax.broadcasted_iota(jnp.int32, (NX // 2, NX), 1)
+    pair = 2 * lax.broadcasted_iota(jnp.int32, (NX // 2, NX), 0)
+    n = [jnp.sum(jnp.where(box == pair + odd, row, 0.0), axis=1, keepdims=True) for odd in (0, 1)]
+    lane = lax.broadcasted_iota(jnp.int32, (NX // 2, 128), 1)
+    return lax.rem(lane, 64).astype(f32) < jnp.where(lane < 64, n[0], n[1])
+
+
+def two_parts(x):
+    hi = x.astype(bf16)
+    return hi, (x - hi.astype(f32)).astype(bf16)
 
 
 def pad_points(points):
@@ -168,7 +176,7 @@
 def upward_kernel(
     coords, weights, solution, counts, check_pts, solve, up_child, pair_up, perm8, perm4,
     feats, pts, boxes, gy_next, gy_prev, gx_edge, up_out,
-    u0, u1, w0, w1, pot, hi, lo,
+    u0, u1, densities, pot, hi, lo, kept, kept_sem,
 ):
     check_cols = col_feats(pad_points(check_pts), 0.0)
     ident = eye(128)
@@ -176,49 +184,64 @@
     split_into(up_child, hi, lo, 1)
     split_into(pair_up, hi, lo, 5)
 
-    def prepare(a, u, w):
-        alive = live_pairs(counts, a)
-        weight = jnp.where(alive, pairs(weights, a), 0.0)
-        parts = [pairs(coords, c, a) for c in range(3)]
-        parts += [weight, weight * pairs(solution, a)]
-        zero = jnp.zeros((3, 128), f32)
-        block = jnp.concatenate(
-            [
-                jnp.concatenate([x[m : m + 1] for x in parts] + [zero], axis=0)
-                for m in range(NX // 2)
-            ],
-            axis=1,
-        )
-        pts[a] = block
-        rows = row_feats(block)
-        for m in range(NX // 2):
-            lanes = slice(128 * m, 128 * m + 128)
-            f = dot_t(ident, rows[:, lanes]).astype(bf16)
-            feats[pl.ds(pl.multiple_of(a * LANES + 128 * m, 128), 128), :] = f
-            w[lanes, :] = jnp.transpose(block[:, lanes])
-            u[lanes, :] = dot(f, check_cols)
-
-    def finish(a, u, w):
-        for m in range(NX // 2):
-            for half in range(2):
-                span = slice(128 * m + 64 * half, 128 * m + 64 * half + 64)
-                k = power(u[span, :])
-                at = (lax.rem(a, 2) * 2 + half) * 128 + m * 16 + lax.div(a, 2) * 2
-                for c in range(2):
-                    pot[pl.ds(at + c, 1), :] = jnp.sum(
-                        k * w[span, 3 + c : 4 + c], axis=0, keepdims=True
-                    )
-
-    prepare(0, u0, w0)
-
-    def step(i, carry):
-        prepare(2 * i + 1, u1, w1)
-        finish(2 * i, u0, w0)
-        prepare(jnp.minimum(2 * i + 2, NX - 1), u0, w0)
-        finish(2 * i + 1, u1, w1)
+    row8 = lax.broadcasted_iota(jnp.int32, (8, 128), 0)
+    lane8 = lax.broadcasted_iota(jnp.int32, (8, 128), 1)
+    own_half = lax.rem(lax.div(row8, 2), 2) == lax.div(lane8, 64)
+
+    def prepare(i, carry):
+        for a in (2 * i, 2 * i + 1):
+            weight = jnp.where(live_pairs(counts, a), pairs(weights, a), 0.0)
+            parts = [pairs(coords, c, a) for c in range(3)]
+            parts += [weight, weight * pairs(solution, a)]
+            zero = jnp.zeros((3, 128), f32)
+            for m in range(NX // 2):
+                lanes = slice(128 * m, 128 * m + 128)
+                block = jnp.concatenate([x[m : m + 1] for x in parts] + [zero], axis=0)
+                pts[a, :, lanes] = block
+                f = dot_t(ident, row_feats(block)).astype(bf16)
+                kept[pl.ds(pl.multiple_of(a * LANES + 128 * m, 128), 128), :] = f
+                both = [x[m : m + 1] for x in parts[3:]]
+                dens = jnp.where(own_half, jnp.concatenate(both * 4, axis=0), 0.0)
+                high = dens.astype(bf16).astype(f32)
+                at = pl.multiple_of(a * 64 + 8 * m, 8)
+                densities[pl.ds(at, 8), 0:128] = jnp.where(row8 < 4, high, dens - high)
+                densities[pl.ds(at, 8), 128:256] = jnp.where(row8 < 4, high, 0.0)
         return carry
 
-    lax.fori_loop(0, NX // 2, step, 0)
+    lax.fori_loop(0, NX // 2, prepare, 0)
+    keep = pltpu.make_async_copy(kept, feats, kept_sem)
+    keep.start()
+
+    def distances(a, m, u):
+        rows = kept[pl.ds(pl.multiple_of(a * LANES + 128 * m, 128), 128), :]
+        at = 128 * (m % 4)
+        u[at : at + 128, :] = dot(rows, check_cols)
+
+    def finish(a, m, u):
+        at = 128 * (m % 4)
+        k_hi, k_lo = two_parts(power(u[at : at + 128, :]))
+        dens = densities[pl.ds(pl.multiple_of(a * 64 + 8 * m, 8), 8), :].astype(bf16)
+        sums = dot(dens, jnp.concatenate([k_hi, k_lo], axis=0))
+        sums = sums[:4] + sums[4:]
+        row = lax.rem(a, 2) * 256 + m * 16 + lax.div(a, 2) * 2
+        for half in range(2):
+            for c in range(2):
+                n = 2 * half + c
+                pot[pl.ds(row + 128 * half + c, 1), :] = sums[n : n + 1]
+
+    for m in range(4):
+        distances(0, m, u0)
+
+    def step(a, carry):
+        for m in range(4):
+            finish(a, m, u0)
+            distances(a, m + 4, u1)
+        for m in range(4, 8):
+            finish(a, m, u1)
+            distances(jnp.minimum(a + 1, NX - 1), m - 4, u0)
+        return carry
+
+    lax.fori_loop(0, NX, step, 0)
     leaf = dot3(pot[...], hi[0], lo[0])
     parent = permute(perm8[...], gather4(leaf, hi, lo, 1))
     leaf_r = leaf.astype(bf16).astype(f32)
@@ -267,12 +290,13 @@
         for bit in range(bits):
             n = 5 + lax.rem(lax.div(place, 2**bit), 2)
             vec = dot3(vec, hi[n], lo[n])
-    up_out[...] = vec
-
-
-def pack_kernel(low, high, edge, out):
-    out[...] = edge[...]
-    for e in range(2):
+    up_out[...] = jnp.broadcast_to(vec[None, :2], (128, 2, 256))
+    keep.wait()
+
+
+def pack_kernel(low, high, edge, first, last):
+    for e, out in enumerate((first, last)):
+        out[...] = edge[e]
         for p in range(4):
             for c in range(2):
                 at = 64 * c + 16 * p
@@ -281,11 +305,11 @@
                 for gap, ref, row in (
                     (0, low, fine), (9, high, fine), (10, low, coarse), (15, high, coarse)
                 ):
-                    out[e, at + gap : at + gap + 1, :] = ref[row : row + 1, :]
+                    out[at + gap : at + gap + 1, :] = ref[row : row + 1, :]
         rows = slice(96, 104) if e == 0 else slice(120, 128)
         lanes = slice(0, 64) if e == 0 else slice(192, 256)
-        out[e, 160:168, 0:64] = low[rows, lanes]
-        out[e, 160:168, 64:128] = high[rows, lanes]
+        out[160:168, 0:64] = low[rows, lanes]
+        out[160:168, 64:128] = high[rows, lanes]
 
 
 def role_tiles():
@@ -314,10 +338,12 @@
 
 
 def middle_kernel(
-    pts, gy_low, gy_high, gx_low, gx_high, feats, boxes, roles, transfer_hbm,
+    pts, gy_low, gy_high, gx_low, gx_high, boxes, roles, feats_hbm, transfer_hbm,
     near, leaf_out, parent_out,
-    transfer, arrived, dens0, dens1, cols0, cols1, u0, u1, extended, windows,
+    feats, feats_sem, transfer, arrived, dens0, dens1, cols0, cols1, u0, u1, extended, windows,
 ):
+    load = pltpu.make_async_copy(feats_hbm, feats, feats_sem)
+    load.start()
     fetch = pltpu.make_async_copy(transfer_hbm, transfer, arrived)
     fetch.start()
     first = lax.broadcasted_iota(jnp.int32, (1, 128), 1) < 64
@@ -347,8 +373,8 @@
 
     lax.fori_loop(0, NX + 2, prepare, 0)
 
-    def distances(a, half, u):
-        for mm in range(4):
+    def distances(a, half, u, mms=range(4)):
+        for mm in mms:
             base = half * 512 + mm * 128
             here, after = slice(base, base + 128), slice(base + 128, base + 256)
             for odd in range(2):
@@ -366,8 +392,8 @@
                 at = 64 * (2 * mm + odd)
                 u[at : at + 64, :] = dot(rows, jnp.concatenate(blocks, axis=1))
 
-    def finish(a, half, u):
-        for mm in range(4):
+    def finish(a, half, u, mms=range(4)):
+        for mm in mms:
             base = half * 512 + mm * 128
             here, after = slice(base, base + 128), slice(base + 128, base + 256)
             sums = []
@@ -394,13 +420,16 @@
             for c in range(2):
                 near[c, pl.ds(a * 8 + half * 4 + mm, 1), :] = total[c : c + 1]
 
+    load.wait()
     distances(0, 0, u0)
 
     def step(a, carry):
-        distances(a, 1, u1)
-        finish(a, 0, u0)
-        distances(jnp.minimum(a + 1, NX - 1), 0, u0)
-        finish(a, 1, u1)
+        for mm in range(4):
+            finish(a, 0, u0, (mm,))
+            distances(a, 1, u1, (mm,))
+        for mm in range(4):
+            finish(a, 1, u1, (mm,))
+            distances(jnp.minimum(a + 1, NX - 1), 0, u0, (mm,))
         return carry
 
     lax.fori_loop(0, NX, step, 0)
@@ -462,8 +491,11 @@
 
 def downward_kernel(
     gathered, lattice, pair_down, down_child, perm8, perm4, far_leaf, far_parent,
-    equiv_pts, feats, near, solution, source, counts, out, local, pot, u0, u1, hi, lo,
+    equiv_pts, near, solution, source, counts, feats_hbm, out,
+    local, pot, u0, u1, hi, lo, feats, feats_sem,
 ):
+    load = pltpu.make_async_copy(feats_hbm, feats, feats_sem)
+    load.start()
     split_into(lattice, hi, lo, 0)
     split_into(pair_down, hi, lo, 1)
     split_into(down_child, hi, lo, 3)
@@ -483,32 +515,40 @@
     local[...] = spread(parent) + far_leaf[...]
     equiv_cols = col_feats(pad_points(equiv_pts), 0.0)
 
-    def distances(a, half, u):
-        rows = feats[pl.ds(pl.multiple_of(a * LANES + half * 512, 512), 512), :]
-        u[...] = dot(rows, equiv_cols)
-
-    def finish(a, half, u):
-        for mm in range(4):
-            m = half * 4 + mm
-            accs = [[], []]
-            for odd in range(2):
-                at = 64 * (2 * mm + odd)
-                k = power(u[at : at + 64, :])
-                for c in range(2):
-                    row = (lax.rem(a, 2) * 2 + odd) * 128 + m * 16 + lax.div(a, 2) * 2 + c
-                    weight = local[pl.ds(row, 1), :]
-                    accs[c].append(k[:, :128] * weight[:, :128] + k[:, 128:] * weight[:, 128:])
-            total = sum_lanes(*[jnp.concatenate(x, axis=0) for x in accs])
-            for c in range(2):
-                pot[c, pl.ds(a * 8 + m, 1), :] = total[c : c + 1]
-
-    distances(0, 0, u0)
+    first = lax.broadcasted_iota(jnp.int32, (2, 128), 1) < 64
+    is_top = jnp.where(lax.broadcasted_iota(jnp.int32, (8, 128), 0) < 4, 1.0, 0.0)
+
+    def distances(a, m, u):
+        rows = feats[pl.ds(pl.multiple_of(a * LANES + 128 * m, 128), 128), :]
+        at = 128 * (m % 4)
+        u[at : at + 128, :] = dot(rows, equiv_cols)
+
+    def finish(a, m, u):
+        at = 128 * (m % 4)
+        k_hi, k_lo = two_parts(power(u[at : at + 128, :]))
+        row = lax.rem(a, 2) * 256 + m * 16 + lax.div(a, 2) * 2
+        weight = jnp.concatenate(
+            [local[pl.ds(row + 128 * half + c, 1), :] for half in range(2) for c in range(2)], axis=0
+        )
+        top = weight.astype(bf16).astype(f32)
+        both = jnp.concatenate([top, weight - top], axis=0).astype(bf16)
+        sums = dot_t(both, k_hi) + dot_t(jnp.concatenate([top, top], axis=0).astype(bf16), k_lo) * is_top
+        sums = sums[:4] + sums[4:]
+        total = jnp.where(first, sums[:2], sums[2:])
+        for c in range(2):
+            pot[c, pl.ds(a * 8 + m, 1), :] = total[c : c + 1]
+
+    load.wait()
+    for m in range(4):
+        distances(0, m, u0)
 
     def step(a, carry):
-        distances(a, 1, u1)
-        finish(a, 0, u0)
-        distances(jnp.minimum(a + 1, NX - 1), 0, u0)
-        finish(a, 1, u1)
+        for m in range(4):
+            finish(a, m, u0)
+            distances(a, m + 4, u1)
+        for m in range(4, 8):
+            finish(a, m, u1)
+            distances(jnp.minimum(a + 1, NX - 1), m - 4, u0)
         return carry
 
     lax.fori_loop(0, NX, step, 0)
@@ -526,12 +566,12 @@
     return [(i, (i + step) % count) for i in range(count)]
 
 
-def call(kernel, in_specs, out_shape, scratch):
+def call(kernel, in_specs, out_shape, scratch, out_specs=None):
     return pl.pallas_call(
         kernel,
         out_shape=out_shape,
         in_specs=in_specs,
-        out_specs=jax.tree.map(lambda _: VMEM, out_shape),
+        out_specs=out_specs or jax.tree.map(lambda _: VMEM, out_shape),
         scratch_shapes=scratch,
         compiler_params=PARAMS,
     )
@@ -545,7 +585,6 @@
     coords, weights, solution, source, counts, check_points, equiv_points, check_solve,
     up_children, far_transfer, down_children, pair_up, lattice_map, pair_down,
 ):
-    counts = counts.reshape(NX * NX // 2, 2)
     perm8, perm4 = box_perm(4), box_perm(2)
     halves = [pltpu.VMEM((7, 256, 256), bf16)] * 2
     feats, pts, boxes, gy_next, gy_prev, gx_edge, up = call(
@@ -558,48 +597,52 @@
             shape(128, 256),
             shape(128, 256),
             shape(2, 168, 256),
-            shape(8, 256),
+            shape(128, 2, 256),
         ),
-        [pltpu.VMEM((LANES, 256), f32)] * 2
-        + [pltpu.VMEM((LANES, 8), f32)] * 2
+        [pltpu.VMEM((512, 256), f32)] * 2
+        + [pltpu.VMEM((LANES, 256), f32)]
         + [pltpu.VMEM((512, 256), f32)]
-        + halves,
+        + halves
+        + [pltpu.VMEM((NX * LANES, FEATS), bf16), pltpu.SemaphoreType.DMA],
+        out_specs=(pl.BlockSpec(memory_space=pl.ANY),) + (VMEM,) * 6,
     )(
         coords, weights, solution, counts, check_points, check_solve[None], up_children, pair_up,
         jnp.asarray(perm8, bf16), jnp.asarray(perm4, bf16),
     )
     gy_low = lax.ppermute(gy_next, "gy", ring("gy", 1))
     gy_high = lax.ppermute(gy_prev, "gy", ring("gy", -1))
-    edge = call(pack_kernel, [VMEM] * 3, shape(2, 168, 256), [])(gy_low, gy_high, gx_edge)
-    gx_low = lax.ppermute(edge[1], "gx", ring("gx", 1))
-    gx_high = lax.ppermute(edge[0], "gx", ring("gx", -1))
-    gathered = lax.all_to_all(
-        jnp.broadcast_to(up[None, :2], (128, 2, 256)), AXES, 0, 0, tiled=True
-    )
+    first, last = call(pack_kernel, [VMEM] * 3, (shape(168, 256), shape(168, 256)), [])(
+        gy_low, gy_high, gx_edge
+    )
+    gx_low = lax.ppermute(last, "gx", ring("gx", 1))
+    gx_high = lax.ppermute(first, "gx", ring("gx", -1))
+    gathered = lax.all_to_all(up, AXES, 0, 0, tiled=True)
     near, far_leaf, far_parent = call(
         middle_kernel,
-        [VMEM] * 8 + [pl.BlockSpec(memory_space=pl.ANY)],
+        [VMEM] * 7 + [pl.BlockSpec(memory_space=pl.ANY)] * 2,
         (shape(2, 128, 128), shape(512, 256), shape(128, 256)),
-        [pltpu.VMEM((40, 256, 256), bf16), pltpu.SemaphoreType.DMA]
+        [pltpu.VMEM((NX * LANES, FEATS), bf16), pltpu.SemaphoreType.DMA]
+        + [pltpu.VMEM((40, 256, 256), bf16), pltpu.SemaphoreType.DMA]
         + [pltpu.VMEM((NX + 2, 8, PADDED), f32)] * 2
         + [pltpu.VMEM((NX + 2, FEATS, PADDED), bf16)] * 2
         + [pltpu.VMEM((512, 640), f32)] * 2
         + [pltpu.VMEM((4, 16, 32, 256), f32), pltpu.VMEM((4, 3, 16, 16, 256), bf16)],
     )(
-        pts, gy_low, gy_high, gx_low, gx_high, feats, boxes, jnp.asarray(role_tiles(), bf16),
+        pts, gy_low, gy_high, gx_low, gx_high, boxes, jnp.asarray(role_tiles(), bf16), feats,
         far_transfer,
     )
     return call(
         downward_kernel,
-        [VMEM] * 14,
+        [VMEM] * 13 + [pl.BlockSpec(memory_space=pl.ANY)],
         shape(NX, NX, 64),
         [pltpu.VMEM((512, 256), f32), pltpu.VMEM((2, 128, 128), f32)]
         + [pltpu.VMEM((512, 256), f32)] * 2
-        + halves,
+        + halves
+        + [pltpu.VMEM((NX * LANES, FEATS), bf16), pltpu.SemaphoreType.DMA],
     )(
         gathered, lattice_map[None], pair_down, down_children,
         jnp.asarray(perm8.T, bf16), jnp.asarray(perm4.T, bf16), far_leaf, far_parent,
-        equiv_points, feats, near, solution, source, counts,
+        equiv_points, near, solution, source, counts, feats,
     )
 
 

time: 97.7 us -> 82.5 us (0.84)
  Pallas kernels: 70.2 us -> 59.5 us
  local copies, waits for them, and re-layouts: 5.93 us -> 2.1 us
  waiting for transfers between devices: 6.04 us -> 3.64 us
  starting transfers between devices: 15.2 us -> 16.2 us
    pallas_call x3, Pallas kernels: 48.6 us -> 41.2 us  [the longest x1 24.8 us: shards(): call(middle_kernel, [VMEM] * 7 + [pl.BlockSpec(memory_space=pl.ANY)] * 2,...]
    pallas_call x1, Pallas kernels: 21.7 us -> 18.3 us  [shards(): call(upward_kernel, [VMEM] * 10, (shape(NX * LANES, FEATS, dtype=bf16), s...]
    ppermute x2, waiting for transfers between devices: 6.04 us -> 3.63 us  [the longest x1 3.62 us: shards(): gx_low = lax.ppermute(last, 'gx', ring('gx', 1))]
    reshape x1 -> x0, local copies, waits for them, and re-layouts: 1.4 us -> none  [shards(): counts = counts.reshape(NX * NX // 2, 2)]
    squeeze x1 -> x0, local copies, waits for them, and re-layouts: 1.02 us -> none  [shards(): gx_high = lax.ppermute(edge[0], 'gx', ring('gx', -1))]
  transfers between devices with their start and end apart: 5 -> 5, of which waited for: 2 -> 1; matrix products, arithmetic and copies ran while one was open for 3% -> 0% of each run, Pallas kernels for 34% -> 33%
where the time goes in v3:
time: 82.5 us; the launch traced here: 81.5 us
  Pallas kernels  59.5 us (72%)
  starting transfers between devices  16.2 us (20%)
  waiting for transfers between devices  3.64 us (4%)
  local copies, waits for them, and re-layouts  2.1 us (3%)
    pallas_call x1, Pallas kernels, shards(): call(middle_kernel, [VMEM] * 7 + [pl.BlockSpec(memory_space=pl.ANY)] * 2,...  24.8 us
    pallas_call x1, Pallas kernels, shards(): call(upward_kernel, [VMEM] * 10, (shape(NX * LANES, FEATS, dtype=bf16), s...  18.3 us
    pallas_call x1, Pallas kernels, shards(): call(downward_kernel, [VMEM] * 13 + [pl.BlockSpec(memory_space=pl.ANY)],...  14.5 us
    all_to_all x1, starting transfers between devices, shards(): gathered = lax.all_to_all(up, AXES, 0, 0, tiled=True)  6.76 us
    ppermute x1, starting transfers between devices, shards(): gy_high = lax.ppermute(gy_prev, 'gy', ring('gy', -1))  4.4 us
    ppermute x1, waiting for transfers between devices, shards(): gx_low = lax.ppermute(last, 'gx', ring('gx', 1))  3.62 us
    ppermute x1, starting transfers between devices, shards(): gx_high = lax.ppermute(first, 'gx', ring('gx', -1))  2.95 us
    unnamed x10, local copies, waits for them, and re-layouts  2.1 us
  transfers between devices with their start and end apart: 5, of which 1 were waited for; matrix products, arithmetic and copies ran while one was open for 0% of the time, Pallas kernels for 33%

profile of v3, /device:TPU:0, one launch (start us, length us, event | category | flops | bytes accessed | tf_op | source)
XLA Modules:
  0.0 81.5 jit_solution(9946246144151939938)
XLA Ops:
  0.0 18.3 %shard_map.181 = (bf16[16384,64]{1,0:T(8,128)(2,1)}, f32[16,8,1024]{2,1,0:T(8,128)}, f32[4,12,16,256]{3,2,1,0:T(8,128)}, f32[128,256]{1,0:T(8,128)}, f32[128,256...) custom-call(f32[3,16,16,64]{3,2,1,0:T(8,128)} %coords.1, f32[16,16,64]{2,1,0:T(8,128)} %weights.1, ...), custom_call_target="tpu_custom_call" | custom-call | tf_op jit(solution)/shard_map/pallas_call | solution.py:590
  18.4 2.1 %collective-permute-start = (f32[128,256]{1,0:T(8,128)}, f32[128,256]{1,0:T(8,128)S(1)}, u32[]{:S(2)}, u32[]{:S(2)}) collective-permute-start(f32[128,256]{1,0:T(8,128)} %get-tuple-element.19), channel_id=1, source_target_pairs={{0,1},{1,2},{2,3},{3,4},{4,5},{5,6},{6,7},{7,8},{8,9},{9,10},{10,1... | collective-permute-start | bytes 393224 | tf_op jit(solution)/shard_map/ppermute | solution.py:612
  20.4 4.4 %collective-permute-start.1 = (f32[128,256]{1,0:T(8,128)}, f32[128,256]{1,0:T(8,128)S(1)}, u32[]{:S(2)}, u32[]{:S(2)}) collective-permute-start(f32[128,256]{1,0:T(8,128)} %get-tuple-element.20), channel_id=1, source_target_pairs={{0,15},{1,0},{2,1},{3,2},{4,3},{5,4},{6,5},{7,6},{8,7},{9,8},{10,9... | collective-permute-start | bytes 393224 | tf_op jit(solution)/shard_map/ppermute | solution.py:613
  24.8 6.8 %all-to-all-start = ((f32[128,2,256]{2,1,0:T(2,128)}), f32[128,2,256]{2,1,0:T(2,128)S(1)}, u32[]{:S(2)}, u32[]{:S(2)}) async-start(f32[128,2,256]{2,1,0:T(2,128)} %get-tuple-element.17), calls=%async_computation | async-start | bytes 524288 | tf_op jit(solution)/shard_map/all_to_all | solution.py:619
  31.6 0.0 collective-permute-done.low.gy_low
  31.6 0.0 copy-start.1
  31.6 0.0 collective-permute-done.1.high.gy_high
  31.6 0.0 copy-start.2
  31.6 0.6 copy-done.1
  32.3 0.0 copy-done.2
  32.3 1.9 %shard_map.182 = (f32[168,256]{1,0:T(8,128)}, f32[168,256]{1,0:T(8,128)}) custom-call(f32[128,256]{1,0:T(8,128)} %copy-done.1, f32[128,256]{1,0:T(8,128)} %copy-done.2, f32[2,168,256]{2,1,0:T(8,128)} %get-tuple-element.21.edge), custom_call_target="tpu_custom_call" | custom-call | tf_op jit(solution)/shard_map/pallas_call | solution.py:614
  34.2 0.0 collective-permute-start.2
  34.2 3.0 %collective-permute-start.3 = (f32[168,256]{1,0:T(8,128)}, f32[168,256]{1,0:T(8,128)S(1)}, u32[]{:S(2)}, u32[]{:S(2)}) collective-permute-start(f32[168,256]{1,0:T(8,128)} %get-tuple-element.23), channel_id=1, source_target_pairs={{0,112},{16,0},{32,16},{48,32},{64,48},{80,64},{96,80},{112,96},{1... | collective-permute-start | bytes 516104 | tf_op jit(solution)/shard_map/ppermute | solution.py:618
  37.2 3.6 %collective-permute-done.2.gx_low = f32[168,256]{1,0:T(8,128)S(1)} collective-permute-done((f32[168,256]{1,0:T(8,128)}, f32[168,256]{1,0:T(8,128)S(1)}, u32[]{:S(2)}, u32[]{:S(2)}) %collective-permute-start.2) | collective-permute-done | bytes 172064 | tf_op jit(solution)/shard_map/ppermute | solution.py:617
  40.8 0.0 copy-start.3
  40.8 0.0 collective-permute-done.3.gx_high
  40.8 0.0 copy-start.4
  40.8 0.7 copy-done.3
  41.5 0.1 copy-done.4
  41.5 24.8 %shard_map.183 = (f32[2,128,128]{2,1,0:T(8,128)}, f32[512,256]{1,0:T(8,128)}, f32[128,256]{1,0:T(8,128)}) custom-call(f32[16,8,1024]{2,1,0:T(8,128)} %get-tuple-element.18.pts, f32[128,256]{1,0:T(8,128)} %copy-done.1, f32[128,256]{1,0:T(8,128)} %copy-done.2, f32[168,256]{1,0:T(8,128)} %copy-done.3, f32[168,256]{1,0:T(8,128)} %copy-done.4, ...), custom_call_target="tpu_custom_call" | custom-call | tf_op jit(solution)/shard_map/pallas_call | solution.py:620
  66.3 0.0 all-to-all-done.gathered
  66.3 0.0 copy-start
  66.3 0.7 copy-done
  67.0 14.5 %shard_map.184 = f32[16,16,64]{2,1,0:T(8,128)} custom-call(f32[128,2,256]{2,1,0:T(2,128)} %copy-done, f32[1,256,256]{2,1,0:T(8,128)} %bitcast.3, f32[2,256,256]{2,1,0:T(8,128)} %pair_down.1, f32[4,256,256]{2,1,0:T(8,128)} %down_child.1, bf16[128,128]{1,0:T(8,128)(2,1)} %constant.13.clone.perm8, bf16[32,32]{1,0:T(8,128)(2,1)} %constant.14.clone.perm4, ...), custom_call_target="tpu_custom_call" | custom-call | tf_op jit(solution)/shard_map/pallas_call | solution.py:634
Async XLA Ops:
  18.4 13.2 %collective-permute-start = (f32[128,256]{1,0:T(8,128)}, f32[128,256]{1,0:T(8,128)S(1)}, u32[]{:S(2)}, u32[]{:S(2)}) collective-permute-start(f32[128,256]{1,0:T(8,128)} %get-tuple-element.19), channel_id=1, source_target_pairs={{0,1},{1,2},{2,3},{3,4},{4,5},{5,6},{6,7},{7,8},{8,9},{9,10},{10,1... | collective-permute-start | bytes 393224 | tf_op jit(solution)/shard_map/ppermute | solution.py:612
  20.4 11.2 %collective-permute-start.1 = (f32[128,256]{1,0:T(8,128)}, f32[128,256]{1,0:T(8,128)S(1)}, u32[]{:S(2)}, u32[]{:S(2)}) collective-permute-start(f32[128,256]{1,0:T(8,128)} %get-tuple-element.20), channel_id=1, source_target_pairs={{0,15},{1,0},{2,1},{3,2},{4,3},{5,4},{6,5},{7,6},{8,7},{9,8},{10,9... | collective-permute-start | bytes 393224 | tf_op jit(solution)/shard_map/ppermute | solution.py:613
  24.8 41.5 %all-to-all-start = ((f32[128,2,256]{2,1,0:T(2,128)}), f32[128,2,256]{2,1,0:T(2,128)S(1)}, u32[]{:S(2)}, u32[]{:S(2)}) async-start(f32[128,2,256]{2,1,0:T(2,128)} %get-tuple-element.17), calls=%async_computation | async-start | bytes 524288 | tf_op jit(solution)/shard_map/all_to_all | solution.py:619
  31.6 0.7 copy-start.1
  31.6 0.7 copy-start.2
  34.2 6.6 %collective-permute-start.2 = (f32[168,256]{1,0:T(8,128)}, f32[168,256]{1,0:T(8,128)S(1)}, u32[]{:S(2)}, u32[]{:S(2)}) collective-permute-start(f32[168,256]{1,0:T(8,128)} %get-tuple-element.22), channel_id=1, source_target_pairs={{0,16},{16,32},{32,48},{48,64},{64,80},{80,96},{96,112},{112,0},{1... | collective-permute-start | bytes 516104 | tf_op jit(solution)/shard_map/ppermute | solution.py:617
  34.2 6.6 %collective-permute-start.3 = (f32[168,256]{1,0:T(8,128)}, f32[168,256]{1,0:T(8,128)S(1)}, u32[]{:S(2)}, u32[]{:S(2)}) collective-permute-start(f32[168,256]{1,0:T(8,128)} %get-tuple-element.23), channel_id=1, source_target_pairs={{0,112},{16,0},{32,16},{48,32},{64,48},{80,64},{96,80},{112,96},{1... | collective-permute-start | bytes 516104 | tf_op jit(solution)/shard_map/ppermute | solution.py:618
  40.8 0.7 copy-start.3
  40.8 0.7 copy-start.4
  66.3 0.7 copy-start

commit v4 on v3

--- a/solution.py
+++ b/solution.py
@@ -60,30 +60,15 @@
 
 def col_feats(block, role_scale=1.0):
     row, moved, norm = centred(block)
-    packed = jnp.where(row < 3, moved, jnp.where(row == 6, norm, 0.0))
+    packed = jnp.where(row < 3, moved * -2.0, jnp.where(row == 6, norm, 0.0))
     hi, mid, lo = split3(packed)
-    one = jnp.where(row == 5, 1.0, 0.0)
-    def part(value, marks, keep_norm):
-        out = jnp.where(row < 3, value * -2.0, 0.0)
-        if keep_norm:
-            out = jnp.where(row == 6, value, out)
-        return out + one if marks else out
-    ones = jnp.where(row < 7, 1.0, 0.0)
+    main = hi + jnp.where(row == 5, 1.0, 0.0)
+    ones = jnp.where(row < 7, role_scale, 0.0)
     role = jnp.concatenate(
         [hi[0:1], mid[0:1], lo[0:1], hi[1:2], mid[1:2], lo[1:2], hi[7:8], hi[7:8]], axis=0
     )
     return jnp.concatenate(
-        [
-            part(hi, True, True),
-            part(mid, False, True),
-            part(lo, False, True),
-            part(hi, True, False),
-            part(mid, False, False),
-            part(hi, True, False),
-            ones * role_scale,
-            role * role_scale,
-        ],
-        axis=0,
+        [main, mid, lo, main, mid, main, ones, role * role_scale], axis=0
     ).astype(bf16)
 
 
@@ -189,7 +174,7 @@
     own_half = lax.rem(lax.div(row8, 2), 2) == lax.div(lane8, 64)
 
     def prepare(i, carry):
-        for a in (2 * i, 2 * i + 1):
+        for a in (4 * i, 4 * i + 1, 4 * i + 2, 4 * i + 3):
             weight = jnp.where(live_pairs(counts, a), pairs(weights, a), 0.0)
             parts = [pairs(coords, c, a) for c in range(3)]
             parts += [weight, weight * pairs(solution, a)]
@@ -208,7 +193,7 @@
                 densities[pl.ds(at, 8), 128:256] = jnp.where(row8 < 4, high, 0.0)
         return carry
 
-    lax.fori_loop(0, NX // 2, prepare, 0)
+    lax.fori_loop(0, NX // 4, prepare, 0)
     keep = pltpu.make_async_copy(kept, feats, kept_sem)
     keep.start()
 
@@ -232,16 +217,17 @@
     for m in range(4):
         distances(0, m, u0)
 
-    def step(a, carry):
-        for m in range(4):
-            finish(a, m, u0)
-            distances(a, m + 4, u1)
-        for m in range(4, 8):
-            finish(a, m, u1)
-            distances(jnp.minimum(a + 1, NX - 1), m - 4, u0)
+    def step(i, carry):
+        for a in (2 * i, 2 * i + 1):
+            for m in range(4):
+                distances(a, m + 4, u1)
+                finish(a, m, u0)
+            for m in range(4, 8):
+                distances(jnp.minimum(a + 1, NX - 1), m - 4, u0)
+                finish(a, m, u1)
         return carry
 
-    lax.fori_loop(0, NX, step, 0)
+    lax.fori_loop(0, NX // 2, step, 0)
     leaf = dot3(pot[...], hi[0], lo[0])
     parent = permute(perm8[...], gather4(leaf, hi, lo, 1))
     leaf_r = leaf.astype(bf16).astype(f32)
@@ -315,8 +301,8 @@
 def role_tiles():
     def column(sx, sy):
         return [-10.0 * sx] * 3 + [-10.0 * sy] * 3 + [float(sx * sx + sy * sy), 0.0] + [
-            float(sx)
-        ] * 3 + [float(sy)] * 3 + [0.0, 0.0]
+            -0.5 * sx
+        ] * 3 + [-0.5 * sy] * 3 + [0.0, 0.0]
     pairs = [((t, -1), (t, 0)) for t in (-1, 0, 1)] + [((-1, 1), (0, 1)), ((1, 1), (1, 1))]
     out = np.zeros((5, 16, 128), np.float32)
     for n, (left, right) in enumerate(pairs):
@@ -340,7 +326,7 @@
 def middle_kernel(
     pts, gy_low, gy_high, gx_low, gx_high, boxes, roles, feats_hbm, transfer_hbm,
     near, leaf_out, parent_out,
-    feats, feats_sem, transfer, arrived, dens0, dens1, cols0, cols1, u0, u1, extended, windows,
+    feats, feats_sem, transfer, arrived, dens0, dens1, cols0, cols1, u0, u1, v0, v1, extended, windows,
 ):
     load = pltpu.make_async_copy(feats_hbm, feats, feats_sem)
     load.start()
@@ -373,26 +359,35 @@
 
     lax.fori_loop(0, NX + 2, prepare, 0)
 
-    def distances(a, half, u, mms=range(4)):
+    spare = jnp.zeros((FEATS, 128), bf16)
+
+    def distances(a, half, u, u_last, mms=range(4)):
         for mm in mms:
             base = half * 512 + mm * 128
             here, after = slice(base, base + 128), slice(base + 128, base + 256)
+            both = []
             for odd in range(2):
                 own, other = ((cols0, cols1), (cols1, cols0))[odd]
                 far = here if odd == 0 else after
                 blocks = [own[a + t, :, here] for t in range(3)]
                 blocks.append(jnp.where(first_cols, own[a, :, after], other[a + 1, :, far]))
-                blocks.append(own[a + 2, :, after])
                 blocks = [
                     jnp.concatenate([x[:48], x[48:] * roles[n]], axis=0)
                     for n, x in enumerate(blocks)
                 ]
                 start = pl.multiple_of(a * LANES + base + 64 * odd, 64)
                 rows = feats[pl.ds(start, 64), :]
+                both.append(rows)
                 at = 64 * (2 * mm + odd)
                 u[at : at + 64, :] = dot(rows, jnp.concatenate(blocks, axis=1))
-
-    def finish(a, half, u, mms=range(4)):
+            last = cols0[a + 2, :, after]
+            last = jnp.concatenate([last[:48], last[48:] * roles[4]], axis=0)
+            split = jnp.concatenate(
+                [jnp.where(first_cols, last, spare), jnp.where(first_cols, spare, last)], axis=0
+            )
+            u_last[64 * mm : 64 * mm + 64, :] = dot(jnp.concatenate(both, axis=1), split)
+
+    def finish(a, half, u, u_last, mms=range(4)):
         for mm in mms:
             base = half * 512 + mm * 128
             here, after = slice(base, base + 128), slice(base + 128, base + 256)
@@ -402,37 +397,48 @@
                 far = here if odd == 0 else after
                 accs = [None, None]
                 at = 64 * (2 * mm + odd)
-                for n in range(5):
+                for n in range(4):
                     k = power(u[at : at + 64, 128 * n : 128 * n + 128])
                     for c in range(2):
                         r = slice(3 + c, 4 + c)
                         if n < 3:
                             dens = d_own[a + n, r, here]
-                        elif n == 3:
+                        else:
                             dens = jnp.where(first, d_own[a, r, after], d_other[a + 1, r, far])
-                        else:
-                            dens = jnp.where(first, d_own[a + 2, r, after], 0.0)
                         term = k * dens
                         accs[c] = term if n == 0 else accs[c] + term
                 sums.append(accs)
-            both = [jnp.concatenate([sums[0][c], sums[1][c]], axis=0) for c in range(2)]
+            k = power(u_last[64 * mm : 64 * mm + 64, :])
+            both = []
+            for c in range(2):
+                term = k * dens0[a + 2, 3 + c : 4 + c, after]
+                both.append(
+                    jnp.concatenate(
+                        [
+                            sums[0][c] + jnp.where(first, term, 0.0),
+                            sums[1][c] + jnp.where(first, 0.0, term),
+                        ],
+                        axis=0,
+                    )
+                )
             total = sum_lanes(*both)
             for c in range(2):
                 near[c, pl.ds(a * 8 + half * 4 + mm, 1), :] = total[c : c + 1]
 
     load.wait()
-    distances(0, 0, u0)
-
-    def step(a, carry):
-        for mm in range(4):
-            finish(a, 0, u0, (mm,))
-            distances(a, 1, u1, (mm,))
-        for mm in range(4):
-            finish(a, 1, u1, (mm,))
-            distances(jnp.minimum(a + 1, NX - 1), 0, u0, (mm,))
+    distances(0, 0, u0, v0)
+
+    def step(i, carry):
+        for a in (2 * i, 2 * i + 1):
+            for mm in range(4):
+                finish(a, 0, u0, v0, (mm,))
+                distances(a, 1, u1, v1, (mm,))
+            for mm in range(4):
+                finish(a, 1, u1, v1, (mm,))
+                distances(jnp.minimum(a + 1, NX - 1), 0, u0, v0, (mm,))
         return carry
 
-    lax.fori_loop(0, NX, step, 0)
+    lax.fori_loop(0, NX // 2, step, 0)
 
     blank = jnp.zeros((8, 256), f32)
     for p in range(4):
@@ -542,16 +548,17 @@
     for m in range(4):
         distances(0, m, u0)
 
-    def step(a, carry):
-        for m in range(4):
-            finish(a, m, u0)
-            distances(a, m + 4, u1)
-        for m in range(4, 8):
-            finish(a, m, u1)
-            distances(jnp.minimum(a + 1, NX - 1), m - 4, u0)
+    def step(i, carry):
+        for a in (2 * i, 2 * i + 1):
+            for m in range(4):
+                distances(a, m + 4, u1)
+                finish(a, m, u0)
+            for m in range(4, 8):
+                distances(jnp.minimum(a + 1, NX - 1), m - 4, u0)
+                finish(a, m, u1)
         return carry
 
-    lax.fori_loop(0, NX, step, 0)
+    lax.fori_loop(0, NX // 2, step, 0)
     for a in range(NX):
         rows = slice(8 * a, 8 * a + 8)
         total = [pot[c, rows, :] + near[c, rows, :] for c in range(2)]
@@ -625,7 +632,8 @@
         + [pltpu.VMEM((40, 256, 256), bf16), pltpu.SemaphoreType.DMA]
         + [pltpu.VMEM((NX + 2, 8, PADDED), f32)] * 2
         + [pltpu.VMEM((NX + 2, FEATS, PADDED), bf16)] * 2
-        + [pltpu.VMEM((512, 640), f32)] * 2
+        + [pltpu.VMEM((512, 512), f32)] * 2
+        + [pltpu.VMEM((256, 128), f32)] * 2
         + [pltpu.VMEM((4, 16, 32, 256), f32), pltpu.VMEM((4, 3, 16, 16, 256), bf16)],
     )(
         pts, gy_low, gy_high, gx_low, gx_high, boxes, jnp.asarray(role_tiles(), bf16), feats,

time: 82.5 us -> 76.3 us (0.925)
  Pallas kernels: 59.5 us -> 53.4 us
    pallas_call x1, Pallas kernels: 18.3 us -> 15.3 us  [shards(): call(upward_kernel, [VMEM] * 10, (shape(NX * LANES, FEATS, dtype=bf16), s...]
    pallas_call x1, Pallas kernels: 24.8 us -> 23.2 us  [shards(): call(middle_kernel, [VMEM] * 7 + [pl.BlockSpec(memory_space=pl.ANY)] * 2,...]
    pallas_call x1, Pallas kernels: 14.5 us -> 13 us  [shards(): call(downward_kernel, [VMEM] * 13 + [pl.BlockSpec(memory_space=pl.ANY)],...]
where the time goes in v4:
time: 76.3 us; the launch traced here: 75.4 us
  Pallas kernels  53.4 us (70%)
  starting transfers between devices  16.2 us (21%)
  waiting for transfers between devices  3.64 us (5%)
  local copies, waits for them, and re-layouts  2.1 us (3%)
    pallas_call x1, Pallas kernels, shards(): call(middle_kernel, [VMEM] * 7 + [pl.BlockSpec(memory_space=pl.ANY)] * 2,...  23.2 us
    pallas_call x1, Pallas kernels, shards(): call(upward_kernel, [VMEM] * 10, (shape(NX * LANES, FEATS, dtype=bf16), s...  15.3 us
    pallas_call x1, Pallas kernels, shards(): call(downward_kernel, [VMEM] * 13 + [pl.BlockSpec(memory_space=pl.ANY)],...  13 us
    all_to_all x1, starting transfers between devices, shards(): gathered = lax.all_to_all(up, AXES, 0, 0, tiled=True)  6.78 us
    ppermute x1, starting transfers between devices, shards(): gy_high = lax.ppermute(gy_prev, 'gy', ring('gy', -1))  4.39 us
    ppermute x1, waiting for transfers between devices, shards(): gx_low = lax.ppermute(last, 'gx', ring('gx', 1))  3.62 us
    ppermute x1, starting transfers between devices, shards(): gx_high = lax.ppermute(first, 'gx', ring('gx', -1))  2.95 us
    unnamed x10, local copies, waits for them, and re-layouts  2.1 us
  transfers between devices with their start and end apart: 5, of which 1 were waited for; matrix products, arithmetic and copies ran while one was open for 0% of the time, Pallas kernels for 33%

profile of v4, /device:TPU:0, one launch (start us, length us, event | category | flops | bytes accessed | tf_op | source)
XLA Modules:
  0.0 75.4 jit_solution(4828118416614709610)
XLA Ops:
  0.0 15.3 %shard_map.181 = (bf16[16384,64]{1,0:T(8,128)(2,1)}, f32[16,8,1024]{2,1,0:T(8,128)}, f32[4,12,16,256]{3,2,1,0:T(8,128)}, f32[128,256]{1,0:T(8,128)}, f32[128,256...) custom-call(f32[3,16,16,64]{3,2,1,0:T(8,128)} %coords.1, f32[16,16,64]{2,1,0:T(8,128)} %weights.1, ...), custom_call_target="tpu_custom_call" | custom-call | tf_op jit(solution)/shard_map/pallas_call | solution.py:597
  15.3 2.1 %collective-permute-start = (f32[128,256]{1,0:T(8,128)}, f32[128,256]{1,0:T(8,128)S(1)}, u32[]{:S(2)}, u32[]{:S(2)}) collective-permute-start(f32[128,256]{1,0:T(8,128)} %get-tuple-element.19), channel_id=1, source_target_pairs={{0,1},{1,2},{2,3},{3,4},{4,5},{5,6},{6,7},{7,8},{8,9},{9,10},{10,1... | collective-permute-start | bytes 393224 | tf_op jit(solution)/shard_map/ppermute | solution.py:619
  17.4 4.4 %collective-permute-start.1 = (f32[128,256]{1,0:T(8,128)}, f32[128,256]{1,0:T(8,128)S(1)}, u32[]{:S(2)}, u32[]{:S(2)}) collective-permute-start(f32[128,256]{1,0:T(8,128)} %get-tuple-element.20), channel_id=1, source_target_pairs={{0,15},{1,0},{2,1},{3,2},{4,3},{5,4},{6,5},{7,6},{8,7},{9,8},{10,9... | collective-permute-start | bytes 393224 | tf_op jit(solution)/shard_map/ppermute | solution.py:620
  21.8 6.8 %all-to-all-start = ((f32[128,2,256]{2,1,0:T(2,128)}), f32[128,2,256]{2,1,0:T(2,128)S(1)}, u32[]{:S(2)}, u32[]{:S(2)}) async-start(f32[128,2,256]{2,1,0:T(2,128)} %get-tuple-element.17), calls=%async_computation | async-start | bytes 524288 | tf_op jit(solution)/shard_map/all_to_all | solution.py:626
  28.6 0.0 collective-permute-done.low.gy_low
  28.6 0.0 copy-start.1
  28.6 0.0 collective-permute-done.1.high.gy_high
  28.6 0.0 copy-start.2
  28.6 0.6 copy-done.1
  29.2 0.0 copy-done.2
  29.3 1.9 %shard_map.182 = (f32[168,256]{1,0:T(8,128)}, f32[168,256]{1,0:T(8,128)}) custom-call(f32[128,256]{1,0:T(8,128)} %copy-done.1, f32[128,256]{1,0:T(8,128)} %copy-done.2, f32[2,168,256]{2,1,0:T(8,128)} %get-tuple-element.21.edge), custom_call_target="tpu_custom_call" | custom-call | tf_op jit(solution)/shard_map/pallas_call | solution.py:621
  31.2 0.0 collective-permute-start.2
  31.2 3.0 %collective-permute-start.3 = (f32[168,256]{1,0:T(8,128)}, f32[168,256]{1,0:T(8,128)S(1)}, u32[]{:S(2)}, u32[]{:S(2)}) collective-permute-start(f32[168,256]{1,0:T(8,128)} %get-tuple-element.23), channel_id=1, source_target_pairs={{0,112},{16,0},{32,16},{48,32},{64,48},{80,64},{96,80},{112,96},{1... | collective-permute-start | bytes 516104 | tf_op jit(solution)/shard_map/ppermute | solution.py:625
  34.1 3.6 %collective-permute-done.2.gx_low = f32[168,256]{1,0:T(8,128)S(1)} collective-permute-done((f32[168,256]{1,0:T(8,128)}, f32[168,256]{1,0:T(8,128)S(1)}, u32[]{:S(2)}, u32[]{:S(2)}) %collective-permute-start.2) | collective-permute-done | bytes 172064 | tf_op jit(solution)/shard_map/ppermute | solution.py:624
  37.8 0.0 copy-start.3
  37.8 0.0 collective-permute-done.3.gx_high
  37.8 0.0 copy-start.4
  37.8 0.7 copy-done.3
  38.5 0.1 copy-done.4
  38.5 23.2 %shard_map.183 = (f32[2,128,128]{2,1,0:T(8,128)}, f32[512,256]{1,0:T(8,128)}, f32[128,256]{1,0:T(8,128)}) custom-call(f32[16,8,1024]{2,1,0:T(8,128)} %get-tuple-element.18.pts, f32[128,256]{1,0:T(8,128)} %copy-done.1, f32[128,256]{1,0:T(8,128)} %copy-done.2, f32[168,256]{1,0:T(8,128)} %copy-done.3, f32[168,256]{1,0:T(8,128)} %copy-done.4, ...), custom_call_target="tpu_custom_call" | custom-call | tf_op jit(solution)/shard_map/pallas_call | solution.py:627
  61.7 0.0 all-to-all-done.gathered
  61.7 0.0 copy-start
  61.7 0.7 copy-done
  62.4 13.0 %shard_map.184 = f32[16,16,64]{2,1,0:T(8,128)} custom-call(f32[128,2,256]{2,1,0:T(2,128)} %copy-done, f32[1,256,256]{2,1,0:T(8,128)} %bitcast.3, f32[2,256,256]{2,1,0:T(8,128)} %pair_down.1, f32[4,256,256]{2,1,0:T(8,128)} %down_child.1, bf16[128,128]{1,0:T(8,128)(2,1)} %constant.13.clone.perm8, bf16[32,32]{1,0:T(8,128)(2,1)} %constant.14.clone.perm4, ...), custom_call_target="tpu_custom_call" | custom-call | tf_op jit(solution)/shard_map/pallas_call | solution.py:642
Async XLA Ops:
  15.3 13.3 %collective-permute-start = (f32[128,256]{1,0:T(8,128)}, f32[128,256]{1,0:T(8,128)S(1)}, u32[]{:S(2)}, u32[]{:S(2)}) collective-permute-start(f32[128,256]{1,0:T(8,128)} %get-tuple-element.19), channel_id=1, source_target_pairs={{0,1},{1,2},{2,3},{3,4},{4,5},{5,6},{6,7},{7,8},{8,9},{9,10},{10,1... | collective-permute-start | bytes 393224 | tf_op jit(solution)/shard_map/ppermute | solution.py:619
  17.4 11.2 %collective-permute-start.1 = (f32[128,256]{1,0:T(8,128)}, f32[128,256]{1,0:T(8,128)S(1)}, u32[]{:S(2)}, u32[]{:S(2)}) collective-permute-start(f32[128,256]{1,0:T(8,128)} %get-tuple-element.20), channel_id=1, source_target_pairs={{0,15},{1,0},{2,1},{3,2},{4,3},{5,4},{6,5},{7,6},{8,7},{9,8},{10,9... | collective-permute-start | bytes 393224 | tf_op jit(solution)/shard_map/ppermute | solution.py:620
  21.8 39.9 %all-to-all-start = ((f32[128,2,256]{2,1,0:T(2,128)}), f32[128,2,256]{2,1,0:T(2,128)S(1)}, u32[]{:S(2)}, u32[]{:S(2)}) async-start(f32[128,2,256]{2,1,0:T(2,128)} %get-tuple-element.17), calls=%async_computation | async-start | bytes 524288 | tf_op jit(solution)/shard_map/all_to_all | solution.py:626
  28.6 0.7 copy-start.1
  28.6 0.7 copy-start.2
  31.2 6.6 %collective-permute-start.2 = (f32[168,256]{1,0:T(8,128)}, f32[168,256]{1,0:T(8,128)S(1)}, u32[]{:S(2)}, u32[]{:S(2)}) collective-permute-start(f32[168,256]{1,0:T(8,128)} %get-tuple-element.22), channel_id=1, source_target_pairs={{0,16},{16,32},{32,48},{48,64},{64,80},{80,96},{96,112},{112,0},{1... | collective-permute-start | bytes 516104 | tf_op jit(solution)/shard_map/ppermute | solution.py:624
  31.2 6.6 %collective-permute-start.3 = (f32[168,256]{1,0:T(8,128)}, f32[168,256]{1,0:T(8,128)S(1)}, u32[]{:S(2)}, u32[]{:S(2)}) collective-permute-start(f32[168,256]{1,0:T(8,128)} %get-tuple-element.23), channel_id=1, source_target_pairs={{0,112},{16,0},{32,16},{48,32},{64,48},{80,64},{96,80},{112,96},{1... | collective-permute-start | bytes 516104 | tf_op jit(solution)/shard_map/ppermute | solution.py:625
  37.8 0.7 copy-start.3
  37.8 0.7 copy-start.4
  61.7 0.7 copy-start

commit v5 on v4

--- a/solution.py
+++ b/solution.py
@@ -323,19 +323,14 @@
     return total
 
 
-def middle_kernel(
-    pts, gy_low, gy_high, gx_low, gx_high, boxes, roles, feats_hbm, transfer_hbm,
-    near, leaf_out, parent_out,
-    feats, feats_sem, transfer, arrived, dens0, dens1, cols0, cols1, u0, u1, v0, v1, extended, windows,
+def near_strips(
+    strips, pts, gy_low, gy_high, gx_low, gx_high, roles, near, feats, dens0, dens1,
+    cols0, cols1,
 ):
-    load = pltpu.make_async_copy(feats_hbm, feats, feats_sem)
-    load.start()
-    fetch = pltpu.make_async_copy(transfer_hbm, transfer, arrived)
-    fetch.start()
     first = lax.broadcasted_iota(jnp.int32, (1, 128), 1) < 64
     first_cols = lax.broadcasted_iota(jnp.int32, (FEATS, 128), 1) < 64
 
-    for t in range(NX + 2):
+    for t in strips:
         if t in (0, NX + 1):
             ref = gx_low if t == 0 else gx_high
             own = jnp.concatenate([ref[128 + 8 * k : 136 + 8 * k, :] for k in range(4)], axis=1)
@@ -352,12 +347,15 @@
         dens1[t, :, LANES : LANES + 64] = high
         dens1[t, :, LANES + 64 :] = jnp.zeros((8, 64), f32)
 
-    def prepare(t, carry):
+    def prepare(i, carry):
+        t = strips[0] + i
+        if len(strips) < NX:
+            t = jnp.where(i < 3, i, i + NX - 4)
         cols0[t] = col_feats(dens0[t])
         cols1[t] = col_feats(dens1[t])
         return carry
 
-    lax.fori_loop(0, NX + 2, prepare, 0)
+    lax.fori_loop(0, len(strips), prepare, 0)
 
     spare = jnp.zeros((FEATS, 128), bf16)
 
@@ -395,19 +393,21 @@
             for odd in range(2):
                 d_own, d_other = ((dens0, dens1), (dens1, dens0))[odd]
                 far = here if odd == 0 else after
-                accs = [None, None]
-                at = 64 * (2 * mm + odd)
-                for n in range(4):
-                    k = power(u[at : at + 64, 128 * n : 128 * n + 128])
+                dens = []
+                for c in range(2):
+                    r = slice(3 + c, 4 + c)
+                    dens.append([d_own[a + n, r, here] for n in range(3)])
+                    dens[c].append(jnp.where(first, d_own[a, r, after], d_other[a + 1, r, far]))
+                parts = [[], []]
+                for chunk in range(4):
+                    at = 64 * (2 * mm + odd) + 16 * chunk
+                    k = [power(u[at : at + 16, 128 * n : 128 * n + 128]) for n in range(4)]
                     for c in range(2):
-                        r = slice(3 + c, 4 + c)
-                        if n < 3:
-                            dens = d_own[a + n, r, here]
-                        else:
-                            dens = jnp.where(first, d_own[a, r, after], d_other[a + 1, r, far])
-                        term = k * dens
-                        accs[c] = term if n == 0 else accs[c] + term
-                sums.append(accs)
+                        parts[c].append(
+                            (k[0] * dens[c][0] + k[1] * dens[c][1])
+                            + (k[2] * dens[c][2] + k[3] * dens[c][3])
+                        )
+                sums.append([jnp.concatenate(p, axis=0) for p in parts])
             k = power(u_last[64 * mm : 64 * mm + 64, :])
             both = []
             for c in range(2):
@@ -425,20 +425,70 @@
             for c in range(2):
                 near[c, pl.ds(a * 8 + half * 4 + mm, 1), :] = total[c : c + 1]
 
+    return distances, finish
+
+
+def inner_kernel(
+    pts, gy_low, gy_high, roles, feats_hbm, near,
+    feats, feats_sem, dens0, dens1, cols0, cols1, u0, u1, v0, v1,
+):
+    load = pltpu.make_async_copy(feats_hbm, feats, feats_sem)
+    load.start()
+    distances, finish = near_strips(
+        range(1, NX + 1), pts, gy_low, gy_high, None, None, roles, near, feats, dens0, dens1,
+        cols0, cols1,
+    )
     load.wait()
-    distances(0, 0, u0, v0)
+    distances(jnp.int32(1), 0, u0, v0)
 
     def step(i, carry):
-        for a in (2 * i, 2 * i + 1):
+        for a in (2 * i + 1, 2 * i + 2):
             for mm in range(4):
                 finish(a, 0, u0, v0, (mm,))
                 distances(a, 1, u1, v1, (mm,))
             for mm in range(4):
                 finish(a, 1, u1, v1, (mm,))
-                distances(jnp.minimum(a + 1, NX - 1), 0, u0, v0, (mm,))
+                distances(jnp.minimum(a + 1, NX - 2), 0, u0, v0, (mm,))
         return carry
 
-    lax.fori_loop(0, NX // 2, step, 0)
+    lax.fori_loop(0, NX // 2 - 1, step, 0)
+
+
+def middle_kernel(
+    pts, gy_low, gy_high, gx_low, gx_high, boxes, roles, feats_hbm, transfer_hbm,
+    near, leaf_out, parent_out,
+    feats, feats_sem, transfer, arrived, dens0, dens1, cols0, cols1, u0, u1, v0, v1,
+    extended, windows,
+):
+    loads = [
+        pltpu.make_async_copy(
+            feats_hbm.at[pl.ds(a * LANES, LANES)], feats.at[pl.ds(a * LANES, LANES)],
+            feats_sem.at[n],
+        )
+        for n, a in enumerate((0, NX - 1))
+    ]
+    for load in loads:
+        load.start()
+    fetch = pltpu.make_async_copy(transfer_hbm, transfer, arrived)
+    fetch.start()
+    distances, finish = near_strips(
+        (0, 1, 2, NX - 1, NX, NX + 1), pts, gy_low, gy_high, gx_low, gx_high, roles, near,
+        feats, dens0, dens1, cols0, cols1,
+    )
+    for load in loads:
+        load.wait()
+    low_strip, high_strip = jnp.int32(0), jnp.int32(NX - 1)
+    distances(low_strip, 0, u0, v0)
+    for mm in range(4):
+        finish(low_strip, 0, u0, v0, (mm,))
+        distances(low_strip, 1, u1, v1, (mm,))
+    for mm in range(4):
+        finish(low_strip, 1, u1, v1, (mm,))
+        distances(high_strip, 0, u0, v0, (mm,))
+    for mm in range(4):
+        finish(high_strip, 0, u0, v0, (mm,))
+        distances(high_strip, 1, u1, v1, (mm,))
+    finish(high_strip, 1, u1, v1)
 
     blank = jnp.zeros((8, 256), f32)
     for p in range(4):
@@ -497,7 +547,7 @@
 
 def downward_kernel(
     gathered, lattice, pair_down, down_child, perm8, perm4, far_leaf, far_parent,
-    equiv_pts, near, solution, source, counts, feats_hbm, out,
+    equiv_pts, inner, near, solution, source, counts, feats_hbm, out,
     local, pot, u0, u1, hi, lo, feats, feats_sem,
 ):
     load = pltpu.make_async_copy(feats_hbm, feats, feats_sem)
@@ -561,7 +611,8 @@
     lax.fori_loop(0, NX // 2, step, 0)
     for a in range(NX):
         rows = slice(8 * a, 8 * a + 8)
-        total = [pot[c, rows, :] + near[c, rows, :] for c in range(2)]
+        close = near if a in (0, NX - 1) else inner
+        total = [pot[c, rows, :] + close[c, rows, :] for c in range(2)]
         value = pairs(source, a) - scale_frac * (pairs(solution, a) * total[0] - total[1])
         value = jnp.where(live_pairs(counts, a), value, 0.0)
         out[a, pl.ds(0, NX // 2, stride=2), :] = value[:, :64]
@@ -573,7 +624,7 @@
     return [(i, (i + step) % count) for i in range(count)]
 
 
-def call(kernel, in_specs, out_shape, scratch, out_specs=None):
+def call(kernel, in_specs, out_shape, scratch, out_specs=None, cost=None):
     return pl.pallas_call(
         kernel,
         out_shape=out_shape,
@@ -581,6 +632,7 @@
         out_specs=out_specs or jax.tree.map(lambda _: VMEM, out_shape),
         scratch_shapes=scratch,
         compiler_params=PARAMS,
+        cost_estimate=cost,
     )
 
 
@@ -624,24 +676,36 @@
     gx_low = lax.ppermute(last, "gx", ring("gx", 1))
     gx_high = lax.ppermute(first, "gx", ring("gx", -1))
     gathered = lax.all_to_all(up, AXES, 0, 0, tiled=True)
+    roles = jnp.asarray(role_tiles(), bf16)
+    near_scratch = (
+        [pltpu.VMEM((NX + 2, 8, PADDED), f32)] * 2
+        + [pltpu.VMEM((NX + 2, FEATS, PADDED), bf16)] * 2
+        + [pltpu.VMEM((512, 512), f32)] * 2
+        + [pltpu.VMEM((256, 128), f32)] * 2
+    )
+    gy_low_in, gy_high_in, _ = lax.optimization_barrier((gy_low, gy_high, first))
+    inner = call(
+        inner_kernel,
+        [VMEM] * 4 + [pl.BlockSpec(memory_space=pl.ANY)],
+        shape(2, 128, 128),
+        [pltpu.VMEM((NX * LANES, FEATS), bf16), pltpu.SemaphoreType.DMA] + near_scratch,
+        cost=pl.CostEstimate(flops=4 * 10**10, bytes_accessed=10**7, transcendentals=2 * 10**7),
+    )(pts, gy_low_in, gy_high_in, roles, feats)
     near, far_leaf, far_parent = call(
         middle_kernel,
         [VMEM] * 7 + [pl.BlockSpec(memory_space=pl.ANY)] * 2,
         (shape(2, 128, 128), shape(512, 256), shape(128, 256)),
-        [pltpu.VMEM((NX * LANES, FEATS), bf16), pltpu.SemaphoreType.DMA]
+        [pltpu.VMEM((NX * LANES, FEATS), bf16), pltpu.SemaphoreType.DMA((2,))]
         + [pltpu.VMEM((40, 256, 256), bf16), pltpu.SemaphoreType.DMA]
-        + [pltpu.VMEM((NX + 2, 8, PADDED), f32)] * 2
-        + [pltpu.VMEM((NX + 2, FEATS, PADDED), bf16)] * 2
-        + [pltpu.VMEM((512, 512), f32)] * 2
-        + [pltpu.VMEM((256, 128), f32)] * 2
+        + near_scratch
         + [pltpu.VMEM((4, 16, 32, 256), f32), pltpu.VMEM((4, 3, 16, 16, 256), bf16)],
     )(
-        pts, gy_low, gy_high, gx_low, gx_high, boxes, jnp.asarray(role_tiles(), bf16), feats,
+        pts, gy_low, gy_high, gx_low, gx_high, boxes, roles, feats,
         far_transfer,
     )
     return call(
         downward_kernel,
-        [VMEM] * 13 + [pl.BlockSpec(memory_space=pl.ANY)],
+        [VMEM] * 14 + [pl.BlockSpec(memory_space=pl.ANY)],
         shape(NX, NX, 64),
         [pltpu.VMEM((512, 256), f32), pltpu.VMEM((2, 128, 128), f32)]
         + [pltpu.VMEM((512, 256), f32)] * 2
@@ -650,7 +714,7 @@
     )(
         gathered, lattice_map[None], pair_down, down_children,
         jnp.asarray(perm8.T, bf16), jnp.asarray(perm4.T, bf16), far_leaf, far_parent,
-        equiv_points, near, solution, source, counts, feats,
+        equiv_points, inner, near, solution, source, counts, feats,
     )
 
 

time: 76.3 us -> 74.5 us (0.976)
  waiting for transfers between devices: 3.64 us -> 0.01 us
  Pallas kernels: 53.4 us -> 56.2 us
  starting transfers between devices: 16.2 us -> 15.2 us
    pallas_call x1 -> x2, Pallas kernels: 13 us -> 30.3 us  [the longest x1 17.2 us: shards(): call(inner_kernel, [VMEM] * 4 + [pl.BlockSpec(memory_space=pl.ANY)], shap...]
    pallas_call x1, Pallas kernels: 23.2 us -> 8.65 us  [shards(): call(middle_kernel, [VMEM] * 7 + [pl.BlockSpec(memory_space=pl.ANY)] * 2,...]
    ppermute x1, waiting for transfers between devices: 3.62 us -> 0.01 us  [shards(): gx_low = lax.ppermute(last, 'gx', ring('gx', 1))]
    ppermute x1, starting transfers between devices: 2.95 us -> 1.8 us  [shards(): gx_high = lax.ppermute(first, 'gx', ring('gx', -1))]
  transfers between devices with their start and end apart: 5 -> 5, of which waited for: 1 -> 0; matrix products, arithmetic and copies ran while one was open for 0% -> 0% of each run, Pallas kernels for 33% -> 38%
where the time goes in v5:
time: 74.5 us; the launch traced here: 73.8 us
  Pallas kernels  56.2 us (75%)
  starting transfers between devices  15.2 us (20%)
  local copies, waits for them, and re-layouts  2.07 us (3%)
    pallas_call x1, Pallas kernels, shards(): call(inner_kernel, [VMEM] * 4 + [pl.BlockSpec(memory_space=pl.ANY)], shap...  17.2 us
    pallas_call x1, Pallas kernels, shards(): call(upward_kernel, [VMEM] * 10, (shape(NX * LANES, FEATS, dtype=bf16), s...  15.3 us
    pallas_call x1, Pallas kernels, shards(): call(downward_kernel, [VMEM] * 14 + [pl.BlockSpec(memory_space=pl.ANY)],...  13.1 us
    pallas_call x1, Pallas kernels, shards(): call(middle_kernel, [VMEM] * 7 + [pl.BlockSpec(memory_space=pl.ANY)] * 2,...  8.65 us
    all_to_all x1, starting transfers between devices, shards(): gathered = lax.all_to_all(up, AXES, 0, 0, tiled=True)  6.95 us
    ppermute x1, starting transfers between devices, shards(): gy_high = lax.ppermute(gy_prev, 'gy', ring('gy', -1))  4.4 us
    unnamed x10, local copies, waits for them, and re-layouts  2.07 us
    ppermute x1, starting transfers between devices, shards(): gy_low = lax.ppermute(gy_next, 'gy', ring('gy', 1))  2.07 us
  transfers between devices with their start and end apart: 5, of which 0 were waited for; matrix products, arithmetic and copies ran while one was open for 0% of the time, Pallas kernels for 38%

profile of v5, /device:TPU:0, one launch (start us, length us, event | category | flops | bytes accessed | tf_op | source)
XLA Modules:
  0.0 73.8 jit_solution(13398117866202864070)
XLA Ops:
  0.0 15.3 %shard_map.181 = (bf16[16384,64]{1,0:T(8,128)(2,1)}, f32[16,8,1024]{2,1,0:T(8,128)}, f32[4,12,16,256]{3,2,1,0:T(8,128)}, f32[128,256]{1,0:T(8,128)}, f32[128,256...) custom-call(f32[3,16,16,64]{3,2,1,0:T(8,128)} %coords.1, f32[16,16,64]{2,1,0:T(8,128)} %weights.1, ...), custom_call_target="tpu_custom_call" | custom-call | tf_op jit(solution)/shard_map/pallas_call | solution.py:649
  15.3 2.1 %collective-permute-start = (f32[128,256]{1,0:T(8,128)}, f32[128,256]{1,0:T(8,128)S(1)}, u32[]{:S(2)}, u32[]{:S(2)}) collective-permute-start(f32[128,256]{1,0:T(8,128)} %get-tuple-element.21), channel_id=1, source_target_pairs={{0,1},{1,2},{2,3},{3,4},{4,5},{5,6},{6,7},{7,8},{8,9},{9,10},{10,1... | collective-permute-start | bytes 393224 | tf_op jit(solution)/shard_map/ppermute | solution.py:671
  17.4 4.4 %collective-permute-start.1 = (f32[128,256]{1,0:T(8,128)}, f32[128,256]{1,0:T(8,128)S(1)}, u32[]{:S(2)}, u32[]{:S(2)}) collective-permute-start(f32[128,256]{1,0:T(8,128)} %get-tuple-element.22), channel_id=1, source_target_pairs={{0,15},{1,0},{2,1},{3,2},{4,3},{5,4},{6,5},{7,6},{8,7},{9,8},{10,9... | collective-permute-start | bytes 393224 | tf_op jit(solution)/shard_map/ppermute | solution.py:672
  21.8 6.9 %all-to-all-start = ((f32[128,2,256]{2,1,0:T(2,128)}), f32[128,2,256]{2,1,0:T(2,128)S(1)}, u32[]{:S(2)}, u32[]{:S(2)}) async-start(f32[128,2,256]{2,1,0:T(2,128)} %get-tuple-element.19), calls=%async_computation | async-start | bytes 524288 | tf_op jit(solution)/shard_map/all_to_all | solution.py:678
  28.8 0.0 collective-permute-done.low.gy_low
  28.8 0.0 copy-start.1
  28.8 0.0 collective-permute-done.1.high.gy_high
  28.8 0.0 copy-start.2
  28.8 0.6 copy-done.1
  29.4 0.0 copy-done.2
  29.5 1.9 %shard_map.182 = (f32[168,256]{1,0:T(8,128)}, f32[168,256]{1,0:T(8,128)}) custom-call(f32[128,256]{1,0:T(8,128)} %copy-done.1, f32[128,256]{1,0:T(8,128)} %copy-done.2, f32[2,168,256]{2,1,0:T(8,128)} %get-tuple-element.23.edge), custom_call_target="tpu_custom_call" | custom-call | tf_op jit(solution)/shard_map/pallas_call | solution.py:673
  31.4 1.8 %collective-permute-start.3 = (f32[168,256]{1,0:T(8,128)}, f32[168,256]{1,0:T(8,128)S(1)}, u32[]{:S(2)}, u32[]{:S(2)}) collective-permute-start(f32[168,256]{1,0:T(8,128)} %get-tuple-element.25), channel_id=1, source_target_pairs={{0,112},{16,0},{32,16},{48,32},{64,48},{80,64},{96,80},{112,96},{1... | collective-permute-start | bytes 516104 | tf_op jit(solution)/shard_map/ppermute | solution.py:677
  33.2 0.0 collective-permute-start.2
  33.2 17.2 %shard_map.184.inner = f32[2,128,128]{2,1,0:T(8,128)} custom-call(f32[16,8,1024]{2,1,0:T(8,128)} %get-tuple-element.20.pts, f32[128,256]{1,0:T(8,128)} %copy-done.1, f32[128,256]{1,0:T(8,128)} %copy-done.2, bf16[5,16,128]{2,1,0:T(8,128)(2,1)} %constant.12.clone.roles, bf16[16384,64]{1,0:T(8,128)(2,1)} %get-tuple-element.27.feats_hbm), custom_call_target="tpu_custom_call" | custom-call | flops 40000000000 | bytes 10000000 | tf_op jit(solution)/shard_map/pallas_call | solution.py:687
  50.5 0.0 collective-permute-done.2.gx_low
  50.5 0.0 copy-start.4
  50.5 0.0 collective-permute-done.3.gx_high
  50.5 0.0 copy-start.3
  50.5 0.6 copy-done.4
  51.1 0.1 copy-done.3
  51.2 8.6 %shard_map.183 = (f32[2,128,128]{2,1,0:T(8,128)}, f32[512,256]{1,0:T(8,128)}, f32[128,256]{1,0:T(8,128)}) custom-call(f32[16,8,1024]{2,1,0:T(8,128)} %get-tuple-element.20.pts, f32[128,256]{1,0:T(8,128)} %copy-done.1, f32[128,256]{1,0:T(8,128)} %copy-done.2, f32[168,256]{1,0:T(8,128)} %copy-done.4, f32[168,256]{1,0:T(8,128)} %copy-done.3, ...), custom_call_target="tpu_custom_call" | custom-call | tf_op jit(solution)/shard_map/pallas_call | solution.py:694
  59.9 0.0 all-to-all-done.gathered
  59.9 0.0 copy-start
  59.9 0.7 copy-done
  60.6 13.1 %shard_map.185 = f32[16,16,64]{2,1,0:T(8,128)} custom-call(f32[128,2,256]{2,1,0:T(2,128)} %copy-done, f32[1,256,256]{2,1,0:T(8,128)} %bitcast.3, f32[2,256,256]{2,1,0:T(8,128)} %pair_down.1, f32[4,256,256]{2,1,0:T(8,128)} %down_child.1, bf16[128,128]{1,0:T(8,128)(2,1)} %constant.13.clone.perm8, bf16[32,32]{1,0:T(8,128)(2,1)} %constant.14.clone.perm4, ...), custom_call_target="tpu_custom_call" | custom-call | tf_op jit(solution)/shard_map/pallas_call | solution.py:706
Async XLA Ops:
  15.3 13.4 %collective-permute-start = (f32[128,256]{1,0:T(8,128)}, f32[128,256]{1,0:T(8,128)S(1)}, u32[]{:S(2)}, u32[]{:S(2)}) collective-permute-start(f32[128,256]{1,0:T(8,128)} %get-tuple-element.21), channel_id=1, source_target_pairs={{0,1},{1,2},{2,3},{3,4},{4,5},{5,6},{6,7},{7,8},{8,9},{9,10},{10,1... | collective-permute-start | bytes 393224 | tf_op jit(solution)/shard_map/ppermute | solution.py:671
  17.4 11.4 %collective-permute-start.1 = (f32[128,256]{1,0:T(8,128)}, f32[128,256]{1,0:T(8,128)S(1)}, u32[]{:S(2)}, u32[]{:S(2)}) collective-permute-start(f32[128,256]{1,0:T(8,128)} %get-tuple-element.22), channel_id=1, source_target_pairs={{0,15},{1,0},{2,1},{3,2},{4,3},{5,4},{6,5},{7,6},{8,7},{9,8},{10,9... | collective-permute-start | bytes 393224 | tf_op jit(solution)/shard_map/ppermute | solution.py:672
  21.8 38.1 %all-to-all-start = ((f32[128,2,256]{2,1,0:T(2,128)}), f32[128,2,256]{2,1,0:T(2,128)S(1)}, u32[]{:S(2)}, u32[]{:S(2)}) async-start(f32[128,2,256]{2,1,0:T(2,128)} %get-tuple-element.19), calls=%async_computation | async-start | bytes 524288 | tf_op jit(solution)/shard_map/all_to_all | solution.py:678
  28.8 0.7 copy-start.1
  28.8 0.7 copy-start.2
  31.4 19.1 %collective-permute-start.3 = (f32[168,256]{1,0:T(8,128)}, f32[168,256]{1,0:T(8,128)S(1)}, u32[]{:S(2)}, u32[]{:S(2)}) collective-permute-start(f32[168,256]{1,0:T(8,128)} %get-tuple-element.25), channel_id=1, source_target_pairs={{0,112},{16,0},{32,16},{48,32},{64,48},{80,64},{96,80},{112,96},{1... | collective-permute-start | bytes 516104 | tf_op jit(solution)/shard_map/ppermute | solution.py:677
  33.2 17.3 %collective-permute-start.2 = (f32[168,256]{1,0:T(8,128)}, f32[168,256]{1,0:T(8,128)S(1)}, u32[]{:S(2)}, u32[]{:S(2)}) collective-permute-start(f32[168,256]{1,0:T(8,128)} %get-tuple-element.24), channel_id=1, source_target_pairs={{0,16},{16,32},{32,48},{48,64},{64,80},{80,96},{96,112},{112,0},{1... | collective-permute-start | bytes 516104 | tf_op jit(solution)/shard_map/ppermute | solution.py:676
  50.5 0.7 copy-start.4
  50.5 0.7 copy-start.3
  59.9 0.7 copy-start

commit v6 on v5

--- a/solution.py
+++ b/solution.py
@@ -159,15 +159,18 @@
 
 
 def upward_kernel(
-    coords, weights, solution, counts, check_pts, solve, up_child, pair_up, perm8, perm4,
-    feats, pts, boxes, gy_next, gy_prev, gx_edge, up_out,
-    u0, u1, densities, pot, hi, lo, kept, kept_sem,
+    coords, weights, solution, counts, check_pts, perm8, perm4, solve, up_child, pair_up,
+    feats, pts_out, boxes, gy_next, gy_prev, gx_edge, up_out,
+    u0, u1, densities, pot, hi, lo, kept, kept_sem, pts, pts_sem, matrices, matrix_sem,
 ):
     check_cols = col_feats(pad_points(check_pts), 0.0)
     ident = eye(128)
-    split_into(solve, hi, lo, 0)
-    split_into(up_child, hi, lo, 1)
-    split_into(pair_up, hi, lo, 5)
+    loads = [
+        pltpu.make_async_copy(source, matrices.at[pl.ds(at, count)], matrix_sem.at[n])
+        for n, (source, at, count) in enumerate(((solve, 0, 1), (up_child, 1, 4), (pair_up, 5, 2)))
+    ]
+    for load in loads:
+        load.start()
 
     row8 = lax.broadcasted_iota(jnp.int32, (8, 128), 0)
     lane8 = lax.broadcasted_iota(jnp.int32, (8, 128), 1)
@@ -196,6 +199,11 @@
     lax.fori_loop(0, NX // 4, prepare, 0)
     keep = pltpu.make_async_copy(kept, feats, kept_sem)
     keep.start()
+    keep_pts = pltpu.make_async_copy(pts, pts_out, pts_sem)
+    keep_pts.start()
+    for load in loads:
+        load.wait()
+    split_into(matrices, hi, lo, 0)
 
     def distances(a, m, u):
         rows = kept[pl.ds(pl.multiple_of(a * LANES + 128 * m, 128), 128), :]
@@ -278,6 +286,7 @@
             vec = dot3(vec, hi[n], lo[n])
     up_out[...] = jnp.broadcast_to(vec[None, :2], (128, 2, 256))
     keep.wait()
+    keep_pts.wait()
 
 
 def pack_kernel(low, high, edge, first, last):
@@ -648,7 +657,7 @@
     halves = [pltpu.VMEM((7, 256, 256), bf16)] * 2
     feats, pts, boxes, gy_next, gy_prev, gx_edge, up = call(
         upward_kernel,
-        [VMEM] * 10,
+        [VMEM] * 7 + [pl.BlockSpec(memory_space=pl.ANY)] * 3,
         (
             shape(NX * LANES, FEATS, dtype=bf16),
             shape(NX, 8, LANES),
@@ -662,11 +671,13 @@
         + [pltpu.VMEM((LANES, 256), f32)]
         + [pltpu.VMEM((512, 256), f32)]
         + halves
-        + [pltpu.VMEM((NX * LANES, FEATS), bf16), pltpu.SemaphoreType.DMA],
-        out_specs=(pl.BlockSpec(memory_space=pl.ANY),) + (VMEM,) * 6,
+        + [pltpu.VMEM((NX * LANES, FEATS), bf16), pltpu.SemaphoreType.DMA]
+        + [pltpu.VMEM((NX, 8, LANES), f32), pltpu.SemaphoreType.DMA]
+        + [pltpu.VMEM((7, 256, 256), f32), pltpu.SemaphoreType.DMA((3,))],
+        out_specs=(pl.BlockSpec(memory_space=pl.ANY),) * 2 + (VMEM,) * 5,
     )(
-        coords, weights, solution, counts, check_points, check_solve[None], up_children, pair_up,
-        jnp.asarray(perm8, bf16), jnp.asarray(perm4, bf16),
+        coords, weights, solution, counts, check_points, jnp.asarray(perm8, bf16),
+        jnp.asarray(perm4, bf16), check_solve[None], up_children, pair_up,
     )
     gy_low = lax.ppermute(gy_next, "gy", ring("gy", 1))
     gy_high = lax.ppermute(gy_prev, "gy", ring("gy", -1))

time: 74.5 us -> 73.8 us (level)
  no operation moved by 1% of the time
where the time goes in v6:
time: 73.8 us; the launch traced here: 73.1 us
  Pallas kernels  55.5 us (75%)
  starting transfers between devices  15.2 us (21%)
  local copies, waits for them, and re-layouts  2.07 us (3%)
    pallas_call x1, Pallas kernels, shards(): call(inner_kernel, [VMEM] * 4 + [pl.BlockSpec(memory_space=pl.ANY)], shap...  17.2 us
    pallas_call x1, Pallas kernels, shards(): call(upward_kernel, [VMEM] * 7 + [pl.BlockSpec(memory_space=pl.ANY)] * 3,...  14.6 us
    pallas_call x1, Pallas kernels, shards(): call(downward_kernel, [VMEM] * 14 + [pl.BlockSpec(memory_space=pl.ANY)],...  13.1 us
    pallas_call x1, Pallas kernels, shards(): call(middle_kernel, [VMEM] * 7 + [pl.BlockSpec(memory_space=pl.ANY)] * 2,...  8.65 us
    all_to_all x1, starting transfers between devices, shards(): gathered = lax.all_to_all(up, AXES, 0, 0, tiled=True)  6.96 us
    ppermute x1, starting transfers between devices, shards(): gy_high = lax.ppermute(gy_prev, 'gy', ring('gy', -1))  4.38 us
    ppermute x1, starting transfers between devices, shards(): gy_low = lax.ppermute(gy_next, 'gy', ring('gy', 1))  2.09 us
    unnamed x10, local copies, waits for them, and re-layouts  2.07 us
  transfers between devices with their start and end apart: 5, of which 0 were waited for; matrix products, arithmetic and copies ran while one was open for 0% of the time, Pallas kernels for 38%

profile of v6, /device:TPU:0, one launch (start us, length us, event | category | flops | bytes accessed | tf_op | source)
XLA Modules:
  0.0 73.1 jit_solution(2342674127459755403)
XLA Ops:
  0.0 14.6 %shard_map.181 = (bf16[16384,64]{1,0:T(8,128)(2,1)}, f32[16,8,1024]{2,1,0:T(8,128)}, f32[4,12,16,256]{3,2,1,0:T(8,128)}, f32[128,256]{1,0:T(8,128)}, f32[128,256...) custom-call(f32[3,16,16,64]{3,2,1,0:T(8,128)} %coords.1, f32[16,16,64]{2,1,0:T(8,128)} %weights.1, ...), custom_call_target="tpu_custom_call" | custom-call | tf_op jit(solution)/shard_map/pallas_call | solution.py:658
  14.6 2.1 %collective-permute-start = (f32[128,256]{1,0:T(8,128)}, f32[128,256]{1,0:T(8,128)S(1)}, u32[]{:S(2)}, u32[]{:S(2)}) collective-permute-start(f32[128,256]{1,0:T(8,128)} %get-tuple-element.21), channel_id=1, source_target_pairs={{0,1},{1,2},{2,3},{3,4},{4,5},{5,6},{6,7},{7,8},{8,9},{9,10},{10,1... | collective-permute-start | bytes 393224 | tf_op jit(solution)/shard_map/ppermute | solution.py:682
  16.7 4.4 %collective-permute-start.1 = (f32[128,256]{1,0:T(8,128)}, f32[128,256]{1,0:T(8,128)S(1)}, u32[]{:S(2)}, u32[]{:S(2)}) collective-permute-start(f32[128,256]{1,0:T(8,128)} %get-tuple-element.22), channel_id=1, source_target_pairs={{0,15},{1,0},{2,1},{3,2},{4,3},{5,4},{6,5},{7,6},{8,7},{9,8},{10,9... | collective-permute-start | bytes 393224 | tf_op jit(solution)/shard_map/ppermute | solution.py:683
  21.1 7.0 %all-to-all-start = ((f32[128,2,256]{2,1,0:T(2,128)}), f32[128,2,256]{2,1,0:T(2,128)S(1)}, u32[]{:S(2)}, u32[]{:S(2)}) async-start(f32[128,2,256]{2,1,0:T(2,128)} %get-tuple-element.19), calls=%async_computation | async-start | bytes 524288 | tf_op jit(solution)/shard_map/all_to_all | solution.py:689
  28.1 0.0 collective-permute-done.low.gy_low
  28.1 0.0 copy-start.1
  28.1 0.0 collective-permute-done.1.high.gy_high
  28.1 0.0 copy-start.2
  28.1 0.6 copy-done.1
  28.7 0.0 copy-done.2
  28.8 1.9 %shard_map.182 = (f32[168,256]{1,0:T(8,128)}, f32[168,256]{1,0:T(8,128)}) custom-call(f32[128,256]{1,0:T(8,128)} %copy-done.1, f32[128,256]{1,0:T(8,128)} %copy-done.2, f32[2,168,256]{2,1,0:T(8,128)} %get-tuple-element.23.edge), custom_call_target="tpu_custom_call" | custom-call | tf_op jit(solution)/shard_map/pallas_call | solution.py:684
  30.7 1.8 %collective-permute-start.3 = (f32[168,256]{1,0:T(8,128)}, f32[168,256]{1,0:T(8,128)S(1)}, u32[]{:S(2)}, u32[]{:S(2)}) collective-permute-start(f32[168,256]{1,0:T(8,128)} %get-tuple-element.25), channel_id=1, source_target_pairs={{0,112},{16,0},{32,16},{48,32},{64,48},{80,64},{96,80},{112,96},{1... | collective-permute-start | bytes 516104 | tf_op jit(solution)/shard_map/ppermute | solution.py:688
  32.5 0.0 collective-permute-start.2
  32.5 17.2 %shard_map.184.inner = f32[2,128,128]{2,1,0:T(8,128)} custom-call(f32[16,8,1024]{2,1,0:T(8,128)} %get-tuple-element.20.pts, f32[128,256]{1,0:T(8,128)} %copy-done.1, f32[128,256]{1,0:T(8,128)} %copy-done.2, bf16[5,16,128]{2,1,0:T(8,128)(2,1)} %constant.12.clone.roles, bf16[16384,64]{1,0:T(8,128)(2,1)} %get-tuple-element.27.feats_hbm), custom_call_target="tpu_custom_call" | custom-call | flops 40000000000 | bytes 10000000 | tf_op jit(solution)/shard_map/pallas_call | solution.py:698
  49.8 0.0 collective-permute-done.2.gx_low
  49.8 0.0 copy-start.4
  49.8 0.0 collective-permute-done.3.gx_high
  49.8 0.0 copy-start.3
  49.8 0.6 copy-done.4
  50.4 0.1 copy-done.3
  50.5 8.6 %shard_map.183 = (f32[2,128,128]{2,1,0:T(8,128)}, f32[512,256]{1,0:T(8,128)}, f32[128,256]{1,0:T(8,128)}) custom-call(f32[16,8,1024]{2,1,0:T(8,128)} %get-tuple-element.20.pts, f32[128,256]{1,0:T(8,128)} %copy-done.1, f32[128,256]{1,0:T(8,128)} %copy-done.2, f32[168,256]{1,0:T(8,128)} %copy-done.4, f32[168,256]{1,0:T(8,128)} %copy-done.3, ...), custom_call_target="tpu_custom_call" | custom-call | tf_op jit(solution)/shard_map/pallas_call | solution.py:705
  59.2 0.0 all-to-all-done.gathered
  59.2 0.0 copy-start
  59.2 0.7 copy-done
  59.9 13.1 %shard_map.185 = f32[16,16,64]{2,1,0:T(8,128)} custom-call(f32[128,2,256]{2,1,0:T(2,128)} %copy-done, f32[1,256,256]{2,1,0:T(8,128)} %bitcast.3, f32[2,256,256]{2,1,0:T(8,128)} %pair_down.1, f32[4,256,256]{2,1,0:T(8,128)} %down_child.1, bf16[128,128]{1,0:T(8,128)(2,1)} %constant.13.clone.perm8, bf16[32,32]{1,0:T(8,128)(2,1)} %constant.14.clone.perm4, ...), custom_call_target="tpu_custom_call" | custom-call | tf_op jit(solution)/shard_map/pallas_call | solution.py:717
Async XLA Ops:
  14.6 13.4 %collective-permute-start = (f32[128,256]{1,0:T(8,128)}, f32[128,256]{1,0:T(8,128)S(1)}, u32[]{:S(2)}, u32[]{:S(2)}) collective-permute-start(f32[128,256]{1,0:T(8,128)} %get-tuple-element.21), channel_id=1, source_target_pairs={{0,1},{1,2},{2,3},{3,4},{4,5},{5,6},{6,7},{7,8},{8,9},{9,10},{10,1... | collective-permute-start | bytes 393224 | tf_op jit(solution)/shard_map/ppermute | solution.py:682
  16.7 11.4 %collective-permute-start.1 = (f32[128,256]{1,0:T(8,128)}, f32[128,256]{1,0:T(8,128)S(1)}, u32[]{:S(2)}, u32[]{:S(2)}) collective-permute-start(f32[128,256]{1,0:T(8,128)} %get-tuple-element.22), channel_id=1, source_target_pairs={{0,15},{1,0},{2,1},{3,2},{4,3},{5,4},{6,5},{7,6},{8,7},{9,8},{10,9... | collective-permute-start | bytes 393224 | tf_op jit(solution)/shard_map/ppermute | solution.py:683
  21.1 38.1 %all-to-all-start = ((f32[128,2,256]{2,1,0:T(2,128)}), f32[128,2,256]{2,1,0:T(2,128)S(1)}, u32[]{:S(2)}, u32[]{:S(2)}) async-start(f32[128,2,256]{2,1,0:T(2,128)} %get-tuple-element.19), calls=%async_computation | async-start | bytes 524288 | tf_op jit(solution)/shard_map/all_to_all | solution.py:689
  28.1 0.7 copy-start.1
  28.1 0.7 copy-start.2
  30.7 19.1 %collective-permute-start.3 = (f32[168,256]{1,0:T(8,128)}, f32[168,256]{1,0:T(8,128)S(1)}, u32[]{:S(2)}, u32[]{:S(2)}) collective-permute-start(f32[168,256]{1,0:T(8,128)} %get-tuple-element.25), channel_id=1, source_target_pairs={{0,112},{16,0},{32,16},{48,32},{64,48},{80,64},{96,80},{112,96},{1... | collective-permute-start | bytes 516104 | tf_op jit(solution)/shard_map/ppermute | solution.py:688
  32.5 17.3 %collective-permute-start.2 = (f32[168,256]{1,0:T(8,128)}, f32[168,256]{1,0:T(8,128)S(1)}, u32[]{:S(2)}, u32[]{:S(2)}) collective-permute-start(f32[168,256]{1,0:T(8,128)} %get-tuple-element.24), channel_id=1, source_target_pairs={{0,16},{16,32},{32,48},{48,64},{64,80},{80,96},{96,112},{112,0},{1... | collective-permute-start | bytes 516104 | tf_op jit(solution)/shard_map/ppermute | solution.py:687
  49.8 0.7 copy-start.4
  49.8 0.7 copy-start.3
  59.2 0.7 copy-start

commit v7 on v6

--- a/solution.py
+++ b/solution.py
@@ -556,11 +556,22 @@
 
 def downward_kernel(
     gathered, lattice, pair_down, down_child, perm8, perm4, far_leaf, far_parent,
-    equiv_pts, inner, near, solution, source, counts, feats_hbm, out,
-    local, pot, u0, u1, hi, lo, feats, feats_sem,
+    equiv_pts, counts, inner_hbm, near_hbm, solution_hbm, source_hbm, feats_hbm, out,
+    local, pot, u0, u1, hi, lo, feats, feats_sem, inner, near, solution, source, late_sem,
 ):
     load = pltpu.make_async_copy(feats_hbm, feats, feats_sem)
     load.start()
+    late = [
+        pltpu.make_async_copy(a, b, late_sem.at[n])
+        for n, (a, b) in enumerate(
+            (
+                (inner_hbm, inner), (near_hbm, near), (solution_hbm, solution),
+                (source_hbm, source),
+            )
+        )
+    ]
+    for one in late:
+        one.start()
     split_into(lattice, hi, lo, 0)
     split_into(pair_down, hi, lo, 1)
     split_into(down_child, hi, lo, 3)
@@ -618,6 +629,8 @@
         return carry
 
     lax.fori_loop(0, NX // 2, step, 0)
+    for one in late:
+        one.wait()
     for a in range(NX):
         rows = slice(8 * a, 8 * a + 8)
         close = near if a in (0, NX - 1) else inner
@@ -716,16 +729,19 @@
     )
     return call(
         downward_kernel,
-        [VMEM] * 14 + [pl.BlockSpec(memory_space=pl.ANY)],
+        [VMEM] * 10 + [pl.BlockSpec(memory_space=pl.ANY)] * 5,
         shape(NX, NX, 64),
         [pltpu.VMEM((512, 256), f32), pltpu.VMEM((2, 128, 128), f32)]
         + [pltpu.VMEM((512, 256), f32)] * 2
         + halves
-        + [pltpu.VMEM((NX * LANES, FEATS), bf16), pltpu.SemaphoreType.DMA],
+        + [pltpu.VMEM((NX * LANES, FEATS), bf16), pltpu.SemaphoreType.DMA]
+        + [pltpu.VMEM((2, 128, 128), f32)] * 2
+        + [pltpu.VMEM((NX, NX, 64), f32)] * 2
+        + [pltpu.SemaphoreType.DMA((4,))],
     )(
         gathered, lattice_map[None], pair_down, down_children,
         jnp.asarray(perm8.T, bf16), jnp.asarray(perm4.T, bf16), far_leaf, far_parent,
-        equiv_points, inner, near, solution, source, counts, feats,
+        equiv_points, counts, inner, near, solution, source, feats,
     )
 
 

time: 73.8 us -> 73.7 us (level)
  no operation moved by 1% of the time
where the time goes in v7:
time: 73.7 us; the launch traced here: 73 us
  Pallas kernels  55.4 us (75%)
  starting transfers between devices  15.2 us (21%)
  local copies, waits for them, and re-layouts  2.07 us (3%)
    pallas_call x1, Pallas kernels, shards(): call(inner_kernel, [VMEM] * 4 + [pl.BlockSpec(memory_space=pl.ANY)], shap...  17.2 us
    pallas_call x1, Pallas kernels, shards(): call(upward_kernel, [VMEM] * 7 + [pl.BlockSpec(memory_space=pl.ANY)] * 3,...  14.6 us
    pallas_call x1, Pallas kernels, shards(): call(downward_kernel, [VMEM] * 10 + [pl.BlockSpec(memory_space=pl.ANY)] *...  12.9 us
    pallas_call x1, Pallas kernels, shards(): call(middle_kernel, [VMEM] * 7 + [pl.BlockSpec(memory_space=pl.ANY)] * 2,...  8.65 us
    all_to_all x1, starting transfers between devices, shards(): gathered = lax.all_to_all(up, AXES, 0, 0, tiled=True)  6.96 us
    ppermute x1, starting transfers between devices, shards(): gy_high = lax.ppermute(gy_prev, 'gy', ring('gy', -1))  4.38 us
    ppermute x1, starting transfers between devices, shards(): gy_low = lax.ppermute(gy_next, 'gy', ring('gy', 1))  2.09 us
    unnamed x10, local copies, waits for them, and re-layouts  2.07 us
  transfers between devices with their start and end apart: 5, of which 0 were waited for; matrix products, arithmetic and copies ran while one was open for 0% of the time, Pallas kernels for 38%

profile of v7, /device:TPU:0, one launch (start us, length us, event | category | flops | bytes accessed | tf_op | source)
XLA Modules:
  0.0 73.0 jit_solution(7309597117969612614)
XLA Ops:
  0.0 14.6 %shard_map.181 = (bf16[16384,64]{1,0:T(8,128)(2,1)}, f32[16,8,1024]{2,1,0:T(8,128)}, f32[4,12,16,256]{3,2,1,0:T(8,128)}, f32[128,256]{1,0:T(8,128)}, f32[128,256...) custom-call(f32[3,16,16,64]{3,2,1,0:T(8,128)} %coords.1, f32[16,16,64]{2,1,0:T(8,128)} %weights.1, ...), custom_call_target="tpu_custom_call" | custom-call | tf_op jit(solution)/shard_map/pallas_call | solution.py:671
  14.6 2.1 %collective-permute-start = (f32[128,256]{1,0:T(8,128)}, f32[128,256]{1,0:T(8,128)S(1)}, u32[]{:S(2)}, u32[]{:S(2)}) collective-permute-start(f32[128,256]{1,0:T(8,128)} %get-tuple-element.21), channel_id=1, source_target_pairs={{0,1},{1,2},{2,3},{3,4},{4,5},{5,6},{6,7},{7,8},{8,9},{9,10},{10,1... | collective-permute-start | bytes 393224 | tf_op jit(solution)/shard_map/ppermute | solution.py:695
  16.7 4.4 %collective-permute-start.1 = (f32[128,256]{1,0:T(8,128)}, f32[128,256]{1,0:T(8,128)S(1)}, u32[]{:S(2)}, u32[]{:S(2)}) collective-permute-start(f32[128,256]{1,0:T(8,128)} %get-tuple-element.22), channel_id=1, source_target_pairs={{0,15},{1,0},{2,1},{3,2},{4,3},{5,4},{6,5},{7,6},{8,7},{9,8},{10,9... | collective-permute-start | bytes 393224 | tf_op jit(solution)/shard_map/ppermute | solution.py:696
  21.1 7.0 %all-to-all-start = ((f32[128,2,256]{2,1,0:T(2,128)}), f32[128,2,256]{2,1,0:T(2,128)S(1)}, u32[]{:S(2)}, u32[]{:S(2)}) async-start(f32[128,2,256]{2,1,0:T(2,128)} %get-tuple-element.19), calls=%async_computation | async-start | bytes 524288 | tf_op jit(solution)/shard_map/all_to_all | solution.py:702
  28.1 0.0 collective-permute-done.low.gy_low
  28.1 0.0 copy-start.1
  28.1 0.0 collective-permute-done.1.high.gy_high
  28.1 0.0 copy-start.2
  28.1 0.6 copy-done.1
  28.7 0.0 copy-done.2
  28.8 1.9 %shard_map.182 = (f32[168,256]{1,0:T(8,128)}, f32[168,256]{1,0:T(8,128)}) custom-call(f32[128,256]{1,0:T(8,128)} %copy-done.1, f32[128,256]{1,0:T(8,128)} %copy-done.2, f32[2,168,256]{2,1,0:T(8,128)} %get-tuple-element.23.edge), custom_call_target="tpu_custom_call" | custom-call | tf_op jit(solution)/shard_map/pallas_call | solution.py:697
  30.7 1.8 %collective-permute-start.3 = (f32[168,256]{1,0:T(8,128)}, f32[168,256]{1,0:T(8,128)S(1)}, u32[]{:S(2)}, u32[]{:S(2)}) collective-permute-start(f32[168,256]{1,0:T(8,128)} %get-tuple-element.25), channel_id=1, source_target_pairs={{0,112},{16,0},{32,16},{48,32},{64,48},{80,64},{96,80},{112,96},{1... | collective-permute-start | bytes 516104 | tf_op jit(solution)/shard_map/ppermute | solution.py:701
  32.5 0.0 collective-permute-start.2
  32.5 17.2 %shard_map.184.inner_hbm = f32[2,128,128]{2,1,0:T(8,128)} custom-call(f32[16,8,1024]{2,1,0:T(8,128)} %get-tuple-element.20.pts, f32[128,256]{1,0:T(8,128)} %copy-done.1, f32[128,256]{1,0:T(8,128)} %copy-done.2, bf16[5,16,128]{2,1,0:T(8,128)(2,1)} %constant.12.clone.roles, bf16[16384,64]{1,0:T(8,128)(2,1)} %get-tuple-element.27.feats_hbm), custom_call_target="tpu_custom_call" | custom-call | flops 40000000000 | bytes 10000000 | tf_op jit(solution)/shard_map/pallas_call | solution.py:711
  49.8 0.0 collective-permute-done.2.gx_low
  49.8 0.0 copy-start.4
  49.8 0.0 collective-permute-done.3.gx_high
  49.8 0.0 copy-start.3
  49.8 0.6 copy-done.4
  50.4 0.1 copy-done.3
  50.5 8.6 %shard_map.183 = (f32[2,128,128]{2,1,0:T(8,128)}, f32[512,256]{1,0:T(8,128)}, f32[128,256]{1,0:T(8,128)}) custom-call(f32[16,8,1024]{2,1,0:T(8,128)} %get-tuple-element.20.pts, f32[128,256]{1,0:T(8,128)} %copy-done.1, f32[128,256]{1,0:T(8,128)} %copy-done.2, f32[168,256]{1,0:T(8,128)} %copy-done.4, f32[168,256]{1,0:T(8,128)} %copy-done.3, ...), custom_call_target="tpu_custom_call" | custom-call | tf_op jit(solution)/shard_map/pallas_call | solution.py:718
  59.2 0.0 all-to-all-done.gathered
  59.2 0.0 copy-start
  59.2 0.7 copy-done
  59.9 12.9 %shard_map.185 = f32[16,16,64]{2,1,0:T(8,128)} custom-call(f32[128,2,256]{2,1,0:T(2,128)} %copy-done, f32[1,256,256]{2,1,0:T(8,128)} %bitcast.3, f32[2,256,256]{2,1,0:T(8,128)} %pair_down.1, f32[4,256,256]{2,1,0:T(8,128)} %down_child.1, bf16[128,128]{1,0:T(8,128)(2,1)} %constant.13.clone.perm8, bf16[32,32]{1,0:T(8,128)(2,1)} %constant.14.clone.perm4, ...), custom_call_target="tpu_custom_call" | custom-call | tf_op jit(solution)/shard_map/pallas_call | solution.py:730
Async XLA Ops:
  14.6 13.4 %collective-permute-start = (f32[128,256]{1,0:T(8,128)}, f32[128,256]{1,0:T(8,128)S(1)}, u32[]{:S(2)}, u32[]{:S(2)}) collective-permute-start(f32[128,256]{1,0:T(8,128)} %get-tuple-element.21), channel_id=1, source_target_pairs={{0,1},{1,2},{2,3},{3,4},{4,5},{5,6},{6,7},{7,8},{8,9},{9,10},{10,1... | collective-permute-start | bytes 393224 | tf_op jit(solution)/shard_map/ppermute | solution.py:695
  16.7 11.4 %collective-permute-start.1 = (f32[128,256]{1,0:T(8,128)}, f32[128,256]{1,0:T(8,128)S(1)}, u32[]{:S(2)}, u32[]{:S(2)}) collective-permute-start(f32[128,256]{1,0:T(8,128)} %get-tuple-element.22), channel_id=1, source_target_pairs={{0,15},{1,0},{2,1},{3,2},{4,3},{5,4},{6,5},{7,6},{8,7},{9,8},{10,9... | collective-permute-start | bytes 393224 | tf_op jit(solution)/shard_map/ppermute | solution.py:696
  21.1 38.1 %all-to-all-start = ((f32[128,2,256]{2,1,0:T(2,128)}), f32[128,2,256]{2,1,0:T(2,128)S(1)}, u32[]{:S(2)}, u32[]{:S(2)}) async-start(f32[128,2,256]{2,1,0:T(2,128)} %get-tuple-element.19), calls=%async_computation | async-start | bytes 524288 | tf_op jit(solution)/shard_map/all_to_all | solution.py:702
  28.1 0.7 copy-start.1
  28.1 0.7 copy-start.2
  30.7 19.1 %collective-permute-start.3 = (f32[168,256]{1,0:T(8,128)}, f32[168,256]{1,0:T(8,128)S(1)}, u32[]{:S(2)}, u32[]{:S(2)}) collective-permute-start(f32[168,256]{1,0:T(8,128)} %get-tuple-element.25), channel_id=1, source_target_pairs={{0,112},{16,0},{32,16},{48,32},{64,48},{80,64},{96,80},{112,96},{1... | collective-permute-start | bytes 516104 | tf_op jit(solution)/shard_map/ppermute | solution.py:701
  32.5 17.3 %collective-permute-start.2 = (f32[168,256]{1,0:T(8,128)}, f32[168,256]{1,0:T(8,128)S(1)}, u32[]{:S(2)}, u32[]{:S(2)}) collective-permute-start(f32[168,256]{1,0:T(8,128)} %get-tuple-element.24), channel_id=1, source_target_pairs={{0,16},{16,32},{32,48},{48,64},{64,80},{80,96},{96,112},{112,0},{1... | collective-permute-start | bytes 516104 | tf_op jit(solution)/shard_map/ppermute | solution.py:700
  49.8 0.7 copy-start.4
  49.8 0.7 copy-start.3
  59.2 0.7 copy-start
